TPU v7x, 256 devices: a whole 4x4x8 slice. The times are simulated.
256 devices in a mesh: seq: 4 (over x), head: 64 (over y, z, core).
Axes of the slice: x: 4, y: 4, z: 8, core: 2. Of those that a mesh axis runs over, the one named last changes fastest.
Arguments:
- queries: bfloat16 [4096, 64, 128], P(('seq', 'head')), may hold values from -160 to 160
- keys: bfloat16 [4096, 64, 128], P(('seq', 'head')), may hold values from -8 to 8
- b_proj: bfloat16 [4096, 64, 128], P(('seq', 'head')), may hold values from -6 to 6
- c_proj: bfloat16 [4096, 64, 128], P(('seq', 'head')), may hold values from -6 to 6
- step_size: bfloat16 [4096, 64], P(('seq', 'head')), may hold values from 0 to 110
- rate_level: int32 [64], P('head'), may hold values from 0 to 15
Outputs:
- grad_b: float32 [4096, 64, 128], P(('seq', 'head'))
- grad_c: float32 [4096, 64, 128], P(('seq', 'head'))
- grad_step: float32 [4096, 64], P(('seq', 'head'))
- loss: float32 [], replicated
All inputs are finite; a program needn't handle non-finite values.
Results may differ from a plain program's by a relative error of at most 0.00098.
Values may be sent and summed in bfloat16 or wider, within the bound.
No kernel may reach another device: no remote copies, remote signals or barrier semaphores. Data moves between devices by JAX's collectives and lax.ppermute only.
A program may use at most 128 MiB of HBM per device.

v0:
```python
import math

import jax
import jax.numpy as jnp
from jax import lax
from jax.sharding import PartitionSpec as P


def carried_in(x, axis, combine, identity, reverse):
    size, place = (lax.axis_size(axis), lax.axis_index(axis))
    everything = lax.all_gather(x, axis)
    start = jnp.broadcast_to(jnp.asarray(identity, x.dtype), x.shape)

    def lap(k, before):
        at = size - 1 - k if reverse else k
        reached = at > place if reverse else at < place
        new = combine(before, everything[at])
        return jnp.where(reached, new, before)

    return lax.fori_loop(0, size, lap, start)


def add_pair(earlier, later):
    return earlier + later


def block_width(count, query_rows, pairs):
    return math.gcd(count, max(128, (1 << 22) // (query_rows * pairs)))


def per_device(queries, keys, b_proj, c_proj, step_size, rate_level):
    query_all, key_own, b_own, c_own, steps = (
        lax.all_to_all(queries, "head", split_axis=1, concat_axis=0, tiled=True),
        lax.all_to_all(keys, "head", split_axis=1, concat_axis=0, tiled=True),
        lax.all_to_all(b_proj, "head", split_axis=1, concat_axis=0, tiled=True),
        lax.all_to_all(c_proj, "head", split_axis=1, concat_axis=0, tiled=True),
        lax.all_to_all(step_size, "head", split_axis=1, concat_axis=0, tiled=True),
    )
    rows, pairs, width = query_all.shape
    state = b_own.shape[2]
    seq_len = rows * lax.axis_size("seq")
    first = lax.axis_index("seq") * rows
    last = first + rows - 1
    beta = 2.0 / math.sqrt(state * seq_len)
    inv_root = 1.0 / math.sqrt(width)
    rate = jnp.exp2(-0.5 * rate_level.astype(jnp.float32))
    log_decay = -rate[None, :] * steps.astype(jnp.float32)
    running = jnp.cumsum(log_decay, axis=0)
    zeros_pairs = jnp.zeros((pairs,), jnp.float32)
    offset = carried_in(running[-1], "seq", add_pair, zeros_pairs, False)
    sums_own = running + offset[None, :]
    sums_all = lax.all_gather(sums_own, "seq", axis=0, tiled=True)
    query_pos = (first + lax.broadcasted_iota(jnp.int32, (rows, 1), 0))[None]
    own_sums = sums_own.T[:, :, None]

    def causal_mask(where_from, size):
        return where_from + lax.broadcasted_iota(jnp.int32, (1, 1, size), 2) <= query_pos

    init_stats = (
        jnp.full((pairs, rows), -1e30, jnp.float32),
        jnp.zeros((pairs, rows), jnp.float32),
    )
    extra_init = (
        jnp.zeros((seq_len, pairs, state), jnp.float32),
        jnp.zeros((seq_len, pairs), jnp.float32),
    )
    init_grad = (
        jnp.zeros((rows, pairs, state), jnp.float32),
        jnp.zeros((pairs, rows), jnp.float32),
        zeros_pairs,
        extra_init,
    )
    key_all, b_all = (
        lax.all_gather(key_own, "seq", axis=0, tiled=True),
        lax.all_gather(b_own, "seq", axis=0, tiled=True),
    )
    carry = init_stats
    count = key_all.shape[0]
    size = block_width(count, rows, pairs)
    begin = 0
    key_part = key_all
    where_from = 0 + begin

    def stats_work(stat, key_part=key_part, where_from=where_from, size=size):
        top, total = stat
        scores = (
            jnp.einsum("ipd,jpd->pij", query_all, key_part, preferred_element_type=jnp.float32)
            * inv_root
        )
        masked = jnp.where(causal_mask(where_from, size), scores, -jnp.inf)
        top_new = jnp.maximum(top, jnp.max(masked, axis=2))
        total_new = jnp.sum(jnp.exp(masked - top_new[:, :, None]), axis=2)
        return (top_new, total_new)

    carry = lax.cond(where_from <= last, stats_work, lambda stat: stat, carry)
    top, total = carry
    carry = init_grad
    count = key_all.shape[0]
    size = block_width(count, rows, pairs)
    begin = 0
    key_part = key_all
    b_part = b_all
    where_from = 0 + begin

    def grad_work(acc, key_part=key_part, b_part=b_part, where_from=where_from, size=size):
        grad_c, row_w, sumsq, extra = acc
        mask = causal_mask(where_from, size)
        scores = (
            jnp.einsum("ipd,jpd->pij", query_all, key_part, preferred_element_type=jnp.float32)
            * inv_root
        )
        teacher = jnp.where(mask, jnp.exp(scores - top[:, :, None]) / total[:, :, None], 0.0)
        decay = jnp.exp(jnp.where(mask, own_sums - sums_all.T[:, None, :], -jnp.inf))
        inner = jnp.einsum("ipn,jpn->pij", c_own, b_part, preferred_element_type=jnp.float32)
        student = beta * inner * decay
        error = student - teacher
        sumsq = sumsq + jnp.sum(error * error, axis=(1, 2))
        held = (error * decay).astype(jnp.bfloat16)
        grad_c = jnp.einsum("pij,jpn->ipn", held, b_part, preferred_element_type=jnp.float32)
        weight = error * student
        row_w = row_w + jnp.sum(weight, axis=2)
        grad_b, col_all = extra
        b_term = jnp.einsum("pij,ipn->jpn", held, c_own, preferred_element_type=jnp.float32)
        grad_b = b_term
        col_old = col_all
        col_all = lax.dynamic_update_slice_in_dim(
            col_all, col_old + jnp.sum(weight, axis=1).T, where_from, 0
        )
        extra = (grad_b, col_all)
        return (grad_c, row_w, sumsq, extra)

    carry = lax.cond(where_from <= last, grad_work, lambda acc: acc, carry)
    grad_c, row_w, sumsq, extra = carry
    error_sq = lax.psum(sumsq, "seq")
    grad_b_raw, col_own = lax.psum_scatter(extra, "seq", scatter_dimension=0, tiled=True)
    slope = row_w.T - col_own
    tails = jnp.cumsum(slope[::-1], axis=0)[::-1]
    after = carried_in(tails[0], "seq", add_pair, zeros_pairs, True)
    grad_log = tails + after[None, :]
    norm = jnp.sqrt(error_sq + 1e-06)
    factor = seq_len / norm
    grad_c_out = grad_c * (factor * beta)[None, :, None]
    grad_b_out = grad_b_raw * (factor * beta)[None, :, None]
    grad_step_out = grad_log * (-(rate * factor))[None, :]
    grad_b_tok, grad_c_tok, grad_step_tok = (
        lax.all_to_all(grad_b_out, "head", split_axis=0, concat_axis=1, tiled=True),
        lax.all_to_all(grad_c_out, "head", split_axis=0, concat_axis=1, tiled=True),
        lax.all_to_all(grad_step_out, "head", split_axis=0, concat_axis=1, tiled=True),
    )
    loss = lax.psum(jnp.sum(norm), "head") / (pairs * lax.axis_size("head"))
    return (grad_b_tok, grad_c_tok, grad_step_tok, loss)


def solution(mesh):
    return jax.shard_map(
        per_device,
        mesh=mesh,
        in_specs=(
            P(("seq", "head"), None, None),
            P(("seq", "head"), None, None),
            P(("seq", "head"), None, None),
            P(("seq", "head"), None, None),
            P(("seq", "head"), None),
            P("head"),
        ),
        out_specs=(
            P(("seq", "head"), None, None),
            P(("seq", "head"), None, None),
            P(("seq", "head"), None),
            P(),
        ),
        check_vma=False,
    )
```

profile of v0, /device:TPU:1, one launch (start us, length us, event | category | flops | bytes accessed | tf_op | source)
XLA Modules:
  0.0 418.5 jit_solution(3932855683422414406)
XLA Ops:
  8.3 25.1 %all_to_all.138 = bf16[16,64,128]{2,0,1:T(8,128)(2,1)} all-to-all(bf16[16,64,128]{2,0,1:T(8,128)(2,1)S(1)} %copy.55), channel_id=1, replica_groups=mesh['seq'=4,'head'=64] {'head'}, dimensions={1} | all-to-all | bytes 524288 | tf_op jit(solution)/shard_map/all_to_all | solution.py:34
  34.6 17.9 %all_to_all.139 = bf16[16,64,128]{2,0,1:T(8,128)(2,1)} all-to-all(bf16[16,64,128]{2,0,1:T(8,128)(2,1)S(1)} %copy.52), channel_id=1, replica_groups=mesh['seq'=4,'head'=64] {'head'}, dimensions={1} | all-to-all | bytes 524288 | tf_op jit(solution)/shard_map/all_to_all | solution.py:35
  54.0 6.0 %all-to-all-start.2 = ((bf16[16,64,1]{0,2,1:T(2,128)(2,1)}), bf16[16,64,1]{0,2,1:T(2,128)(2,1)S(1)}, u32[]{:S(2)}, u32[]{:S(2)}) async-start(bf16[16,64,1]{0,2,1:T(2,128)(2,1)} %copy.53), calls=%async_computation.2 | async-start | bytes 65536 | tf_op jit(solution)/shard_map/all_to_all | solution.py:37
  61.8 7.4 %all-to-all-done.2 = bf16[16,64,1]{0,2,1:T(2,128)(2,1)S(1)} async-done(((bf16[16,64,1]{0,2,1:T(2,128)(2,1)}), bf16[16,64,1]{0,2,1:T(2,128)(2,1)S(1)}, u32[]{:S(2)}, u32[]{:S(2)}) %all-to-all-start.2) | async-done | bytes 2080 | tf_op jit(solution)/shard_map/all_to_all | solution.py:37
  78.3 7.7 %all-to-all-done = bf16[16,64,128]{2,0,1:T(8,128)(2,1)S(1)} async-done(((bf16[16,64,128]{2,0,1:T(8,128)(2,1)}), bf16[16,64,128]{2,0,1:T(8,128)(2,1)S(1)}, u32[]{:S(2)}, u32[]{:S(2)}) %all-to-all-start) | async-done | bytes 262176 | tf_op jit(solution)/shard_map/all_to_all | solution.py:36
  86.0 6.1 %all-to-all-start.3 = ((bf16[16,64,128]{2,0,1:T(8,128)(2,1)}), bf16[16,64,128]{2,0,1:T(8,128)(2,1)S(1)}, u32[]{:S(2)}, u32[]{:S(2)}) async-start(bf16[16,64,128]{2,0,1:T(8,128)(2,1)} %copy.54), calls=%async_computation.3 | async-start | bytes 524288 | tf_op jit(solution)/shard_map/all_to_all | solution.py:33
  94.5 9.1 %all-reduce = f32[4]{0:T(128)S(1)} all-reduce(f32[4]{0:T(128)S(1)} %bitcast_dynamic-update-slice_fusion.1), channel_id=1, replica_groups=mesh['seq'=4,'head'=64] {'seq'}, use_global_device_ids=true, to_apply=%add | all-reduce | flops 4 | bytes 32
  108.3 9.0 %all_gather.17 = f32[4096,1]{0,1:T(1,128)S(1)} all-gather(f32[1024,1]{0,1:T(1,128)S(1)} %broadcast_add_fusion), channel_id=1, replica_groups=mesh['seq'=4,'head'=64] {'seq'}, dimensions={0}, use_global_device_ids=true | all-gather | bytes 20480 | tf_op jit(solution)/shard_map/all_gather | solution.py:52
  117.5 11.7 %conditional.2 = (f32[1,1024]{1,0:T(1,128)}, f32[1,1024]{1,0:T(1,128)S(1)}) conditional(s32[]{:T(128)} %convert_element_type.25, () %tuple.64, (s32[1,1024,1]{1,2,0:T(1,128)S(1)}, bf16[1024,1,128]{2,0,1:T(8,128)(2,1)S(1)}, bf16[4096,1,128]{2,0,1:T(8,128)(2,1)}) %tuple.116), branch_computations={%region_0.0_spmd, %region_1.4_spmd} | conditional | flops 1111489536 | bytes 34893840 | solution.py:95
  117.5 5.1 %fusion = (f32[1024]{0:T(1024)S(1)}, f32[1024,4096]{1,0:T(8,128)S(1)}) fusion(s32[1024]{0:T(1024)S(1)} %bitcast.152, bf16[4096,1,128]{2,0,1:T(8,128)(2,1)} %get-tuple-element.215, bf16[1024,1,128]{2,0,1:T(8,128)(2,1)S(1)} %get-tuple-element.214), kind=kOutput, calls=%fused_computation.3 | convolution fusion | flops 1090518016 | bytes 18096128 | tf_op jit(solution)/shard_map/cond/branch_1_fun/ipd,jpd->pij/dot_general | solution.py:87
  123.1 6.1 %exponential_reduce_fusion = f32[1024]{0:T(1024)S(1)} fusion(f32[1024,4096]{1,0:T(8,128)S(1)} %get-tuple-element.340, f32[1024]{0:T(1024)} %broadcast_maximum_fusion, s32[1024]{0:T(1024)S(1)} %bitcast.153), kind=kLoop, calls=%fused_computation | loop fusion | flops 20970496 | bytes 16789504 | tf_op jit(solution)/shard_map/cond/branch_1_fun/reduce_sum | solution.py:92
  129.2 39.2 %conditional.3 = (f32[1024,1,128]{2,0,1:T(8,128)S(1)}, f32[1]{0:T(128)}, f32[4096,1,128]{2,0,1:T(8,128)S(1)}, f32[4096,1]{0,1:T(1,128)S(1)}, f32[1024,1]{0,1:T(1,128)S(1)}) conditional(s32[]{:T(128)} %convert_element_type.25, () %tuple.62, (bf16[64,16,1,128]{3,0,1,2:T(8,128)(2,1)S(1)}, bf16[4096,1,128]{2,0,1:T(8,128)(2,1)}, ...), branch_computations={%region_8.9_spmd, %region_9.0_spmd} | conditional | flops 4366267392 | bytes 107810952 | solution.py:132
  133.2 16.0 %fusion.5 = (f32[1024,4096]{1,0:T(8,128)}, bf16[1024,4096]{1,0:T(8,128)(2,1)}, f32[]{:T(128)}) fusion(f32[1024,4096]{1,0:T(8,128)S(1)} %fusion.8, f32[4096]{0:T(1024)S(1)} %bitcast.155, f32[1024]{0:T(1024)S(1)} %fusion.11, s32[1024]{0:T(1024)S(1)} %bitcast.154, f32[1024]{0:T(1024)S(1)} %bitcast.163, f32[1024]{0:T(1024)} %bitcast.15, ...), kind=kOutput, calls=%fused_computation.15 | convolution fusion | flops 1136656384 | bytes 43286532 | tf_op jit(solution)/shard_map/cond/branch_1_fun/ipd,jpd->pij/dot_general | solution.py:109
  149.2 5.7 %convolution_bitcast_fusion.1 = f32[1024,1,128]{2,0,1:T(8,128)S(1)} fusion(bf16[1024,4096]{1,0:T(8,128)(2,1)} %get-tuple-element.342, bf16[4096,1,128]{2,0,1:T(8,128)(2,1)S(1)} %copy-done.1), kind=kOutput, calls=%fused_computation.17 | convolution fusion | flops 1073741824 | bytes 9961472 | tf_op jit(solution)/shard_map/cond/branch_1_fun/pij,jpn->ipn/dot_general | solution.py:119
  154.9 7.2 %fusion.12 = (f32[1024]{0:T(1024)S(1)}, f32[4096]{0:T(1024)S(1)}) fusion(f32[1024,4096]{1,0:T(8,128)} %get-tuple-element.341), kind=kLoop, calls=%fused_computation.38 | loop fusion | flops 8383488 | bytes 16797696 | tf_op jit(solution)/shard_map/cond/branch_1_fun/reduce_sum | solution.py:121
  162.1 5.8 %convolution_bitcast_fusion = f32[4096,1,128]{2,0,1:T(8,128)S(1)} fusion(bf16[1024,4096]{1,0:T(8,128)(2,1)} %get-tuple-element.342, bf16[1024,128]{1,0:T(8,128)(2,1)S(1)} %bitcast.138), kind=kOutput, calls=%fused_computation.16 | convolution fusion | flops 1073741824 | bytes 10747904 | tf_op jit(solution)/shard_map/cond/branch_1_fun/pij,ipn->jpn/dot_general | solution.py:123
  171.0 35.5 %reduce-scatter.7.cloned.1.call-done = f32[1024,1]{1,0:T(8,128)} async-done(((f32[4096,1]{1,0:T(8,128)}), f32[1024,1]{1,0:T(8,128)}) %reduce-scatter.7.cloned.1.call-update) | async-done | bytes 4112
  211.2 7.8 %all-reduce.2 = (f32[1]{0:T(128)}, f32[4]{0:T(128)S(1)}) all-reduce(f32[1]{0:T(128)} %get-tuple-element.254, f32[4]{0:T(128)S(1)} %bitcast_dynamic-update-slice_fusion), channel_id=1, replica_groups=mesh['seq'=4,'head'=64] {'seq'}, use_global_device_ids=true, to_apply=%region_14.15 | all-reduce | flops 5 | bytes 40 | tf_op jit(solution)/shard_map/psum | solution.py:134
  225.7 12.7 %all-to-all-start.7 = ((f32[64,16,1]{1,2,0:T(1,128)}), f32[64,16,1]{1,2,0:T(1,128)S(1)}, u32[]{:S(2)}, u32[]{:S(2)}) async-start(f32[64,16,1]{1,2,0:T(1,128)} %bitcast.69), calls=%async_computation.8 | async-start | bytes 65536 | tf_op jit(solution)/shard_map/all_to_all | solution.py:148
  239.5 8.1 %all-to-all-done.7 = f32[64,16,1]{1,2,0:T(1,128)S(1)} async-done(((f32[64,16,1]{1,2,0:T(1,128)}), f32[64,16,1]{1,2,0:T(1,128)S(1)}, u32[]{:S(2)}, u32[]{:S(2)}) %all-to-all-start.7) | async-done | bytes 4128 | tf_op jit(solution)/shard_map/all_to_all | solution.py:148
  247.6 4.7 %all-to-all-start.6 = ((f32[1024,1,128]{2,1,0:T(1,128)}), f32[1024,1,128]{2,1,0:T(1,128)S(1)}, u32[]{:S(2)}, u32[]{:S(2)}) async-start(f32[1024,1,128]{2,1,0:T(1,128)} %bitcast.57), calls=%async_computation.7 | async-start | bytes 1048576 | tf_op jit(solution)/shard_map/all_to_all | solution.py:147
  254.2 15.5 %all-to-all-done.6 = f32[1024,1,128]{2,1,0:T(1,128)S(1)} async-done(((f32[1024,1,128]{2,1,0:T(1,128)}), f32[1024,1,128]{2,1,0:T(1,128)S(1)}, u32[]{:S(2)}, u32[]{:S(2)}) %all-to-all-start.6) | async-done | bytes 524320 | tf_op jit(solution)/shard_map/all_to_all | solution.py:147
  269.7 6.4 %all-to-all-start.5 = ((f32[1024,1,128]{2,1,0:T(1,128)}), f32[1024,1,128]{2,1,0:T(1,128)S(1)}, u32[]{:S(2)}, u32[]{:S(2)}) async-start(f32[1024,1,128]{2,1,0:T(1,128)} %bitcast.127), calls=%async_computation.6 | async-start | bytes 1048576 | tf_op jit(solution)/shard_map/all_to_all | solution.py:146
  276.1 131.5 %psum.15 = f32[]{:T(128)} all-reduce(f32[]{:T(128)} %bitcast.72), channel_id=1, replica_groups=mesh['seq'=4,'head'=64] {'head'}, use_global_device_ids=true, to_apply=%region_20.21 | all-reduce | flops 1 | bytes 8 | tf_op jit(solution)/shard_map/psum | solution.py:150
  (77 shorter events, 48.9 us)
Async XLA Ops:
  7.2 110.3 %all-gather.5.cloned.1.call-start = ((), (), s32[]{:S(2)}) async-start(), calls=%async_computation.11 | async-start | bytes 1310720 | tf_op jit(solution)/shard_map/all_gather | solution.py:74
  33.4 95.8 %all-gather.3.cloned.1.call-start = ((), (), s32[]{:S(2)}) async-start(), calls=%async_computation.10 | async-start | bytes 1310720 | tf_op jit(solution)/shard_map/all_gather | solution.py:75
  54.0 15.2 %all-to-all-start.2 = ((bf16[16,64,1]{0,2,1:T(2,128)(2,1)}), bf16[16,64,1]{0,2,1:T(2,128)(2,1)S(1)}, u32[]{:S(2)}, u32[]{:S(2)}) async-start(bf16[16,64,1]{0,2,1:T(2,128)(2,1)} %copy.53), calls=%async_computation.2 | async-start | bytes 65536 | tf_op jit(solution)/shard_map/all_to_all | solution.py:37
  69.2 16.8 %all-to-all-start = ((bf16[16,64,128]{2,0,1:T(8,128)(2,1)}), bf16[16,64,128]{2,0,1:T(8,128)(2,1)S(1)}, u32[]{:S(2)}, u32[]{:S(2)}) async-start(bf16[16,64,128]{2,0,1:T(8,128)(2,1)} %copy.50), calls=%async_computation | async-start | bytes 524288 | tf_op jit(solution)/shard_map/all_to_all | solution.py:36
  86.0 31.5 %all-to-all-start.3 = ((bf16[16,64,128]{2,0,1:T(8,128)(2,1)}), bf16[16,64,128]{2,0,1:T(8,128)(2,1)S(1)}, u32[]{:S(2)}, u32[]{:S(2)}) async-start(bf16[16,64,128]{2,0,1:T(8,128)(2,1)} %copy.54), calls=%async_computation.3 | async-start | bytes 524288 | tf_op jit(solution)/shard_map/all_to_all | solution.py:33
  92.1 114.5 %reduce-scatter.7.cloned.1.call-start = ((), (), s32[]{:S(2)}) async-start(), calls=%async_computation.13 | async-start | bytes 2621440
  129.2 3.9 copy-start.2
  133.1 16.0 %copy-start.1 = (bf16[4096,1,128]{2,0,1:T(8,128)(2,1)S(1)}, bf16[4096,1,128]{2,0,1:T(8,128)(2,1)}, u32[]{:S(2)}) copy-start(bf16[4096,1,128]{2,0,1:T(8,128)(2,1)} %get-tuple-element.222) | copy-start | bytes 3145732 | tf_op jit(solution)/shard_map/cond
  168.5 2.0 copy-start
  170.5 81.9 %reduce-scatter.5.cloned.1.call-start = ((), (), s32[]{:S(2)}) async-start(), calls=%async_computation.12 | async-start | bytes 2621440 | tf_op jit(solution)/shard_map/reduce_scatter | solution.py:135
  225.7 21.9 %all-to-all-start.7 = ((f32[64,16,1]{1,2,0:T(1,128)}), f32[64,16,1]{1,2,0:T(1,128)S(1)}, u32[]{:S(2)}, u32[]{:S(2)}) async-start(f32[64,16,1]{1,2,0:T(1,128)} %bitcast.69), calls=%async_computation.8 | async-start | bytes 65536 | tf_op jit(solution)/shard_map/all_to_all | solution.py:148
  247.6 22.1 %all-to-all-start.6 = ((f32[1024,1,128]{2,1,0:T(1,128)}), f32[1024,1,128]{2,1,0:T(1,128)S(1)}, u32[]{:S(2)}, u32[]{:S(2)}) async-start(f32[1024,1,128]{2,1,0:T(1,128)} %bitcast.57), calls=%async_computation.7 | async-start | bytes 1048576 | tf_op jit(solution)/shard_map/all_to_all | solution.py:147
  269.7 140.2 %all-to-all-start.5 = ((f32[1024,1,128]{2,1,0:T(1,128)}), f32[1024,1,128]{2,1,0:T(1,128)S(1)}, u32[]{:S(2)}, u32[]{:S(2)}) async-start(f32[1024,1,128]{2,1,0:T(1,128)} %bitcast.127), calls=%async_computation.6 | async-start | bytes 1048576 | tf_op jit(solution)/shard_map/all_to_all | solution.py:146
Sparse Core Ops, SparseCore 0:
  33.5 22.2 all-gather.4
  57.6 26.8 all-gather.2
  170.6 35.9 reduce-scatter.6
  209.1 31.9 reduce-scatter.4
where the time goes:
time: 420 us; the launch traced here: 418 us
  blocking collectives  200 us (48%)
  waiting for transfers between devices  74.8 us (18%)
  starting transfers between devices  40.8 us (10%)
  matrix products  36.2 us (9%)
  local copies, waits for them, and re-layouts  26.1 us (6%)
  other arithmetic  17.7 us (4%)
  between operations  17.2 us (4%)
  loops' own time  5.42 us (1%)
    psum x1, blocking collectives, per_device(): loss = lax.psum(jnp.sum(norm), 'head') / (pairs * lax.axis_size('head'))  132 us
    unnamed x5, waiting for transfers between devices  36.1 us
    all_to_all x1, blocking collectives, per_device(): lax.all_to_all(keys, 'head', split_axis=1, concat_axis=0, tiled=True)  25.1 us
    all_to_all x1, blocking collectives, per_device(): lax.all_to_all(b_proj, 'head', split_axis=1, concat_axis=0, tiled=True)  17.9 us
    dot_general x1, matrix products, grad_work(): jnp.einsum('ipd,jpd->pij', query_all, key_part, preferred_element_type=jn...  16 us
    unnamed x16, local copies, waits for them, and re-layouts  15.7 us
    all_to_all x1, waiting for transfers between devices, per_device(): lax.all_to_all(grad_c_out, 'head', split_axis=0, concat_axis=1, tiled=True)  15.5 us
    all_to_all x1, starting transfers between devices, per_device(): lax.all_to_all(grad_step_out, 'head', split_axis=0, concat_axis=1, tiled=...  12.7 us
  transfers between devices with their start and end apart: 10, of which 5 were waited for; matrix products, arithmetic and copies ran while one was open for 9% of the time, Pallas kernels for 0%

commit v1 on v0

v1 whole, which is shorter than its diff:
```python
import functools
import math

import jax
import jax.numpy as jnp
from jax import lax
from jax.experimental import pallas as pl
from jax.experimental.pallas import tpu as pltpu
from jax.sharding import PartitionSpec as P

F32 = jnp.float32
BF16 = jnp.bfloat16
F16 = jnp.float16
LOG2E = math.log2(math.e)
TILE = 256
LOWEST = -1e30
VMEM_BYTES = 56 * 1024 * 1024


def dot_nt(a, b):
    return lax.dot_general(a, b, (((1,), (1,)), ((), ())), preferred_element_type=F32)


def dot_nn(a, b):
    return lax.dot_general(a, b, (((1,), (0,)), ((), ())), preferred_element_type=F32)


def dot_full(a, b):
    return lax.dot_general(
        a, b, (((1,), (0,)), ((), ())),
        precision=lax.Precision.HIGHEST, preferred_element_type=F32,
    )


def fold_rows(x):
    rows, cols = x.shape
    x = jnp.sum(x.reshape(rows // 8, 8, cols), axis=0)
    out = x[:, :128]
    for at in range(128, cols, 128):
        out = out + x[:, at:at + 128]
    return out


def total_of(x):
    return jnp.sum(jnp.sum(x, axis=0, keepdims=True), axis=1, keepdims=True)


def exponent_of(x):
    top = jnp.max(jnp.max(jnp.abs(x), axis=0, keepdims=True), axis=1, keepdims=True)
    return jnp.floor(jnp.log2(jnp.maximum(top, 1e-30)))


def earlier_kernel(
    scale, beta, block_ref, qc_ref, kb0_ref, kb1_ref, kb2_ref, kb3_ref, vec_ref,
    part1_ref, part2_ref, part3_ref, gc_ref, top_ref, rinv_ref, small_ref,
    q_s, c_s, ct_s, k_s, b_s, max_s, sum_s, gbt_s, cols_s, sq_s,
):
    block = block_ref[0]
    rows, width = q_s.shape
    n = qc_ref.shape[1] // 2
    tiles = rows // TILE
    q_s[...] = qc_ref[:, 0:n, :].reshape(rows, width)
    c_s[...] = qc_ref[:, n:2 * n, :].reshape(rows, width)
    ct_s[...] = jnp.transpose(c_s[...].astype(F32)).astype(BF16)
    cols_s[...] = jnp.transpose(vec_ref[...])
    kbs = (kb0_ref, kb1_ref, kb2_ref, kb3_ref)
    parts = (None, part1_ref, part2_ref, part3_ref)
    max_s[...] = jnp.full(max_s.shape, LOWEST, F32)
    sum_s[...] = jnp.zeros(sum_s.shape, F32)
    gc_ref[...] = jnp.zeros(gc_ref.shape, F32)
    small_ref[...] = jnp.zeros(small_ref.shape, F32)
    sq_s[...] = jnp.zeros(sq_s.shape, F32)

    def stats(at, d, size, masked):
        ti = pl.ds(at, TILE)
        s = dot_nt(q_s[ti, :], k_s[d, 0:size, :])
        if masked:
            row = lax.broadcasted_iota(jnp.int32, s.shape, 0) + at
            col = lax.broadcasted_iota(jnp.int32, s.shape, 1)
            s = jnp.where(col <= row, s, LOWEST)
        old = max_s[ti, :]
        new = old
        for g in range(0, size, 128):
            new = jnp.maximum(new, s[:, g:g + 128])
        acc = sum_s[ti, :] * jnp.exp2((old - new) * scale)
        for g in range(0, size, 128):
            acc = acc + jnp.exp2((s[:, g:g + 128] - new) * scale)
        max_s[ti, :] = new
        sum_s[ti, :] = acc

    for d in range(4):
        @pl.when(block >= d)
        def _(d=d):
            k_s[d, :, :] = kbs[d][:, 0:n, :].reshape(rows, width)
            b_s[d, :, :] = kbs[d][:, n:2 * n, :].reshape(rows, width)
            if d == 0:
                for it in range(tiles):
                    stats(it * TILE, 0, (it + 1) * TILE, True)
            else:
                @pl.loop(0, tiles)
                def _(it):
                    stats(pl.multiple_of(it * TILE, TILE), d, rows, False)

    top = jnp.max(max_s[...], axis=1, keepdims=True)
    total = jnp.sum(sum_s[...] * jnp.exp2((max_s[...] - top) * scale), axis=1, keepdims=True)
    top_ref[...] = jnp.broadcast_to(top, top_ref.shape)
    rinv_ref[...] = jnp.broadcast_to(1.0 / total, rinv_ref.shape)

    for d in range(1, 4):
        @pl.when(block >= d)
        def _(d=d):
            gbt_s[...] = jnp.zeros(gbt_s.shape, F32)

            @pl.loop(0, tiles)
            def _(it):
                ti = pl.ds(pl.multiple_of(it * TILE, TILE), TILE)
                q, c, ct = q_s[ti, :], c_s[ti, :], ct_s[:, ti]
                top_i = top_ref[ti, 0:1]
                rinv_i = rinv_ref[ti, 0:1]
                u_i = cols_s[ti, 3 + d:4 + d]
                gc = gc_ref[ti, :]
                sq = sq_s[...]
                for j in range(0, rows, TILE):
                    k, b = k_s[d, j:j + TILE, :], b_s[d, j:j + TILE, :]
                    v_j = vec_ref[d:d + 1, j:j + TILE]
                    teacher = jnp.exp2((dot_nt(q, k) - top_i) * scale) * rinv_i
                    decay = u_i * v_j
                    error = (dot_nt(c, b) * beta) * decay - teacher
                    sq = sq + fold_rows(error * error)
                    held = (error * decay).astype(BF16)
                    gc = gc + dot_nn(held, b)
                    gbt_s[:, j:j + TILE] += dot_nn(ct, held)
                gc_ref[ti, :] = gc
                sq_s[...] = sq

            part = jnp.transpose(gbt_s[...])
            small_ref[d:d + 1, :] = jnp.broadcast_to(
                total_of(part * b_s[d, :, :].astype(F32)) * beta, (1, 128)
            )
            e = exponent_of(part)
            parts[d][0:rows, :] = part * jnp.exp2(14.0 - e)
            parts[d][rows:, :] = jnp.broadcast_to(e, (parts[d].shape[0] - rows, width))

    small_ref[0:1, :] = jnp.broadcast_to(total_of(sq_s[...]), (1, 128))


def own_kernel(
    scale, beta, block_ref, qc_ref, kb_ref, vec_ref, top_ref, rinv_ref, gc_in_ref, small_ref,
    gc_ref, gb_ref, out_ref, q_s, c_s, ct_s, k_s, b_s, gbt_s, cols_s,
):
    block = block_ref[0]
    rows, width = q_s.shape
    n = qc_ref.shape[1] // 2
    q_s[...] = qc_ref[:, 0:n, :].reshape(rows, width)
    c_s[...] = qc_ref[:, n:2 * n, :].reshape(rows, width)
    ct_s[...] = jnp.transpose(c_s[...].astype(F32)).astype(BF16)
    k_s[...] = kb_ref[:, 0:n, :].reshape(rows, width)
    b_s[...] = kb_ref[:, n:2 * n, :].reshape(rows, width)
    cols_s[...] = jnp.transpose(vec_ref[...])
    sq = jnp.zeros((8, 128), F32)
    gbt_s[...] = jnp.zeros(gbt_s.shape, F32)
    for i in range(0, rows, TILE):
        ti = slice(i, i + TILE)
        q, c, ct = q_s[ti, :], c_s[ti, :], ct_s[:, ti]
        top_i = top_ref[ti, 0:1]
        rinv_i = rinv_ref[ti, 0:1]
        sum_i = cols_s[ti, 0:1]
        gc = gc_in_ref[ti, :]
        for j in range(0, i + TILE, TILE):
            k, b = k_s[j:j + TILE, :], b_s[j:j + TILE, :]
            sum_j = vec_ref[0:1, j:j + TILE]
            s = dot_nt(q, k) - top_i
            gap = sum_i - sum_j
            if i == j:
                row = lax.broadcasted_iota(jnp.int32, s.shape, 0)
                col = lax.broadcasted_iota(jnp.int32, s.shape, 1)
                s = jnp.where(col <= row, s, LOWEST)
                gap = jnp.where(col <= row, gap, LOWEST)
            teacher = jnp.exp2(s * scale) * rinv_i
            decay = jnp.exp2(gap * LOG2E)
            error = (dot_nt(c, b) * beta) * decay - teacher
            sq = sq + fold_rows(error * error)
            held = (error * decay).astype(BF16)
            gc = gc + dot_nn(held, b)
            gbt_s[:, j:j + TILE] += dot_nn(ct, held)
        gc_ref[ti, :] = gc
    gb_ref[...] = jnp.transpose(gbt_s[...])
    lane = lax.broadcasted_iota(jnp.int32, (1, 128), 1)
    sums = jnp.where(lane == 3, small_ref[0:1, :] + total_of(sq), 0.0)
    for d in range(1, 4):
        crosses = jnp.logical_and(lane < block, lane >= block - d)
        sums = sums + jnp.where(
            jnp.logical_and(crosses, d <= block), small_ref[d:d + 1, :], 0.0
        )
    out_ref[...] = jnp.broadcast_to(sums, out_ref.shape)


def split_scaled(x, e):
    y = x * jnp.exp2(14.0 - e)
    high = jnp.floor(y * (1.0 / 16.0)) * 16.0
    return high, y - high


def finish_kernel(
    beta, seq_len, block_ref, qc_ref, kb_ref, gc_ref, gb_ref, part1_ref, part2_ref, part3_ref,
    sums_ref, rate_ref, out_ref, gb_s,
):
    block = block_ref[0]
    heads, span, width = qc_ref.shape
    n = span // 2
    rows = heads * n
    gb_s[...] = gb_ref[...]
    for d, part in ((1, part1_ref), (2, part2_ref), (3, part3_ref)):
        @pl.when(block + d <= 3)
        def _(part=part):
            gb_s[...] += part[0:rows, :] * jnp.exp2(part[rows:rows + 1, 0:1] - 14.0)
    gb = gb_s[...]
    gc = gc_ref[...]
    c = qc_ref[:, n:2 * n, :].reshape(rows, width).astype(F32)
    b = kb_ref[:, n:2 * n, :].reshape(rows, width).astype(F32)
    slope = jnp.sum(c * gc - b * gb, axis=1, keepdims=True) * beta
    slope = jnp.broadcast_to(slope, (rows, 128)).reshape(heads, n, 128)
    place = lax.broadcasted_iota(jnp.int32, (heads, n, 128), 1)
    lane3 = lax.broadcasted_iota(jnp.int32, (heads, n, 128), 2)
    slope = jnp.sum(jnp.where(place == lane3, slope, 0.0), axis=1)
    up = lax.broadcasted_iota(jnp.int32, (128, 128), 0)
    across = lax.broadcasted_iota(jnp.int32, (128, 128), 1)
    inside = dot_full(slope, jnp.where(up >= across, 1.0, 0.0).astype(F32))
    down = lax.broadcasted_iota(jnp.int32, (heads, heads), 0)
    right = lax.broadcasted_iota(jnp.int32, (heads, heads), 1)
    whole = jnp.broadcast_to(jnp.sum(slope, axis=1, keepdims=True), (heads, 128))
    behind = dot_full(jnp.where(right > down, 1.0, 0.0).astype(F32), whole)
    lane1 = lax.broadcasted_iota(jnp.int32, (1, 128), 1)
    sums = sums_ref[0:1, :]
    after = jnp.sum(
        jnp.where(jnp.logical_and(lane1 == block, block < 3), sums, 0.0), axis=1, keepdims=True
    )
    error_sq = jnp.sum(jnp.where(lane1 == 3, sums, 0.0), axis=1, keepdims=True)
    norm = jnp.sqrt(error_sq + 1e-06)
    factor = seq_len / norm
    step = (inside + behind + after) * (-(rate_ref[0:1, 0:1] * factor))
    lane = lax.broadcasted_iota(jnp.int32, (heads, 128), 1)
    step = jnp.where(lane < n, step, 0.0)
    gb = gb * (factor * beta)
    gc = gc * (factor * beta)
    eb, ec, es, en = exponent_of(gb), exponent_of(gc), exponent_of(step), exponent_of(norm)
    out_ref[:, 0:n, :] = (gb * jnp.exp2(14.0 - eb)).reshape(heads, n, width)
    out_ref[:, n:2 * n, :] = (gc * jnp.exp2(14.0 - ec)).reshape(heads, n, width)
    high, low = split_scaled(step, es)
    norm_high, norm_low = split_scaled(norm, en)
    extra = jnp.where(lane == 0, eb, 0.0)
    for at, value in ((1, ec), (2, es), (3, norm_high), (4, norm_low), (5, en)):
        extra = jnp.where(lane == at, value, extra)
    out_ref[:, 2 * n:2 * n + 1, :] = high.reshape(heads, 1, 128)
    out_ref[:, 2 * n + 1:2 * n + 2, :] = low.reshape(heads, 1, 128)
    out_ref[:, 2 * n + 2:2 * n + 3, :] = extra.reshape(heads, 1, 128)


def unpack_kernel(x_ref, gb_ref, gc_ref, step_ref, loss_ref):
    heads = x_ref.shape[0]
    n = gb_ref.shape[0]
    extra = x_ref[:, 2 * n + 2:2 * n + 3, :].reshape(heads, 128)
    lane = lax.broadcasted_iota(jnp.int32, (heads, 128), 1)

    def pick(at):
        return jnp.sum(jnp.where(lane == at, extra, 0.0), axis=1, keepdims=True)

    scale_b, scale_c, scale_s = (jnp.exp2(pick(at) - 14.0) for at in range(3))
    norm = (pick(3) + pick(4)) * jnp.exp2(pick(5) - 14.0)
    gb_ref[...] = jnp.swapaxes(x_ref[:, 0:n, :] * scale_b[:, :, None], 0, 1)
    gc_ref[...] = jnp.swapaxes(x_ref[:, n:2 * n, :] * scale_c[:, :, None], 0, 1)
    high = x_ref[:, 2 * n:2 * n + 1, :].reshape(heads, 128)
    low = x_ref[:, 2 * n + 1:2 * n + 2, :].reshape(heads, 128)
    step = jnp.transpose((high + low) * scale_s)
    step_ref[...] = step[0:n, :]
    loss_ref[...] = jnp.broadcast_to(
        jnp.sum(norm, axis=0, keepdims=True) * (1.0 / heads), loss_ref.shape
    )


def call(kernel, out_shape, scratch, count):
    return pl.pallas_call(
        kernel,
        out_shape=out_shape,
        in_specs=[pl.BlockSpec(memory_space=pltpu.SMEM)]
        + [pl.BlockSpec(memory_space=pltpu.VMEM)] * (count - 1),
        out_specs=jax.tree.map(lambda _: pl.BlockSpec(memory_space=pltpu.VMEM), out_shape),
        scratch_shapes=scratch,
        compiler_params=pltpu.CompilerParams(vmem_limit_bytes=VMEM_BYTES),
    )


def shape(*dims, dtype=F32):
    return jax.ShapeDtypeStruct(dims, dtype)


def per_device(queries, keys, b_proj, c_proj, step_size, rate_level):
    n, heads, width = queries.shape
    blocks = lax.axis_size("seq")
    block = lax.axis_index("seq")
    rows = n * heads
    seq_len = rows * blocks
    beta = 2.0 / math.sqrt(width * seq_len)
    scale = LOG2E / math.sqrt(width)

    def to_heads(x):
        return lax.all_to_all(x, "head", split_axis=0, concat_axis=0, tiled=True)

    def flip(x):
        return jnp.swapaxes(x, 0, 1)

    steps = jnp.pad(jnp.transpose(step_size)[:, None, :], ((0, 0), (0, 0), (0, 128 - n % 128 if n % 128 else 0)))
    pad_rows = steps.shape[2] // 128
    steps = steps.reshape(heads, pad_rows, 128)
    kb = to_heads(jnp.concatenate([flip(keys), flip(b_proj), steps], axis=1))
    kb_from = [
        lax.ppermute(kb, "seq", [(i, i + d) for i in range(blocks - d)]) for d in range(1, blocks)
    ]
    qc_mine = jnp.concatenate([flip(queries), flip(c_proj)], axis=1)
    qc_mine, _ = lax.optimization_barrier((qc_mine, kb))
    qc = to_heads(qc_mine)

    rate = jnp.exp2(-0.5 * rate_level.astype(F32))
    dt = jnp.stack([x[:, 2 * n:, :].reshape(heads, -1)[:, :n] for x in [kb] + kb_from])
    local = jnp.cumsum(-rate * dt.reshape(blocks, rows).astype(F32), axis=1)
    total = local[:, -1]
    before = jnp.exp(total[1:, None] - local[1:])
    middle = jnp.stack([jnp.zeros((), F32), total[1], total[1] + total[2]])
    since = jnp.exp(local[0][None] + middle[:, None])
    vec = jnp.concatenate([local[:1], before, since, jnp.zeros((1, rows), F32)], axis=0)

    where = jnp.reshape(block, (1,)).astype(jnp.int32)
    part_rows = rows + 16
    mat = pltpu.VMEM((rows, width), BF16)
    cols = pltpu.VMEM((rows, 8), F32)
    part1, part2, part3, gc, top, rinv, small = call(
        functools.partial(earlier_kernel, scale, beta),
        [shape(part_rows, width)] * 3 + [shape(rows, width)] * 3 + [shape(8, 128)],
        [
            mat, mat, pltpu.VMEM((width, rows), BF16),
            pltpu.VMEM((4, rows, width), BF16), pltpu.VMEM((4, rows, width), BF16),
            pltpu.VMEM((rows, 128), F32), pltpu.VMEM((rows, 128), F32),
            pltpu.VMEM((width, rows), F32), cols, pltpu.VMEM((8, 128), F32),
        ],
        7,
    )(where, qc, kb, *kb_from, vec)
    got = [
        lax.ppermute(part.astype(F16), "seq", [(i, i - d) for i in range(d, blocks)]).astype(F32)
        for d, part in ((1, part1), (2, part2), (3, part3))
    ]
    gc, gb, small = call(
        functools.partial(own_kernel, scale, beta),
        [shape(rows, width), shape(rows, width), shape(8, 128)],
        [
            mat, mat, pltpu.VMEM((width, rows), BF16), mat, mat,
            pltpu.VMEM((width, rows), F32), cols,
        ],
        8,
    )(where, qc, kb, vec, top, rinv, gc, small)
    sums = lax.psum(small, "seq")
    rates = jnp.broadcast_to(rate[None, :], (8, 128))
    packed = call(
        functools.partial(finish_kernel, beta, float(seq_len)),
        shape(heads, 2 * n + 3, width),
        [pltpu.VMEM((rows, width), F32)],
        10,
    )(where, qc, kb, gc, gb, *got, sums, rates)
    back = to_heads(packed.astype(F16)).astype(F32)
    grad_b, grad_c, grad_step, loss = pl.pallas_call(
        unpack_kernel,
        out_shape=[
            shape(n, heads, width), shape(n, heads, width), shape(n, heads), shape(8, 128),
        ],
        compiler_params=pltpu.CompilerParams(vmem_limit_bytes=VMEM_BYTES),
    )(back)
    return grad_b, grad_c, grad_step, loss[0, 0]


def solution(mesh):
    tokens = P(("seq", "head"), None, None)
    return jax.shard_map(
        per_device,
        mesh=mesh,
        in_specs=(tokens, tokens, tokens, tokens, P(("seq", "head"), None), P("head")),
        out_specs=(tokens, tokens, P(("seq", "head"), None), P()),
        check_vma=False,
    )
```

time: 420 us -> 165 us (0.39)
  blocking collectives: 200 us -> 91.5 us
  waiting for transfers between devices: 74.8 us -> 12.3 us
  matrix products: 36.2 us -> 0 us
  starting transfers between devices: 40.8 us -> 19.7 us
  Pallas kernels: 0 us -> 16.9 us
  local copies, waits for them, and re-layouts: 26.1 us -> 10.2 us
  between operations: 17.2 us -> 2.83 us
  other arithmetic: 17.7 us -> 11.3 us
  loops' own time: 5.42 us -> 0 us
    psum x2 -> x1, blocking collectives: 139 us -> 30.2 us  [per_device(): sums = lax.psum(small, 'seq')]
    all_to_all x6 -> x1, waiting for transfers between devices: 38.6 us -> 0.01 us  [to_heads(): return lax.all_to_all(x, 'head', split_axis=0, concat_axis=0, tiled=True)]
    dot_general x5 -> x0, matrix products: 36.2 us -> none  [the longest x1 16 us: grad_work(): jnp.einsum('ipd,jpd->pij', query_all, key_part, preferred_element_type=jn...]
    unnamed x5 -> x0, waiting for transfers between devices: 36.1 us -> none
    all_to_all x6 -> x1, starting transfers between devices: 40.6 us -> 6.82 us  [to_heads(): return lax.all_to_all(x, 'head', split_axis=0, concat_axis=0, tiled=True)]
    all_to_all x2, blocking collectives: 43 us -> 61.3 us  [to_heads(): return lax.all_to_all(x, 'head', split_axis=0, concat_axis=0, tiled=True)]
    pallas_call x0 -> x4, Pallas kernels: none -> 16.9 us  [the longest x1 5.07 us: per_device(): call(functools.partial(earlier_kernel, scale, beta), [shape(part_rows, wi...]
    unnamed x16 -> x14, local copies, waits for them, and re-layouts: 15.7 us -> 0.93 us
  transfers between devices with their start and end apart: 10 -> 7, of which waited for: 5 -> 2; matrix products, arithmetic and copies ran while one was open for 9% -> 7% of each run, Pallas kernels for 0% -> 3%
where the time goes in v1:
time: 165 us
  blocking collectives  91.5 us (55%)
  starting transfers between devices  19.7 us (12%)
  Pallas kernels  16.9 us (10%)
  waiting for transfers between devices  12.3 us (7%)
  other arithmetic  11.3 us (7%)
  local copies, waits for them, and re-layouts  10.2 us (6%)
  between operations  2.83 us (2%)
    all_to_all x2, blocking collectives, to_heads(): return lax.all_to_all(x, 'head', split_axis=0, concat_axis=0, tiled=True)  61.3 us
    psum x1, blocking collectives, per_device(): sums = lax.psum(small, 'seq')  30.2 us
    ppermute x3, waiting for transfers between devices, per_device(): lax.ppermute(kb, 'seq', [(i, i + d) for i in range(blocks - d)])  12.3 us
    ppermute x3, starting transfers between devices, per_device(): lax.ppermute(kb, 'seq', [(i, i + d) for i in range(blocks - d)])  8.82 us
    all_to_all x1, starting transfers between devices, to_heads(): return lax.all_to_all(x, 'head', split_axis=0, concat_axis=0, tiled=True)  6.82 us
    pallas_call x1, Pallas kernels, per_device(): call(functools.partial(earlier_kernel, scale, beta), [shape(part_rows, wi...  5.07 us
    pallas_call x1, Pallas kernels, per_device(): call(functools.partial(own_kernel, scale, beta), [shape(rows, width), sha...  5.07 us
    pallas_call x1, Pallas kernels, per_device(): call(functools.partial(finish_kernel, beta, float(seq_len)), shape(heads,...  4.22 us
  transfers between devices with their start and end apart: 7, of which 2 were waited for; matrix products, arithmetic and copies ran while one was open for 7% of the time, Pallas kernels for 3%

profile of v1, /device:TPU:1, one launch (start us, length us, event | category | flops | bytes accessed | tf_op | source)
XLA Modules:
  0.0 164.8 jit_solution(16395440033384116175)
XLA Ops:
  1.4 1.4 copy_bitcast_fusion
  2.9 33.2 %all_to_all.15.kb0_ref.kb_ref = bf16[64,33,128]{2,1,0:T(8,128)(2,1)S(1)} all-to-all(bf16[64,33,128]{2,1,0:T(8,128)(2,1)S(1)} %fusion.1), channel_id=1, replica_groups=mesh['seq'=4,'head'=64] {'head'}, dimensions={0} | all-to-all | bytes 1081344 | tf_op jit(solution)/shard_map/all_to_all | solution.py:307
  36.2 3.1 %collective-permute-start = (bf16[64,33,128]{2,0,1:T(8,128)(2,1)S(1)}, bf16[64,33,128]{2,0,1:T(8,128)(2,1)S(1)}, u32[]{:S(2)}, u32[]{:S(2)}) collective-permute-start(bf16[64,33,128]{2,0,1:T(8,128)(2,1)S(1)} %copy.27), channel_id=1, source_target_pairs={{0,64},{64,128},{128,192},{1,65},{65,129},{129,193},{2,66},{66,130... | collective-permute-start | bytes 1622024 | tf_op jit(solution)/shard_map/ppermute | solution.py:317
  40.2 4.3 %collective-permute-start.1 = (bf16[64,33,128]{2,0,1:T(8,128)(2,1)S(1)}, bf16[64,33,128]{2,0,1:T(8,128)(2,1)S(1)}, u32[]{:S(2)}, u32[]{:S(2)}) collective-permute-start(bf16[64,33,128]{2,0,1:T(8,128)(2,1)S(1)} %copy.27), channel_id=1, source_target_pairs={{0,128},{64,192},{1,129},{65,193},{2,130},{66,194},{3,131},{67,195... | collective-permute-start | bytes 1622024 | tf_op jit(solution)/shard_map/ppermute | solution.py:317
  44.9 1.3 collective-permute-start.2
  47.2 6.8 %all-to-all-start.1 = ((bf16[64,32,128]{2,1,0:T(8,128)(2,1)}), bf16[64,32,128]{2,1,0:T(8,128)(2,1)S(1)}, u32[]{:S(2)}, u32[]{:S(2)}) async-start(bf16[64,32,128]{2,1,0:T(8,128)(2,1)} %pad_maximum_fusion), calls=%async_computation.1 | async-start | bytes 1048576 | tf_op jit(solution)/shard_map/all_to_all | solution.py:307
  54.1 8.2 %collective-permute-done.1 = bf16[64,33,128]{2,0,1:T(8,128)(2,1)S(1)} collective-permute-done((bf16[64,33,128]{2,0,1:T(8,128)(2,1)S(1)}, bf16[64,33,128]{2,0,1:T(8,128)(2,1)S(1)}, u32[]{:S(2)}, u32[]{:S(2)}) %collective-permute-start.1) | collective-permute-done | bytes 540704 | tf_op jit(solution)/shard_map/ppermute | solution.py:317
  62.4 4.1 %collective-permute-done.2 = bf16[64,33,128]{2,0,1:T(8,128)(2,1)S(1)} collective-permute-done((bf16[64,33,128]{2,0,1:T(8,128)(2,1)S(1)}, bf16[64,33,128]{2,0,1:T(8,128)(2,1)S(1)}, u32[]{:S(2)}, u32[]{:S(2)}) %collective-permute-start.2) | collective-permute-done | bytes 540704 | tf_op jit(solution)/shard_map/ppermute | solution.py:317
  66.6 1.1 reduce-window.6
  70.4 1.2 copy.31.kb1_ref
  71.5 1.2 copy.32.kb2_ref
  72.8 1.2 copy.33.kb3_ref
  76.4 5.1 %shard_map.93 = (f32[1040,128]{1,0:T(8,128)}, f32[1040,128]{1,0:T(8,128)}, f32[1040,128]{1,0:T(8,128)}, f32[1024,128]{1,0:T(8,128)}, f32[1024,128]{1,0:T(8,128)}, /*index=5*/f32[1024,128]{1,0:T(8,128)}, f32[8,128]{1,0:T(8,128)}) custom-call(s32[1]{0:T(128)} %bitcast.block_ref, bf16[64,32,128]{2,1,0:T(8,128)(2,1)} %copy-done.1, bf16[64,33,128]{2,1,0:T(8,128)(2,1)} %copy-done, ...), custom_call_target="tpu_custom_call" | custom-call | tf_op jit(solution)/shard_map/pallas_call | solution.py:336
  82.6 1.3 collective-permute-start.3
  85.0 1.3 collective-permute-start.4
  86.3 1.5 collective-permute-start.5
  87.8 5.1 %shard_map.94 = (f32[1024,128]{1,0:T(8,128)}, f32[1024,128]{1,0:T(8,128)}, f32[8,128]{1,0:T(8,128)}) custom-call(s32[1]{0:T(128)} %bitcast.block_ref, bf16[64,32,128]{2,1,0:T(8,128)(2,1)} %copy-done.1, bf16[64,33,128]{2,1,0:T(8,128)(2,1)} %copy-done, f32[8,1024]{1,0:T(8,128)} %maximum_maximum_fusion.vec_ref, f32[1024,128]{1,0:T(8,128)} %get-tuple-element.20.top_ref, ...), custom_call_target="tpu_custom_call" | custom-call | tf_op jit(solution)/shard_map/pallas_call | solution.py:351
  92.9 30.2 %psum.7.sums_ref = f32[8,128]{1,0:T(8,128)} all-reduce(f32[8,128]{1,0:T(8,128)} %get-tuple-element.29), channel_id=1, replica_groups=mesh['seq'=4,'head'=64] {'seq'}, use_global_device_ids=true, to_apply=%region_2.3 | all-reduce | flops 1024 | bytes 8192 | tf_op jit(solution)/shard_map/psum | solution.py:360
  126.2 4.2 %shard_map.95 = f32[64,35,128]{2,1,0:T(8,128)} custom-call(s32[1]{0:T(128)} %bitcast.block_ref, bf16[64,32,128]{2,1,0:T(8,128)(2,1)} %copy-done.1, bf16[64,33,128]{2,1,0:T(8,128)(2,1)} %copy-done, f32[1024,128]{1,0:T(8,128)} %get-tuple-element.24.gc_ref, f32[1024,128]{1,0:T(8,128)} %get-tuple-element.25.gb_ref, f32[1040,128]{1,0:T(8,128)} %convert_element_type.36.part1_ref, ...), custom_call_target="tpu_custom_call" | custom-call | tf_op jit(solution)/shard_map/pallas_call | solution.py:362
  130.4 1.4 convert_element_type.41
  131.8 28.1 %all_to_all.16 = f16[64,35,128]{2,1,0:T(8,128)(2,1)S(1)} all-to-all(f16[64,35,128]{2,1,0:T(8,128)(2,1)S(1)} %convert_element_type.41), channel_id=1, replica_groups=mesh['seq'=4,'head'=64] {'head'}, dimensions={0} | all-to-all | bytes 1146880 | tf_op jit(solution)/shard_map/all_to_all | solution.py:307
  159.9 1.2 convert_element_type.42.x_ref
  161.0 2.5 %shard_map.96 = (f32[16,64,128]{2,1,0:T(8,128)}, f32[16,64,128]{2,1,0:T(8,128)}, f32[16,64]{1,0:T(8,128)}, f32[8,128]{1,0:T(8,128)}) custom-call(f32[64,35,128]{2,1,0:T(8,128)} %convert_element_type.42.x_ref), custom_call_target="tpu_custom_call" | custom-call | tf_op jit(solution)/shard_map/pallas_call | solution.py:369
  163.6 1.2 slice.83
  (52 shorter events, 11.6 us)
Async XLA Ops:
  2.9 41.6 %copy-start.3 = (bf16[16,64,128]{2,1,0:T(8,128)(2,1)S(1)}, bf16[16,64,128]{2,1,0:T(8,128)(2,1)}, u32[]{:S(2)}) copy-start(bf16[16,64,128]{2,1,0:T(8,128)(2,1)} %param.9) | copy-start | bytes 786436
  2.9 41.6 %copy-start.4 = (bf16[16,64,128]{2,1,0:T(8,128)(2,1)S(1)}, bf16[16,64,128]{2,1,0:T(8,128)(2,1)}, u32[]{:S(2)}) copy-start(bf16[16,64,128]{2,1,0:T(8,128)(2,1)} %param.6) | copy-start | bytes 786436
  36.1 10.9 %copy-start = (bf16[64,33,128]{2,1,0:T(8,128)(2,1)}, bf16[64,33,128]{2,1,0:T(8,128)(2,1)S(1)}, u32[]{:S(2)}) copy-start(bf16[64,33,128]{2,1,0:T(8,128)(2,1)S(1)} %all_to_all.15.kb0_ref.kb_ref) | copy-start | bytes 1622020
  36.2 17.8 %collective-permute-start = (bf16[64,33,128]{2,0,1:T(8,128)(2,1)S(1)}, bf16[64,33,128]{2,0,1:T(8,128)(2,1)S(1)}, u32[]{:S(2)}, u32[]{:S(2)}) collective-permute-start(bf16[64,33,128]{2,0,1:T(8,128)(2,1)S(1)} %copy.27), channel_id=1, source_target_pairs={{0,64},{64,128},{128,192},{1,65},{65,129},{129,193},{2,66},{66,130... | collective-permute-start | bytes 1622024 | tf_op jit(solution)/shard_map/ppermute | solution.py:317
  40.2 22.1 %collective-permute-start.1 = (bf16[64,33,128]{2,0,1:T(8,128)(2,1)S(1)}, bf16[64,33,128]{2,0,1:T(8,128)(2,1)S(1)}, u32[]{:S(2)}, u32[]{:S(2)}) collective-permute-start(bf16[64,33,128]{2,0,1:T(8,128)(2,1)S(1)} %copy.27), channel_id=1, source_target_pairs={{0,128},{64,192},{1,129},{65,193},{2,130},{66,194},{3,131},{67,195... | collective-permute-start | bytes 1622024 | tf_op jit(solution)/shard_map/ppermute | solution.py:317
  44.9 21.7 %collective-permute-start.2 = (bf16[64,33,128]{2,0,1:T(8,128)(2,1)S(1)}, bf16[64,33,128]{2,0,1:T(8,128)(2,1)S(1)}, u32[]{:S(2)}, u32[]{:S(2)}) collective-permute-start(bf16[64,33,128]{2,0,1:T(8,128)(2,1)S(1)} %copy.27), channel_id=1, source_target_pairs={{0,192},{1,193},{2,194},{3,195},{4,196},{5,197},{6,198},{7,199},{8... | collective-permute-start | bytes 1622024 | tf_op jit(solution)/shard_map/ppermute | solution.py:317
  47.2 28.4 %all-to-all-start.1 = ((bf16[64,32,128]{2,1,0:T(8,128)(2,1)}), bf16[64,32,128]{2,1,0:T(8,128)(2,1)S(1)}, u32[]{:S(2)}, u32[]{:S(2)}) async-start(bf16[64,32,128]{2,1,0:T(8,128)(2,1)} %pad_maximum_fusion), calls=%async_computation.1 | async-start | bytes 1048576 | tf_op jit(solution)/shard_map/all_to_all | solution.py:307
  75.6 0.8 copy-start.1
  81.4 4.8 %copy-start.2 = (f32[1040,128]{1,0:T(8,128)S(1)}, f32[1040,128]{1,0:T(8,128)}, u32[]{:S(2)}) copy-start(f32[1040,128]{1,0:T(8,128)} %get-tuple-element.28) | copy-start | bytes 1597444
  82.6 40.5 %collective-permute-start.3 = (f16[1040,128]{1,0:T(8,128)(2,1)S(1)}, f16[1040,128]{1,0:T(8,128)(2,1)S(1)}, u32[]{:S(2)}, u32[]{:S(2)}) collective-permute-start(f16[1040,128]{1,0:T(8,128)(2,1)S(1)} %convert_element_type.35), channel_id=1, source_target_pairs={{64,0},{128,64},{192,128},{65,1},{129,65},{193,129},{66,2},{130,66... | collective-permute-start | bytes 798728 | tf_op jit(solution)/shard_map/ppermute | solution.py:348
  85.0 39.0 %collective-permute-start.4 = (f16[1040,128]{1,0:T(8,128)(2,1)S(1)}, f16[1040,128]{1,0:T(8,128)(2,1)S(1)}, u32[]{:S(2)}, u32[]{:S(2)}) collective-permute-start(f16[1040,128]{1,0:T(8,128)(2,1)S(1)} %convert_element_type.37), channel_id=1, source_target_pairs={{128,0},{192,64},{129,1},{193,65},{130,2},{194,66},{131,3},{195,67... | collective-permute-start | bytes 798728 | tf_op jit(solution)/shard_map/ppermute | solution.py:348
  86.3 38.5 %collective-permute-start.5 = (f16[1040,128]{1,0:T(8,128)(2,1)S(1)}, f16[1040,128]{1,0:T(8,128)(2,1)S(1)}, u32[]{:S(2)}, u32[]{:S(2)}) collective-permute-start(f16[1040,128]{1,0:T(8,128)(2,1)S(1)} %convert_element_type.39), channel_id=1, source_target_pairs={{192,0},{193,1},{194,2},{195,3},{196,4},{197,5},{198,6},{199,7},{2... | collective-permute-start | bytes 798728 | tf_op jit(solution)/shard_map/ppermute | solution.py:348

commit v2 on v1

v2 whole, which is shorter than its diff:
```python
import functools
import math

import jax
import jax.numpy as jnp
from jax import lax
from jax.experimental import pallas as pl
from jax.experimental.pallas import tpu as pltpu
from jax.sharding import PartitionSpec as P

F32 = jnp.float32
BF16 = jnp.bfloat16
F16 = jnp.float16
LOG2E = math.log2(math.e)
TILE = 256
WIDE = 512
OWN = 512
LOWEST = -1e30
VMEM_BYTES = 32 * 1024 * 1024


def dot_nt(a, b):
    return lax.dot_general(a, b, (((1,), (1,)), ((), ())), preferred_element_type=F32)


def dot_nn(a, b):
    return lax.dot_general(a, b, (((1,), (0,)), ((), ())), preferred_element_type=F32)


def dot_full(a, b):
    return lax.dot_general(
        a, b, (((1,), (0,)), ((), ())),
        precision=lax.Precision.HIGHEST, preferred_element_type=F32,
    )


def fold_rows(x):
    rows, cols = x.shape
    x = jnp.sum(x.reshape(rows // 8, 8, cols), axis=0)
    out = x[:, :128]
    for at in range(128, cols, 128):
        out = out + x[:, at:at + 128]
    return out


def total_of(x):
    return jnp.sum(jnp.sum(x, axis=0, keepdims=True), axis=1, keepdims=True)


def exponent_of(x):
    top = jnp.max(jnp.max(jnp.abs(x), axis=0, keepdims=True), axis=1, keepdims=True)
    return jnp.floor(jnp.log2(jnp.maximum(top, 1e-30)))


def sums_rows(log_decay, rows, n):
    heads, lanes = log_decay.shape
    up = lax.broadcasted_iota(jnp.int32, (lanes, lanes), 0)
    across = lax.broadcasted_iota(jnp.int32, (lanes, lanes), 1)
    same = up // n == across // n
    inside = dot_full(log_decay, jnp.where(same & (up <= across), 1.0, 0.0).astype(F32))
    whole = dot_full(log_decay, jnp.where(same, 1.0, 0.0).astype(F32))
    down = lax.broadcasted_iota(jnp.int32, (heads, heads), 0)
    right = lax.broadcasted_iota(jnp.int32, (heads, heads), 1)
    sums = inside + dot_full(jnp.where(right < down, 1.0, 0.0).astype(F32), whole)
    lane = lax.broadcasted_iota(jnp.int32, (lanes, rows), 0)
    place = lax.broadcasted_iota(jnp.int32, (lanes, rows), 1)
    owner = lax.broadcasted_iota(jnp.int32, (heads, rows), 0)
    token = lax.broadcasted_iota(jnp.int32, (heads, rows), 1)
    high = sums.astype(BF16)
    rest = sums - high.astype(F32)
    mid = rest.astype(BF16)
    low = (rest - mid.astype(F32)).astype(BF16)
    terms = jnp.concatenate([high, mid, low], axis=0)
    pick = jnp.where(lane == place % n, 1.0, 0.0).astype(BF16)
    spread = dot_nn(terms, pick)
    spread = spread[0:heads] + spread[heads:2 * heads] + spread[2 * heads:]
    return jnp.sum(jnp.where(token // n == owner, spread, 0.0), axis=0, keepdims=True)


def split_scaled(x, e):
    y = x * jnp.exp2(14.0 - e)
    high = jnp.floor(y * (1.0 / 16.0)) * 16.0
    return high, y - high


def add_stats(s, scale, max_ref, sum_ref, ti, first):
    new = LOWEST if first else max_ref[ti, :]
    size = s.shape[1]
    for g in range(0, size, 128):
        new = jnp.maximum(new, s[:, g:g + 128])
    acc = 0.0 if first else sum_ref[ti, :] * jnp.exp2((max_ref[ti, :] - new) * scale)
    for g in range(0, size, 128):
        acc = acc + jnp.exp2((s[:, g:g + 128] - new) * scale)
    max_ref[ti, :] = new
    sum_ref[ti, :] = acc


def take(ref, at, n):
    heads, _, width = ref.shape
    return ref[:, at * n:(at + 1) * n, :].reshape(heads * n, width)


def pack_kernel(*refs):
    x_ref, y_ref, out_ref = refs[0], refs[1], refs[-1]
    n, heads, _ = x_ref.shape
    out_ref[:, 0:n, :] = jnp.swapaxes(x_ref[...], 0, 1)
    out_ref[:, n:2 * n, :] = jnp.swapaxes(y_ref[...], 0, 1)
    if len(refs) == 4:
        steps = refs[2][...].astype(F32)
        steps = jnp.concatenate([steps, jnp.zeros((128 - n, heads), F32)], axis=0)
        out_ref[:, 2 * n:2 * n + 1, :] = jnp.transpose(steps).reshape(heads, 1, 128).astype(BF16)


def own_stats_kernel(n, scale, level_ref, kq_ref, local_ref, max_ref, sum_ref):
    rows = max_ref.shape[0]
    heads = kq_ref.shape[0]
    k, q = take(kq_ref, 0, n), take(kq_ref, 1, n)
    for at in range(0, rows, TILE):
        ti = slice(at, at + TILE)
        s = dot_nt(q[ti, :], k[0:at + TILE, :])
        row = lax.broadcasted_iota(jnp.int32, s.shape, 0) + at
        col = lax.broadcasted_iota(jnp.int32, s.shape, 1)
        add_stats(jnp.where(col <= row, s, LOWEST), scale, max_ref, sum_ref, ti, True)

    level = jnp.full((1, 1), level_ref[0], jnp.int32).astype(F32)
    steps = kq_ref[:, 2 * n:2 * n + 1, :].astype(F32).reshape(heads, 128)
    local = sums_rows(-jnp.exp2(-0.5 * level) * steps, rows, n)
    local_ref[...] = jnp.broadcast_to(local, local_ref.shape)


def stats_kernel(
    n, scale, block_ref, kq_ref, in1_ref, in2_ref, in3_ref, max_ref, sum_ref,
    local0_ref, local1_ref, local2_ref, local3_ref, out_ref, vec_ref, q_s, k_s, max_s, sum_s,
):
    block = block_ref[0]
    q_s[...] = take(kq_ref, 1, n)
    max_s[...] = max_ref[...]
    sum_s[...] = sum_ref[...]
    for d, in_ref in enumerate((in1_ref, in2_ref, in3_ref)):
        k_s[d + 1, :, :] = take(in_ref, 0, n)

    rows = q_s.shape[0]
    local = [x[0:1, :] for x in (local0_ref, local1_ref, local2_ref, local3_ref)]
    ends = [x[:, rows - 1:rows] for x in local]
    vec_ref[0:1, :] = local[0]
    vec_ref[7:8, :] = jnp.zeros((1, rows), F32)
    for d in range(1, 4):
        nearer, farther = jnp.zeros((1, 1), F32), jnp.zeros((1, 1), F32)
        for g in range(1, d):
            nearer = nearer + ends[g]
        for g in range(d + 1, 4):
            farther = farther + ends[g]
        row_side = block >= d
        v = jnp.where(row_side, ends[d] - local[d], ends[0] - local[0])
        u = jnp.where(row_side, local[0] + nearer, local[d] + farther)
        vec_ref[d:d + 1, :] = jnp.exp2(v * LOG2E)
        vec_ref[3 + d:4 + d, :] = jnp.exp2(u * LOG2E)

    @pl.loop(1, block + 1)
    def _(d):
        add_stats(dot_nt(q_s[...], k_s[d]), scale, max_s, sum_s, slice(None), False)

    top = jnp.max(max_s[...], axis=1, keepdims=True)
    total = jnp.sum(sum_s[...] * jnp.exp2((max_s[...] - top) * scale), axis=1, keepdims=True)
    lane = lax.broadcasted_iota(jnp.int32, (rows, 8), 1)
    out_ref[...] = jnp.transpose(jnp.where(lane == 0, top, 1.0 / total))


def rows_kernel(
    n, scale, beta, block_ref, kq_ref, bc_ref, k1_ref, k2_ref, k3_ref, b1_ref, b2_ref, b3_ref,
    vec_ref, stats_ref, gc_ref, gb_ref, out_ref, q_s, c_s, k_s, b_s, gbt_s, cols_s, u_s, sq_s, cross_s,
):
    block = block_ref[0]
    rows, width = q_s.shape
    k_s[0, :, :] = take(kq_ref, 0, n)
    b_s[0, :, :] = take(bc_ref, 0, n)
    q_s[...] = take(kq_ref, 1, n)
    c_s[...] = take(bc_ref, 1, n)
    ct = jnp.transpose(c_s[...].astype(F32)).astype(BF16)
    for d, (k_ref, b_ref) in enumerate(((k1_ref, b1_ref), (k2_ref, b2_ref), (k3_ref, b3_ref))):
        k_s[d + 1, :, :] = take(k_ref, 0, n)
        b_s[d + 1, :, :] = take(b_ref, 0, n)
    place = lax.broadcasted_iota(jnp.int32, (8, rows), 0)
    vec = vec_ref[...]
    cols_s[...] = jnp.transpose(
        jnp.where(place == 1, stats_ref[0:1, :], jnp.where(place == 2, stats_ref[1:2, :], vec))
    )
    spread = jnp.transpose(vec)
    for d in range(1, 4):
        u_s[d, :, :] = spread[:, 3 + d:4 + d]

    sq = jnp.zeros((8, 128), F32)
    gbt_s[...] = jnp.zeros(gbt_s.shape, F32)
    for i in range(0, rows, OWN):
        ti = slice(i, i + OWN)
        q, c = q_s[ti, :], c_s[ti, :]
        top_i, rinv_i, sum_i = cols_s[ti, 1:2], cols_s[ti, 2:3], cols_s[ti, 0:1]
        gc = 0.0
        for j in range(0, i + OWN, OWN):
            tj = slice(j, j + OWN)
            k, b = k_s[0, tj, :], b_s[0, tj, :]
            s = dot_nt(q, k) - top_i
            gap = sum_i - vec_ref[0:1, tj]
            if i == j:
                row = lax.broadcasted_iota(jnp.int32, s.shape, 0)
                col = lax.broadcasted_iota(jnp.int32, s.shape, 1)
                s = jnp.where(col <= row, s, LOWEST)
                gap = jnp.where(col <= row, gap, LOWEST)
            teacher = jnp.exp2(s * scale) * rinv_i
            decay = jnp.exp2(gap * LOG2E)
            error = (dot_nt(c, b) * beta) * decay - teacher
            sq = sq + fold_rows(error * error)
            held = (error * decay).astype(BF16)
            gc = gc + dot_nn(held, b)
            gbt_s[:, tj] += dot_nn(ct[:, ti], held)
        gc_ref[ti, :] = gc
    gb_ref[...] = jnp.transpose(gbt_s[...])
    sq_s[...] = sq
    cross_s[...] = jnp.zeros(cross_s.shape, F32)
    lane = lax.broadcasted_iota(jnp.int32, (1, 128), 1)

    @pl.loop(1, block + 1)
    def _(d):
        q, c = q_s[...], c_s[...]
        top_i, rinv_i, u_i = cols_s[:, 1:2], cols_s[:, 2:3], u_s[d]
        gc = 0.0
        sq = sq_s[...]
        for j in range(0, rows, WIDE):
            tj = slice(j, j + WIDE)
            k, b = k_s[d, tj, :], b_s[d, tj, :]
            teacher = jnp.exp2((dot_nt(q, k) - top_i) * scale) * rinv_i
            decay = u_i * vec_ref[pl.ds(d, 1), tj]
            error = (dot_nt(c, b) * beta) * decay - teacher
            sq = sq + fold_rows(error * error)
            gc = gc + dot_nn((error * decay).astype(BF16), b)
        cross = total_of(gc * c.astype(F32)) * beta
        cross_s[...] += jnp.where((lane < block) & (lane >= block - d), cross, 0.0)
        gc_ref[...] += gc
        sq_s[...] = sq

    sums = jnp.where(lane == 3, total_of(sq_s[...]), cross_s[...])
    out_ref[...] = jnp.broadcast_to(sums, out_ref.shape)


def cols_kernel(
    n, scale, beta, block_ref, kq_ref, bc_ref, q1_ref, q2_ref, q3_ref, c1_ref, c2_ref, c3_ref,
    vec_ref, st1_ref, st2_ref, st3_ref, gb_in_ref, sums_in_ref, gb_ref, sums_ref,
    k_s, b_s, q_s, c_s, cols_s, gbt_s,
):
    block = block_ref[0]
    rows, width = k_s.shape
    sums_ref[...] = sums_in_ref[...]
    k_s[...] = take(kq_ref, 0, n)
    b_s[...] = take(bc_ref, 0, n)
    place = lax.broadcasted_iota(jnp.int32, (8, rows), 0)
    incoming = ((q1_ref, c1_ref, st1_ref), (q2_ref, c2_ref, st2_ref), (q3_ref, c3_ref, st3_ref))
    for d, (q_ref, c_ref, st_ref) in enumerate(incoming):
        q_s[d + 1, :, :] = take(q_ref, 0, n)
        c_s[d + 1, :, :] = take(c_ref, 0, n)
        cols_s[d + 1, :, :] = jnp.transpose(
            jnp.where(place == 0, st_ref[0:1, :],
                      jnp.where(place == 1, st_ref[1:2, :], vec_ref[4 + d:5 + d, :]))
        )
    gbt_s[...] = jnp.zeros(gbt_s.shape, F32)

    @pl.loop(block + 1, 4)
    def _(d):
        q, c = q_s[d], c_s[d]
        ct = jnp.transpose(c.astype(F32)).astype(BF16)
        top_i, rinv_i, u_i = cols_s[d, :, 0:1], cols_s[d, :, 1:2], cols_s[d, :, 2:3]
        for j in range(0, rows, WIDE):
            tj = slice(j, j + WIDE)
            k, b = k_s[tj, :], b_s[tj, :]
            teacher = jnp.exp2((dot_nt(q, k) - top_i) * scale) * rinv_i
            decay = u_i * vec_ref[pl.ds(d, 1), tj]
            error = (dot_nt(c, b) * beta) * decay - teacher
            gbt_s[:, tj] += dot_nn(ct, (error * decay).astype(BF16))

    gb_ref[...] = gb_in_ref[...] + jnp.transpose(gbt_s[...])


def finish_kernel(
    n, beta, seq_len, block_ref, level_ref, bc_ref, gc_ref, gb_ref,
    sums0_ref, sums1_ref, sums2_ref, sums3_ref, out_ref,
):
    block = block_ref[0]
    heads, _, width = bc_ref.shape
    rows = heads * n
    gb = gb_ref[...]
    gc = gc_ref[...]
    c = take(bc_ref, 1, n).astype(F32)
    b = take(bc_ref, 0, n).astype(F32)
    slope = jnp.sum(c * gc - b * gb, axis=1, keepdims=True) * beta
    slope = jnp.broadcast_to(slope, (rows, 128)).reshape(heads, n, 128)
    place = lax.broadcasted_iota(jnp.int32, (heads, n, 128), 1)
    lane3 = lax.broadcasted_iota(jnp.int32, (heads, n, 128), 2)
    slope = jnp.sum(jnp.where(place == lane3 % n, slope, 0.0), axis=1)
    up = lax.broadcasted_iota(jnp.int32, (128, 128), 0)
    across = lax.broadcasted_iota(jnp.int32, (128, 128), 1)
    same = up // n == across // n
    inside = dot_full(slope, jnp.where(same & (up >= across), 1.0, 0.0).astype(F32))
    whole = dot_full(slope, jnp.where(same, 1.0, 0.0).astype(F32))
    down = lax.broadcasted_iota(jnp.int32, (heads, heads), 0)
    right = lax.broadcasted_iota(jnp.int32, (heads, heads), 1)
    behind = dot_full(jnp.where(right > down, 1.0, 0.0).astype(F32), whole)
    lane1 = lax.broadcasted_iota(jnp.int32, (1, 128), 1)
    sums = (sums0_ref[0:1, :] + sums1_ref[0:1, :]) + (sums2_ref[0:1, :] + sums3_ref[0:1, :])
    after = jnp.sum(
        jnp.where(jnp.logical_and(lane1 == block, block < 3), sums, 0.0), axis=1, keepdims=True
    )
    error_sq = jnp.sum(jnp.where(lane1 == 3, sums, 0.0), axis=1, keepdims=True)
    norm = jnp.sqrt(error_sq + 1e-06)
    factor = seq_len / norm
    rate = jnp.exp2(-0.5 * jnp.full((1, 1), level_ref[0], jnp.int32).astype(F32))
    step = (inside + behind + after) * (-(rate * factor))
    lane = lax.broadcasted_iota(jnp.int32, (heads, 128), 1)
    gb = gb * (factor * beta)
    gc = gc * (factor * beta)
    eb, ec, es, en = exponent_of(gb), exponent_of(gc), exponent_of(step), exponent_of(norm)
    out_ref[:, 0:n, :] = (gb * jnp.exp2(14.0 - eb)).reshape(heads, n, width)
    out_ref[:, n:2 * n, :] = (gc * jnp.exp2(14.0 - ec)).reshape(heads, n, width)
    high, low = split_scaled(step, es)
    norm_high, norm_low = split_scaled(norm, en)
    last = jnp.where(lane < n, high, low)
    for at, value in enumerate((eb, ec, es, norm_high, norm_low, en)):
        last = jnp.where(lane == 2 * n + at, value, last)
    out_ref[:, 2 * n:2 * n + 1, :] = last.reshape(heads, 1, 128)


def unpack_kernel(x_ref, gb_ref, gc_ref, step_ref, loss_ref):
    heads = x_ref.shape[0]
    n = gb_ref.shape[0]
    last = x_ref[:, 2 * n:2 * n + 1, :].reshape(heads, 128)
    lane = lax.broadcasted_iota(jnp.int32, (heads, 128), 1)

    def pick(at):
        return jnp.sum(jnp.where(lane == 2 * n + at, last, 0.0), axis=1, keepdims=True)

    scale_b, scale_c, scale_s = (jnp.exp2(pick(at) - 14.0) for at in range(3))
    norm = (pick(3) + pick(4)) * jnp.exp2(pick(5) - 14.0)
    gb_ref[...] = jnp.swapaxes(x_ref[:, 0:n, :] * scale_b[:, :, None], 0, 1)
    gc_ref[...] = jnp.swapaxes(x_ref[:, n:2 * n, :] * scale_c[:, :, None], 0, 1)
    step = jnp.transpose(last * scale_s)
    step_ref[...] = step[0:n, :] + step[n:2 * n, :]
    loss_ref[...] = jnp.sum(norm, axis=0, keepdims=True) * (1.0 / heads)


def call(kernel, out_shape, scratch, scalars, count):
    return pl.pallas_call(
        kernel,
        out_shape=out_shape,
        in_specs=[pl.BlockSpec(memory_space=pltpu.SMEM)] * scalars
        + [pl.BlockSpec(memory_space=pltpu.VMEM)] * (count - scalars),
        out_specs=jax.tree.map(lambda _: pl.BlockSpec(memory_space=pltpu.VMEM), out_shape),
        scratch_shapes=scratch,
        compiler_params=pltpu.CompilerParams(vmem_limit_bytes=VMEM_BYTES),
    )


def shape(*dims, dtype=F32):
    return jax.ShapeDtypeStruct(dims, dtype)


def near(*dims, dtype=F32):
    return pltpu.VMEM(dims, dtype)


def held_near(x):
    return pltpu.with_memory_space_constraint(x, pltpu.VMEM)


def per_device(queries, keys, b_proj, c_proj, step_size, rate_level):
    n, heads, width = queries.shape
    blocks = lax.axis_size("seq")
    block = lax.axis_index("seq")
    rows = n * heads
    seq_len = rows * blocks
    beta = 2.0 / math.sqrt(width * seq_len)
    scale = LOG2E / math.sqrt(width)

    def to_heads(x):
        return lax.all_to_all(x, "head", split_axis=0, concat_axis=0, tiled=True)

    def around(x):
        return [
            lax.ppermute(x, "seq", [(i, (i + d) % blocks) for i in range(blocks)])
            for d in range(1, blocks)
        ]

    def exchange(pair):
        mine, after = pair[:, 0:n], pair[:, n:2 * n]
        return [
            held_near(
                lax.ppermute(
                    jnp.where(block + d < blocks, mine, after),
                    "seq", [(i, (i + d) % blocks) for i in range(blocks)],
                )
            )
            for d in range(1, blocks)
        ]

    kq = to_heads(
        call(pack_kernel, near(heads, 2 * n + 1, width, dtype=BF16), [], 0, 3)(
            keys, queries, step_size
        )
    )
    bc = call(pack_kernel, near(heads, 2 * n, width, dtype=BF16), [], 0, 2)(b_proj, c_proj)
    bc, kq = lax.optimization_barrier((bc, kq))
    bc = to_heads(bc)
    kq_from, bc_from = exchange(kq), exchange(bc)
    kq, bc = held_near(kq), held_near(bc)
    where = jnp.reshape(block, (1,)).astype(jnp.int32)
    mat = pltpu.VMEM((rows, width), BF16)
    mats = pltpu.VMEM((blocks, rows, width), BF16)
    flat = pltpu.VMEM((width, rows), F32)
    state = pltpu.VMEM((rows, 128), F32)
    local, top, total = call(
        functools.partial(own_stats_kernel, n, scale),
        [near(8, rows), near(rows, 128), near(rows, 128)], [], 1, 2,
    )(rate_level, kq)
    local_from = [held_near(x) for x in around(local)]
    stats, vec = call(
        functools.partial(stats_kernel, n, scale), [near(8, rows), near(8, rows)],
        [mat, mats, state, state], 1, 11,
    )(where, kq, *kq_from, top, total, local, *local_from)
    stats_from = [held_near(x) for x in around(stats)]
    gc, gb, sums = call(
        functools.partial(rows_kernel, n, scale, beta),
        [near(rows, width), near(rows, width), near(8, 128)],
        [
            mat, mat, mats, mats, flat, pltpu.VMEM((rows, 8), F32),
            pltpu.VMEM((4, rows, 1), F32), pltpu.VMEM((8, 128), F32), pltpu.VMEM((1, 128), F32),
        ],
        1, 11,
    )(where, kq, bc, *kq_from, *bc_from, vec, stats)
    gb, sums = call(
        functools.partial(cols_kernel, n, scale, beta),
        [near(rows, width), near(8, 128)],
        [mat, mat, mats, mats, pltpu.VMEM((4, rows, 8), F32), flat],
        1, 15,
    )(where, kq, bc, *kq_from, *bc_from, vec, *stats_from, gb, sums)
    sums_from = [held_near(x) for x in around(sums)]
    packed = call(
        functools.partial(finish_kernel, n, beta, float(seq_len)),
        near(heads, 2 * n + 1, width), [], 2, 9,
    )(where, rate_level, bc, gc, gb, sums, *sums_from)
    back = to_heads(packed.astype(F16)).astype(F32)
    grad_b, grad_c, grad_step, loss = pl.pallas_call(
        unpack_kernel,
        out_shape=[
            shape(n, heads, width), shape(n, heads, width), shape(n, heads), shape(1, 1),
        ],
        compiler_params=pltpu.CompilerParams(vmem_limit_bytes=VMEM_BYTES),
    )(held_near(back))
    return grad_b, grad_c, grad_step, jnp.reshape(loss, ())


def solution(mesh):
    tokens = P(("seq", "head"), None, None)
    return jax.shard_map(
        per_device,
        mesh=mesh,
        in_specs=(tokens, tokens, tokens, tokens, P(("seq", "head"), None), P("head")),
        out_specs=(tokens, tokens, P(("seq", "head"), None), P()),
        check_vma=False,
    )
```

time: 165 us -> 132 us (0.80)
  blocking collectives: 91.5 us -> 32.7 us
  starting transfers between devices: 19.7 us -> 46.1 us
  waiting for transfers between devices: 12.3 us -> 31.2 us
  other arithmetic: 11.3 us -> 1.08 us
  local copies, waits for them, and re-layouts: 10.2 us -> 2.59 us
    psum x1 -> x0, blocking collectives: 30.2 us -> none  [per_device(): sums = lax.psum(small, 'seq')]
    all_to_all x2 -> x1, blocking collectives: 61.3 us -> 32.7 us  [to_heads(): return lax.all_to_all(x, 'head', split_axis=0, concat_axis=0, tiled=True)]
    all_to_all x1 -> x2, waiting for transfers between devices: 0.01 us -> 26.1 us  [to_heads(): return lax.all_to_all(x, 'head', split_axis=0, concat_axis=0, tiled=True)]
    ppermute x6 -> x15, starting transfers between devices: 12.9 us -> 26.7 us  [the longest x9 19.1 us: around(): lax.ppermute(x, 'seq', [(i, (i + d) % blocks) for i in range(blocks)])]
    all_to_all x1 -> x2, starting transfers between devices: 6.82 us -> 19.4 us  [to_heads(): return lax.all_to_all(x, 'head', split_axis=0, concat_axis=0, tiled=True)]
    ppermute x6 -> x15, waiting for transfers between devices: 12.3 us -> 5.13 us  [the longest x9 2.77 us: around(): lax.ppermute(x, 'seq', [(i, (i + d) % blocks) for i in range(blocks)])]
    convert_element_type x6 -> x0, other arithmetic: 4.79 us -> none  [the longest x3 2.53 us: per_device(): lax.ppermute(part.astype(F16), 'seq', [(i, i - d) for i in range(d, block...]
    ppermute x3 -> x0, local copies, waits for them, and re-layouts: 3.62 us -> none  [per_device(): lax.ppermute(kb, 'seq', [(i, i + d) for i in range(blocks - d)])]
  transfers between devices with their start and end apart: 7 -> 17, of which waited for: 2 -> 6; matrix products, arithmetic and copies ran while one was open for 7% -> 1% of each run, Pallas kernels for 3% -> 4%
where the time goes in v2:
time: 132 us
  starting transfers between devices  46.1 us (35%)
  blocking collectives  32.7 us (25%)
  waiting for transfers between devices  31.2 us (24%)
  Pallas kernels  16.4 us (12%)
  local copies, waits for them, and re-layouts  2.59 us (2%)
  between operations  1.41 us (1%)
    all_to_all x1, blocking collectives, to_heads(): return lax.all_to_all(x, 'head', split_axis=0, concat_axis=0, tiled=True)  32.7 us
    all_to_all x2, waiting for transfers between devices, to_heads(): return lax.all_to_all(x, 'head', split_axis=0, concat_axis=0, tiled=True)  26.1 us
    all_to_all x2, starting transfers between devices, to_heads(): return lax.all_to_all(x, 'head', split_axis=0, concat_axis=0, tiled=True)  19.4 us
    ppermute x9, starting transfers between devices, around(): lax.ppermute(x, 'seq', [(i, (i + d) % blocks) for i in range(blocks)])  19.1 us
    pallas_call x1, Pallas kernels, per_device(): call(functools.partial(cols_kernel, n, scale, beta), [near(rows, width),...  7.65 us
    ppermute x6, starting transfers between devices, exchange(): lax.ppermute(jnp.where(block + d < blocks, mine, after), 'seq', [(i, (i +...  7.61 us
    ppermute x9, waiting for transfers between devices, around(): lax.ppermute(x, 'seq', [(i, (i + d) % blocks) for i in range(blocks)])  2.77 us
    pallas_call x1, Pallas kernels, per_device(): call(functools.partial(rows_kernel, n, scale, beta), [near(rows, width),...  2.75 us
  transfers between devices with their start and end apart: 17, of which 6 were waited for; matrix products, arithmetic and copies ran while one was open for 1% of the time, Pallas kernels for 4%

profile of v2, /device:TPU:1, one launch (start us, length us, event | category | flops | bytes accessed | tf_op | source)
XLA Modules:
  0.0 131.6 jit_solution(16966489793476028708)
XLA Ops:
  3.2 1.1 shard_map.94
  4.3 13.2 %all-to-all-start = ((bf16[64,33,128]{2,1,0:T(8,128)(2,1)}), bf16[64,33,128]{2,1,0:T(8,128)(2,1)S(1)}, u32[]{:S(2)}, u32[]{:S(2)}) async-start(bf16[64,33,128]{2,1,0:T(8,128)(2,1)} %shard_map.94), calls=%async_computation | async-start | bytes 1310720 | tf_op jit(solution)/shard_map/all_to_all | solution.py:382
  18.4 19.2 %all-to-all-done.kq_ref = bf16[64,33,128]{2,1,0:T(8,128)(2,1)S(1)} async-done(((bf16[64,33,128]{2,1,0:T(8,128)(2,1)}), bf16[64,33,128]{2,1,0:T(8,128)(2,1)S(1)}, u32[]{:S(2)}, u32[]{:S(2)}) %all-to-all-start) | async-done | bytes 540704 | tf_op jit(solution)/shard_map/all_to_all | solution.py:382
  37.6 6.3 %all-to-all-start.1 = ((bf16[64,32,128]{2,1,0:T(8,128)(2,1)}), bf16[64,32,128]{2,1,0:T(8,128)(2,1)S(1)}, u32[]{:S(2)}, u32[]{:S(2)}) async-start(bf16[64,32,128]{2,1,0:T(8,128)(2,1)} %shard_map.93), calls=%async_computation.1 | async-start | bytes 1048576 | tf_op jit(solution)/shard_map/all_to_all | solution.py:382
  44.5 1.3 shard_map.95
  45.8 1.3 collective-permute-start.6
  47.1 2.5 %collective-permute-start.7 = (f32[8,1024]{1,0:T(8,128)S(1)}, f32[8,1024]{1,0:T(8,128)S(1)}, u32[]{:S(2)}, u32[]{:S(2)}) collective-permute-start(f32[8,1024]{1,0:T(8,128)S(1)} %get-tuple-element.24.local0_ref), channel_id=1, source_target_pairs={{0,128},{64,192},{128,0},{192,64},{1,129},{65,193},{129,1},{193,65... | collective-permute-start | bytes 98312 | tf_op jit(solution)/shard_map/ppermute | solution.py:386
  49.5 1.1 collective-permute-start.8
  52.7 1.5 %collective-permute-start.2 = (bf16[64,16,128]{2,1,0:T(8,128)(2,1)S(1)}, bf16[64,16,128]{2,1,0:T(8,128)(2,1)S(1)}, u32[]{:S(2)}, u32[]{:S(2)}) collective-permute-start(bf16[64,16,128]{2,1,0:T(8,128)(2,1)S(1)} %get-tuple-element.36), channel_id=1, source_target_pairs={{0,192},{64,0},{128,64},{192,128},{1,193},{65,1},{129,65},{193,129... | collective-permute-start | bytes 786440 | tf_op jit(solution)/shard_map/ppermute | solution.py:394
  54.3 6.9 %all-to-all-done.1.bc_ref = bf16[64,32,128]{2,1,0:T(8,128)(2,1)S(1)} async-done(((bf16[64,32,128]{2,1,0:T(8,128)(2,1)}), bf16[64,32,128]{2,1,0:T(8,128)(2,1)S(1)}, u32[]{:S(2)}, u32[]{:S(2)}) %all-to-all-start.1) | async-done | bytes 524320 | tf_op jit(solution)/shard_map/all_to_all | solution.py:382
  61.2 1.3 collective-permute-start.3
  62.5 2.5 %collective-permute-start.4 = (bf16[64,16,128]{2,1,0:T(8,128)(2,1)S(1)}, bf16[64,16,128]{2,1,0:T(8,128)(2,1)S(1)}, u32[]{:S(2)}, u32[]{:S(2)}) collective-permute-start(bf16[64,16,128]{2,1,0:T(8,128)(2,1)S(1)} %get-tuple-element.41), channel_id=1, source_target_pairs={{0,128},{64,192},{128,0},{192,64},{1,129},{65,193},{129,1},{193,65... | collective-permute-start | bytes 786440 | tf_op jit(solution)/shard_map/ppermute | solution.py:394
  65.0 1.2 collective-permute-start.5
  66.8 2.7 %collective-permute-start.9 = (f32[8,1024]{1,0:T(8,128)S(1)}, f32[8,1024]{1,0:T(8,128)S(1)}, u32[]{:S(2)}, u32[]{:S(2)}) collective-permute-start(f32[8,1024]{1,0:T(8,128)S(1)} %get-tuple-element.26.stats_ref), channel_id=1, source_target_pairs={{0,64},{64,128},{128,192},{192,0},{1,65},{65,129},{129,193},{193,1... | collective-permute-start | bytes 98312 | tf_op jit(solution)/shard_map/ppermute | solution.py:386
  69.4 5.4 %collective-permute-start.10 = (f32[8,1024]{1,0:T(8,128)S(1)}, f32[8,1024]{1,0:T(8,128)S(1)}, u32[]{:S(2)}, u32[]{:S(2)}) collective-permute-start(f32[8,1024]{1,0:T(8,128)S(1)} %get-tuple-element.26.stats_ref), channel_id=1, source_target_pairs={{0,128},{64,192},{128,0},{192,64},{1,129},{65,193},{129,1},{193,65... | collective-permute-start | bytes 98312 | tf_op jit(solution)/shard_map/ppermute | solution.py:386
  74.8 1.9 %collective-permute-done.4.b2_ref.c2_ref = bf16[64,16,128]{2,1,0:T(8,128)(2,1)S(1)} collective-permute-done((bf16[64,16,128]{2,1,0:T(8,128)(2,1)S(1)}, bf16[64,16,128]{2,1,0:T(8,128)(2,1)S(1)}, u32[]{:S(2)}, u32[]{:S(2)}) %collective-permute-start.4) | collective-permute-done | bytes 262176 | tf_op jit(solution)/shard_map/ppermute | solution.py:394
  77.2 2.7 %shard_map.97 = (f32[1024,128]{1,0:T(8,128)S(1)}, f32[1024,128]{1,0:T(8,128)S(1)}, f32[8,128]{1,0:T(8,128)S(1)}) custom-call(s32[1]{0:T(128)} %bitcast.block_ref, bf16[64,33,128]{2,1,0:T(8,128)(2,1)S(1)} %all-to-all-done.kq_ref, bf16[64,32,128]{2,1,0:T(8,128)(2,1)S(1)} %all-to-all-done.1.bc_ref, ...), custom_call_target="tpu_custom_call" | custom-call | tf_op jit(solution)/shard_map/pallas_call | solution.py:427
  79.9 7.7 %shard_map.98 = (f32[1024,128]{1,0:T(8,128)S(1)}, f32[8,128]{1,0:T(8,128)S(1)}) custom-call(s32[1]{0:T(128)} %bitcast.block_ref, bf16[64,33,128]{2,1,0:T(8,128)(2,1)S(1)} %all-to-all-done.kq_ref, bf16[64,32,128]{2,1,0:T(8,128)(2,1)S(1)} %all-to-all-done.1.bc_ref, bf16[64,16,128]{2,1,0:T(8,128)(2,1)S(1)} %collective-permute-done.in1_ref.k1_ref.q1_ref, ...), custom_call_target="tpu_custom_call" | custom-call | tf_op jit(solution)/shard_map/pallas_call | solution.py:436
  87.6 1.6 %collective-permute-start.12 = (f32[8,128]{1,0:T(8,128)S(1)}, f32[8,128]{1,0:T(8,128)S(1)}, u32[]{:S(2)}, u32[]{:S(2)}) collective-permute-start(f32[8,128]{1,0:T(8,128)S(1)} %get-tuple-element.31.sums0_ref), channel_id=1, source_target_pairs={{0,64},{64,128},{128,192},{192,0},{1,65},{65,129},{129,193},{193,1... | collective-permute-start | bytes 12296 | tf_op jit(solution)/shard_map/ppermute | solution.py:386
  89.2 4.6 %collective-permute-start.13 = (f32[8,128]{1,0:T(8,128)S(1)}, f32[8,128]{1,0:T(8,128)S(1)}, u32[]{:S(2)}, u32[]{:S(2)}) collective-permute-start(f32[8,128]{1,0:T(8,128)S(1)} %get-tuple-element.31.sums0_ref), channel_id=1, source_target_pairs={{0,128},{64,192},{128,0},{192,64},{1,129},{65,193},{129,1},{193,65... | collective-permute-start | bytes 12296 | tf_op jit(solution)/shard_map/ppermute | solution.py:386
  93.8 1.0 collective-permute-done.13.sums2_ref
  94.8 1.7 %collective-permute-done.14.sums3_ref = f32[8,128]{1,0:T(8,128)S(1)} collective-permute-done((f32[8,128]{1,0:T(8,128)S(1)}, f32[8,128]{1,0:T(8,128)S(1)}, u32[]{:S(2)}, u32[]{:S(2)}) %collective-permute-start.14) | collective-permute-done | bytes 4128 | tf_op jit(solution)/shard_map/ppermute | solution.py:386
  97.5 32.7 %all_to_all.15 = f16[64,33,128]{2,1,0:T(8,128)(2,1)S(1)} all-to-all(f16[64,33,128]{2,1,0:T(8,128)(2,1)S(1)} %convert_element_type.6), channel_id=1, replica_groups=mesh['seq'=4,'head'=64] {'head'}, dimensions={0} | all-to-all | bytes 1081344 | tf_op jit(solution)/shard_map/all_to_all | solution.py:382
  130.3 1.2 shard_map.100
  (33 shorter events, 7.7 us)
Async XLA Ops:
  0.6 1.0 copy-start
  1.6 0.9 copy-start.1
  2.5 0.7 copy-start.4
  3.2 14.2 %copy-start.2 = (bf16[16,64,128]{2,1,0:T(8,128)(2,1)S(1)}, bf16[16,64,128]{2,1,0:T(8,128)(2,1)}, u32[]{:S(2)}) copy-start(bf16[16,64,128]{2,1,0:T(8,128)(2,1)} %refs_0_.2) | copy-start | bytes 786436
  3.2 14.2 %copy-start.3 = (bf16[16,64,128]{2,1,0:T(8,128)(2,1)S(1)}, bf16[16,64,128]{2,1,0:T(8,128)(2,1)}, u32[]{:S(2)}) copy-start(bf16[16,64,128]{2,1,0:T(8,128)(2,1)} %refs_1_.2) | copy-start | bytes 786436
  4.3 33.3 %all-to-all-start = ((bf16[64,33,128]{2,1,0:T(8,128)(2,1)}), bf16[64,33,128]{2,1,0:T(8,128)(2,1)S(1)}, u32[]{:S(2)}, u32[]{:S(2)}) async-start(bf16[64,33,128]{2,1,0:T(8,128)(2,1)} %shard_map.94), calls=%async_computation | async-start | bytes 1310720 | tf_op jit(solution)/shard_map/all_to_all | solution.py:382
  37.6 23.6 %all-to-all-start.1 = ((bf16[64,32,128]{2,1,0:T(8,128)(2,1)}), bf16[64,32,128]{2,1,0:T(8,128)(2,1)S(1)}, u32[]{:S(2)}, u32[]{:S(2)}) async-start(bf16[64,32,128]{2,1,0:T(8,128)(2,1)} %shard_map.93), calls=%async_computation.1 | async-start | bytes 1048576 | tf_op jit(solution)/shard_map/all_to_all | solution.py:382
  45.8 6.9 %collective-permute-start.6 = (f32[8,1024]{1,0:T(8,128)S(1)}, f32[8,1024]{1,0:T(8,128)S(1)}, u32[]{:S(2)}, u32[]{:S(2)}) collective-permute-start(f32[8,1024]{1,0:T(8,128)S(1)} %get-tuple-element.24.local0_ref), channel_id=1, source_target_pairs={{0,64},{64,128},{128,192},{192,0},{1,65},{65,129},{129,193},{193,1... | collective-permute-start | bytes 98312 | tf_op jit(solution)/shard_map/ppermute | solution.py:386
  47.1 14.2 %collective-permute-start.7 = (f32[8,1024]{1,0:T(8,128)S(1)}, f32[8,1024]{1,0:T(8,128)S(1)}, u32[]{:S(2)}, u32[]{:S(2)}) collective-permute-start(f32[8,1024]{1,0:T(8,128)S(1)} %get-tuple-element.24.local0_ref), channel_id=1, source_target_pairs={{0,128},{64,192},{128,0},{192,64},{1,129},{65,193},{129,1},{193,65... | collective-permute-start | bytes 98312 | tf_op jit(solution)/shard_map/ppermute | solution.py:386
  49.5 13.0 %collective-permute-start.8 = (f32[8,1024]{1,0:T(8,128)S(1)}, f32[8,1024]{1,0:T(8,128)S(1)}, u32[]{:S(2)}, u32[]{:S(2)}) collective-permute-start(f32[8,1024]{1,0:T(8,128)S(1)} %get-tuple-element.24.local0_ref), channel_id=1, source_target_pairs={{0,192},{64,0},{128,64},{192,128},{1,193},{65,1},{129,65},{193,129... | collective-permute-start | bytes 98312 | tf_op jit(solution)/shard_map/ppermute | solution.py:386
  51.5 13.5 %collective-permute-start = (bf16[64,16,128]{2,1,0:T(8,128)(2,1)}, bf16[64,16,128]{2,1,0:T(8,128)(2,1)S(1)}, u32[]{:S(2)}, u32[]{:S(2)}) collective-permute-start(bf16[64,16,128]{2,1,0:T(8,128)(2,1)} %get-tuple-element.37), channel_id=1, source_target_pairs={{0,64},{64,128},{128,192},{192,0},{1,65},{65,129},{129,193},{193,1... | collective-permute-start | bytes 786440 | tf_op jit(solution)/shard_map/ppermute | solution.py:394
  51.9 14.3 %collective-permute-start.1 = (bf16[64,16,128]{2,1,0:T(8,128)(2,1)}, bf16[64,16,128]{2,1,0:T(8,128)(2,1)S(1)}, u32[]{:S(2)}, u32[]{:S(2)}) collective-permute-start(bf16[64,16,128]{2,1,0:T(8,128)(2,1)} %get-tuple-element.38), channel_id=1, source_target_pairs={{0,128},{64,192},{128,0},{192,64},{1,129},{65,193},{129,1},{193,65... | collective-permute-start | bytes 786440 | tf_op jit(solution)/shard_map/ppermute | solution.py:394
  52.7 13.4 %collective-permute-start.2 = (bf16[64,16,128]{2,1,0:T(8,128)(2,1)S(1)}, bf16[64,16,128]{2,1,0:T(8,128)(2,1)S(1)}, u32[]{:S(2)}, u32[]{:S(2)}) collective-permute-start(bf16[64,16,128]{2,1,0:T(8,128)(2,1)S(1)} %get-tuple-element.36), channel_id=1, source_target_pairs={{0,192},{64,0},{128,64},{192,128},{1,193},{65,1},{129,65},{193,129... | collective-permute-start | bytes 786440 | tf_op jit(solution)/shard_map/ppermute | solution.py:394
  61.2 13.6 %collective-permute-start.3 = (bf16[64,16,128]{2,1,0:T(8,128)(2,1)S(1)}, bf16[64,16,128]{2,1,0:T(8,128)(2,1)S(1)}, u32[]{:S(2)}, u32[]{:S(2)}) collective-permute-start(bf16[64,16,128]{2,1,0:T(8,128)(2,1)S(1)} %get-tuple-element.40), channel_id=1, source_target_pairs={{0,64},{64,128},{128,192},{192,0},{1,65},{65,129},{129,193},{193,1... | collective-permute-start | bytes 786440 | tf_op jit(solution)/shard_map/ppermute | solution.py:394
  62.5 14.2 %collective-permute-start.4 = (bf16[64,16,128]{2,1,0:T(8,128)(2,1)S(1)}, bf16[64,16,128]{2,1,0:T(8,128)(2,1)S(1)}, u32[]{:S(2)}, u32[]{:S(2)}) collective-permute-start(bf16[64,16,128]{2,1,0:T(8,128)(2,1)S(1)} %get-tuple-element.41), channel_id=1, source_target_pairs={{0,128},{64,192},{128,0},{192,64},{1,129},{65,193},{129,1},{193,65... | collective-permute-start | bytes 786440 | tf_op jit(solution)/shard_map/ppermute | solution.py:394
  65.0 12.2 %collective-permute-start.5 = (bf16[64,16,128]{2,1,0:T(8,128)(2,1)S(1)}, bf16[64,16,128]{2,1,0:T(8,128)(2,1)S(1)}, u32[]{:S(2)}, u32[]{:S(2)}) collective-permute-start(bf16[64,16,128]{2,1,0:T(8,128)(2,1)S(1)} %get-tuple-element.39), channel_id=1, source_target_pairs={{0,192},{64,0},{128,64},{192,128},{1,193},{65,1},{129,65},{193,129... | collective-permute-start | bytes 786440 | tf_op jit(solution)/shard_map/ppermute | solution.py:394
  66.8 13.1 %collective-permute-start.9 = (f32[8,1024]{1,0:T(8,128)S(1)}, f32[8,1024]{1,0:T(8,128)S(1)}, u32[]{:S(2)}, u32[]{:S(2)}) collective-permute-start(f32[8,1024]{1,0:T(8,128)S(1)} %get-tuple-element.26.stats_ref), channel_id=1, source_target_pairs={{0,64},{64,128},{128,192},{192,0},{1,65},{65,129},{129,193},{193,1... | collective-permute-start | bytes 98312 | tf_op jit(solution)/shard_map/ppermute | solution.py:386
  69.4 10.5 %collective-permute-start.10 = (f32[8,1024]{1,0:T(8,128)S(1)}, f32[8,1024]{1,0:T(8,128)S(1)}, u32[]{:S(2)}, u32[]{:S(2)}) collective-permute-start(f32[8,1024]{1,0:T(8,128)S(1)} %get-tuple-element.26.stats_ref), channel_id=1, source_target_pairs={{0,128},{64,192},{128,0},{192,64},{1,129},{65,193},{129,1},{193,65... | collective-permute-start | bytes 98312 | tf_op jit(solution)/shard_map/ppermute | solution.py:386
  74.8 5.1 %collective-permute-start.11 = (f32[8,1024]{1,0:T(8,128)S(1)}, f32[8,1024]{1,0:T(8,128)S(1)}, u32[]{:S(2)}, u32[]{:S(2)}) collective-permute-start(f32[8,1024]{1,0:T(8,128)S(1)} %get-tuple-element.26.stats_ref), channel_id=1, source_target_pairs={{0,192},{64,0},{128,64},{192,128},{1,193},{65,1},{129,65},{193,129... | collective-permute-start | bytes 98312 | tf_op jit(solution)/shard_map/ppermute | solution.py:386
  87.6 6.2 %collective-permute-start.12 = (f32[8,128]{1,0:T(8,128)S(1)}, f32[8,128]{1,0:T(8,128)S(1)}, u32[]{:S(2)}, u32[]{:S(2)}) collective-permute-start(f32[8,128]{1,0:T(8,128)S(1)} %get-tuple-element.31.sums0_ref), channel_id=1, source_target_pairs={{0,64},{64,128},{128,192},{192,0},{1,65},{65,129},{129,193},{193,1... | collective-permute-start | bytes 12296 | tf_op jit(solution)/shard_map/ppermute | solution.py:386
  89.2 5.6 %collective-permute-start.13 = (f32[8,128]{1,0:T(8,128)S(1)}, f32[8,128]{1,0:T(8,128)S(1)}, u32[]{:S(2)}, u32[]{:S(2)}) collective-permute-start(f32[8,128]{1,0:T(8,128)S(1)} %get-tuple-element.31.sums0_ref), channel_id=1, source_target_pairs={{0,128},{64,192},{128,0},{192,64},{1,129},{65,193},{129,1},{193,65... | collective-permute-start | bytes 12296 | tf_op jit(solution)/shard_map/ppermute | solution.py:386
  93.8 2.8 %collective-permute-start.14 = (f32[8,128]{1,0:T(8,128)S(1)}, f32[8,128]{1,0:T(8,128)S(1)}, u32[]{:S(2)}, u32[]{:S(2)}) collective-permute-start(f32[8,128]{1,0:T(8,128)S(1)} %get-tuple-element.31.sums0_ref), channel_id=1, source_target_pairs={{0,192},{64,0},{128,64},{192,128},{1,193},{65,1},{129,65},{193,129... | collective-permute-start | bytes 12296 | tf_op jit(solution)/shard_map/ppermute | solution.py:386

commit v3 on v2

--- a/solution.py
+++ b/solution.py
@@ -101,20 +101,19 @@
 
 
 def pack_kernel(*refs):
-    x_ref, y_ref, out_ref = refs[0], refs[1], refs[-1]
-    n, heads, _ = x_ref.shape
-    out_ref[:, 0:n, :] = jnp.swapaxes(x_ref[...], 0, 1)
-    out_ref[:, n:2 * n, :] = jnp.swapaxes(y_ref[...], 0, 1)
-    if len(refs) == 4:
-        steps = refs[2][...].astype(F32)
-        steps = jnp.concatenate([steps, jnp.zeros((128 - n, heads), F32)], axis=0)
-        out_ref[:, 2 * n:2 * n + 1, :] = jnp.transpose(steps).reshape(heads, 1, 128).astype(BF16)
-
-
-def own_stats_kernel(n, scale, level_ref, kq_ref, local_ref, max_ref, sum_ref):
+    parts, steps_ref, out_ref = refs[:-2], refs[-2], refs[-1]
+    n, heads, _ = parts[0].shape
+    for at, ref in enumerate(parts):
+        out_ref[:, at * n:(at + 1) * n, :] = jnp.swapaxes(ref[...], 0, 1)
+    steps = jnp.concatenate([steps_ref[...].astype(F32), jnp.zeros((128 - n, heads), F32)], axis=0)
+    last = len(parts) * n
+    out_ref[:, last:last + 1, :] = jnp.transpose(steps).reshape(heads, 1, 128).astype(BF16)
+
+
+def own_stats_kernel(n, scale, level_ref, own_ref, local_ref, max_ref, sum_ref):
     rows = max_ref.shape[0]
-    heads = kq_ref.shape[0]
-    k, q = take(kq_ref, 0, n), take(kq_ref, 1, n)
+    heads = own_ref.shape[0]
+    k, q = take(own_ref, 0, n), take(own_ref, 1, n)
     for at in range(0, rows, TILE):
         ti = slice(at, at + TILE)
         s = dot_nt(q[ti, :], k[0:at + TILE, :])
@@ -123,24 +122,37 @@
         add_stats(jnp.where(col <= row, s, LOWEST), scale, max_ref, sum_ref, ti, True)
 
     level = jnp.full((1, 1), level_ref[0], jnp.int32).astype(F32)
-    steps = kq_ref[:, 2 * n:2 * n + 1, :].astype(F32).reshape(heads, 128)
+    steps = own_ref[:, 4 * n:4 * n + 1, :].astype(F32).reshape(heads, 128)
     local = sums_rows(-jnp.exp2(-0.5 * level) * steps, rows, n)
     local_ref[...] = jnp.broadcast_to(local, local_ref.shape)
 
 
 def stats_kernel(
-    n, scale, block_ref, kq_ref, in1_ref, in2_ref, in3_ref, max_ref, sum_ref,
-    local0_ref, local1_ref, local2_ref, local3_ref, out_ref, vec_ref, q_s, k_s, max_s, sum_s,
+    n, scale, block_ref, own_ref, in1_ref, in2_ref, in3_ref, local_ref, max_ref, sum_ref,
+    out_ref, q_s, k_s, max_s, sum_s,
 ):
     block = block_ref[0]
-    q_s[...] = take(kq_ref, 1, n)
+    rows = q_s.shape[0]
+    q_s[...] = take(own_ref, 1, n)
     max_s[...] = max_ref[...]
     sum_s[...] = sum_ref[...]
     for d, in_ref in enumerate((in1_ref, in2_ref, in3_ref)):
         k_s[d + 1, :, :] = take(in_ref, 0, n)
 
-    rows = q_s.shape[0]
-    local = [x[0:1, :] for x in (local0_ref, local1_ref, local2_ref, local3_ref)]
+    @pl.loop(1, block + 1)
+    def _(d):
+        add_stats(dot_nt(q_s[...], k_s[d]), scale, max_s, sum_s, slice(None), False)
+
+    top = jnp.max(max_s[...], axis=1, keepdims=True)
+    total = jnp.sum(sum_s[...] * jnp.exp2((max_s[...] - top) * scale), axis=1, keepdims=True)
+    lane = lax.broadcasted_iota(jnp.int32, (rows, 8), 1)
+    out_ref[...] = jnp.transpose(jnp.where(lane == 0, top, 1.0 / total))
+    out_ref[2:3, :] = local_ref[0:1, :]
+
+
+def fill_vec(block, stats_refs, vec_ref):
+    local = [x[2:3, :] for x in stats_refs]
+    rows = vec_ref.shape[1]
     ends = [x[:, rows - 1:rows] for x in local]
     vec_ref[0:1, :] = local[0]
     vec_ref[7:8, :] = jnp.zeros((1, rows), F32)
@@ -156,51 +168,26 @@
         vec_ref[d:d + 1, :] = jnp.exp2(v * LOG2E)
         vec_ref[3 + d:4 + d, :] = jnp.exp2(u * LOG2E)
 
-    @pl.loop(1, block + 1)
-    def _(d):
-        add_stats(dot_nt(q_s[...], k_s[d]), scale, max_s, sum_s, slice(None), False)
-
-    top = jnp.max(max_s[...], axis=1, keepdims=True)
-    total = jnp.sum(sum_s[...] * jnp.exp2((max_s[...] - top) * scale), axis=1, keepdims=True)
-    lane = lax.broadcasted_iota(jnp.int32, (rows, 8), 1)
-    out_ref[...] = jnp.transpose(jnp.where(lane == 0, top, 1.0 / total))
-
-
-def rows_kernel(
-    n, scale, beta, block_ref, kq_ref, bc_ref, k1_ref, k2_ref, k3_ref, b1_ref, b2_ref, b3_ref,
-    vec_ref, stats_ref, gc_ref, gb_ref, out_ref, q_s, c_s, k_s, b_s, gbt_s, cols_s, u_s, sq_s, cross_s,
+
+def own_kernel(
+    n, scale, beta, own_ref, stats_ref, gc_ref, gb_ref, sq_ref, gbt_s, cols_s,
 ):
-    block = block_ref[0]
-    rows, width = q_s.shape
-    k_s[0, :, :] = take(kq_ref, 0, n)
-    b_s[0, :, :] = take(bc_ref, 0, n)
-    q_s[...] = take(kq_ref, 1, n)
-    c_s[...] = take(bc_ref, 1, n)
-    ct = jnp.transpose(c_s[...].astype(F32)).astype(BF16)
-    for d, (k_ref, b_ref) in enumerate(((k1_ref, b1_ref), (k2_ref, b2_ref), (k3_ref, b3_ref))):
-        k_s[d + 1, :, :] = take(k_ref, 0, n)
-        b_s[d + 1, :, :] = take(b_ref, 0, n)
-    place = lax.broadcasted_iota(jnp.int32, (8, rows), 0)
-    vec = vec_ref[...]
-    cols_s[...] = jnp.transpose(
-        jnp.where(place == 1, stats_ref[0:1, :], jnp.where(place == 2, stats_ref[1:2, :], vec))
-    )
-    spread = jnp.transpose(vec)
-    for d in range(1, 4):
-        u_s[d, :, :] = spread[:, 3 + d:4 + d]
-
+    rows = gc_ref.shape[0]
+    k_all, q_all, b_all, c_all = (take(own_ref, at, n) for at in range(4))
+    ct = jnp.transpose(c_all.astype(F32)).astype(BF16)
+    cols_s[...] = jnp.transpose(stats_ref[...])
     sq = jnp.zeros((8, 128), F32)
     gbt_s[...] = jnp.zeros(gbt_s.shape, F32)
     for i in range(0, rows, OWN):
         ti = slice(i, i + OWN)
-        q, c = q_s[ti, :], c_s[ti, :]
-        top_i, rinv_i, sum_i = cols_s[ti, 1:2], cols_s[ti, 2:3], cols_s[ti, 0:1]
+        q, c = q_all[ti, :], c_all[ti, :]
+        top_i, rinv_i, sum_i = cols_s[ti, 0:1], cols_s[ti, 1:2], cols_s[ti, 2:3]
         gc = 0.0
         for j in range(0, i + OWN, OWN):
             tj = slice(j, j + OWN)
-            k, b = k_s[0, tj, :], b_s[0, tj, :]
+            k, b = k_all[tj, :], b_all[tj, :]
             s = dot_nt(q, k) - top_i
-            gap = sum_i - vec_ref[0:1, tj]
+            gap = sum_i - stats_ref[2:3, tj]
             if i == j:
                 row = lax.broadcasted_iota(jnp.int32, s.shape, 0)
                 col = lax.broadcasted_iota(jnp.int32, s.shape, 1)
@@ -215,14 +202,35 @@
             gbt_s[:, tj] += dot_nn(ct[:, ti], held)
         gc_ref[ti, :] = gc
     gb_ref[...] = jnp.transpose(gbt_s[...])
-    sq_s[...] = sq
+    sq_ref[...] = sq
+
+
+def rows_kernel(
+    n, scale, beta, block_ref, own_ref, k1_ref, k2_ref, k3_ref, b1_ref, b2_ref, b3_ref,
+    stats_ref, st1_ref, st2_ref, st3_ref, gc_in_ref, sq_in_ref, gc_ref, out_ref, vec_ref,
+    q_s, c_s, k_s, b_s, cols_s, u_s, sq_s, cross_s,
+):
+    block = block_ref[0]
+    rows, width = q_s.shape
+    fill_vec(block, (stats_ref, st1_ref, st2_ref, st3_ref), vec_ref)
+    q_s[...] = take(own_ref, 1, n)
+    c_s[...] = take(own_ref, 3, n)
+    for d, (k_ref, b_ref) in enumerate(((k1_ref, b1_ref), (k2_ref, b2_ref), (k3_ref, b3_ref))):
+        k_s[d + 1, :, :] = take(k_ref, 0, n)
+        b_s[d + 1, :, :] = take(b_ref, 0, n)
+    cols_s[...] = jnp.transpose(stats_ref[...])
+    spread = jnp.transpose(vec_ref[...])
+    for d in range(1, 4):
+        u_s[d, :, :] = spread[:, 3 + d:4 + d]
+    gc_ref[...] = gc_in_ref[...]
+    sq_s[...] = sq_in_ref[...]
     cross_s[...] = jnp.zeros(cross_s.shape, F32)
     lane = lax.broadcasted_iota(jnp.int32, (1, 128), 1)
 
     @pl.loop(1, block + 1)
     def _(d):
         q, c = q_s[...], c_s[...]
-        top_i, rinv_i, u_i = cols_s[:, 1:2], cols_s[:, 2:3], u_s[d]
+        top_i, rinv_i, u_i = cols_s[:, 0:1], cols_s[:, 1:2], u_s[d]
         gc = 0.0
         sq = sq_s[...]
         for j in range(0, rows, WIDE):
@@ -243,15 +251,15 @@
 
 
 def cols_kernel(
-    n, scale, beta, block_ref, kq_ref, bc_ref, q1_ref, q2_ref, q3_ref, c1_ref, c2_ref, c3_ref,
+    n, scale, beta, block_ref, own_ref, q1_ref, q2_ref, q3_ref, c1_ref, c2_ref, c3_ref,
     vec_ref, st1_ref, st2_ref, st3_ref, gb_in_ref, sums_in_ref, gb_ref, sums_ref,
     k_s, b_s, q_s, c_s, cols_s, gbt_s,
 ):
     block = block_ref[0]
     rows, width = k_s.shape
     sums_ref[...] = sums_in_ref[...]
-    k_s[...] = take(kq_ref, 0, n)
-    b_s[...] = take(bc_ref, 0, n)
+    k_s[...] = take(own_ref, 0, n)
+    b_s[...] = take(own_ref, 2, n)
     place = lax.broadcasted_iota(jnp.int32, (8, rows), 0)
     incoming = ((q1_ref, c1_ref, st1_ref), (q2_ref, c2_ref, st2_ref), (q3_ref, c3_ref, st3_ref))
     for d, (q_ref, c_ref, st_ref) in enumerate(incoming):
@@ -280,16 +288,16 @@
 
 
 def finish_kernel(
-    n, beta, seq_len, block_ref, level_ref, bc_ref, gc_ref, gb_ref,
+    n, beta, seq_len, block_ref, level_ref, own_ref, gc_ref, gb_ref,
     sums0_ref, sums1_ref, sums2_ref, sums3_ref, out_ref,
 ):
     block = block_ref[0]
-    heads, _, width = bc_ref.shape
+    heads, _, width = own_ref.shape
     rows = heads * n
     gb = gb_ref[...]
     gc = gc_ref[...]
-    c = take(bc_ref, 1, n).astype(F32)
-    b = take(bc_ref, 0, n).astype(F32)
+    c = take(own_ref, 3, n).astype(F32)
+    b = take(own_ref, 2, n).astype(F32)
     slope = jnp.sum(c * gc - b * gb, axis=1, keepdims=True) * beta
     slope = jnp.broadcast_to(slope, (rows, 128)).reshape(heads, n, 128)
     place = lax.broadcasted_iota(jnp.int32, (heads, n, 128), 1)
@@ -399,16 +407,15 @@
             for d in range(1, blocks)
         ]
 
-    kq = to_heads(
-        call(pack_kernel, near(heads, 2 * n + 1, width, dtype=BF16), [], 0, 3)(
-            keys, queries, step_size
-        )
+    inputs = [
+        pltpu.with_memory_space_constraint(x, pltpu.HBM)
+        for x in (keys, queries, b_proj, c_proj, step_size)
+    ]
+    arrived = to_heads(
+        call(pack_kernel, near(heads, 4 * n + 1, width, dtype=BF16), [], 0, 5)(*inputs)
     )
-    bc = call(pack_kernel, near(heads, 2 * n, width, dtype=BF16), [], 0, 2)(b_proj, c_proj)
-    bc, kq = lax.optimization_barrier((bc, kq))
-    bc = to_heads(bc)
-    kq_from, bc_from = exchange(kq), exchange(bc)
-    kq, bc = held_near(kq), held_near(bc)
+    kq_from = exchange(arrived[:, 0:2 * n])
+    own = held_near(arrived)
     where = jnp.reshape(block, (1,)).astype(jnp.int32)
     mat = pltpu.VMEM((rows, width), BF16)
     mats = pltpu.VMEM((blocks, rows, width), BF16)
@@ -417,33 +424,38 @@
     local, top, total = call(
         functools.partial(own_stats_kernel, n, scale),
         [near(8, rows), near(rows, 128), near(rows, 128)], [], 1, 2,
-    )(rate_level, kq)
-    local_from = [held_near(x) for x in around(local)]
-    stats, vec = call(
-        functools.partial(stats_kernel, n, scale), [near(8, rows), near(8, rows)],
-        [mat, mats, state, state], 1, 11,
-    )(where, kq, *kq_from, top, total, local, *local_from)
+    )(rate_level, own)
+    bc, local = lax.optimization_barrier((arrived[:, 2 * n:4 * n], local))
+    bc_from = exchange(bc)
+    stats = call(
+        functools.partial(stats_kernel, n, scale), near(8, rows), [mat, mats, state, state], 1, 8,
+    )(where, own, *kq_from, local, top, total)
     stats_from = [held_near(x) for x in around(stats)]
-    gc, gb, sums = call(
+    gc, gb, sq = call(
+        functools.partial(own_kernel, n, scale, beta),
+        [near(rows, width), near(rows, width), near(8, 128)],
+        [flat, pltpu.VMEM((rows, 8), F32)], 0, 2,
+    )(own, stats)
+    gc, sums, vec = call(
         functools.partial(rows_kernel, n, scale, beta),
-        [near(rows, width), near(rows, width), near(8, 128)],
+        [near(rows, width), near(8, 128), near(8, rows)],
         [
-            mat, mat, mats, mats, flat, pltpu.VMEM((rows, 8), F32),
+            mat, mat, mats, mats, pltpu.VMEM((rows, 8), F32),
             pltpu.VMEM((4, rows, 1), F32), pltpu.VMEM((8, 128), F32), pltpu.VMEM((1, 128), F32),
         ],
-        1, 11,
-    )(where, kq, bc, *kq_from, *bc_from, vec, stats)
+        1, 14,
+    )(where, own, *kq_from, *bc_from, stats, *stats_from, gc, sq)
     gb, sums = call(
         functools.partial(cols_kernel, n, scale, beta),
         [near(rows, width), near(8, 128)],
         [mat, mat, mats, mats, pltpu.VMEM((4, rows, 8), F32), flat],
-        1, 15,
-    )(where, kq, bc, *kq_from, *bc_from, vec, *stats_from, gb, sums)
+        1, 14,
+    )(where, own, *kq_from, *bc_from, vec, *stats_from, gb, sums)
     sums_from = [held_near(x) for x in around(sums)]
     packed = call(
         functools.partial(finish_kernel, n, beta, float(seq_len)),
         near(heads, 2 * n + 1, width), [], 2, 9,
-    )(where, rate_level, bc, gc, gb, sums, *sums_from)
+    )(where, rate_level, own, gc, gb, sums, *sums_from)
     back = to_heads(packed.astype(F16)).astype(F32)
     grad_b, grad_c, grad_step, loss = pl.pallas_call(
         unpack_kernel,

time: 132 us -> 126 us (0.955)
  waiting for transfers between devices: 31.2 us -> 49.4 us
  starting transfers between devices: 46.1 us -> 28 us
  blocking collectives: 32.7 us -> 28.9 us
  local copies, waits for them, and re-layouts: 2.59 us -> 0.03 us
  Pallas kernels: 16.4 us -> 17.8 us
    ppermute x6, waiting for transfers between devices: 2.35 us -> 14.1 us  [exchange(): lax.ppermute(jnp.where(block + d < blocks, mine, after), 'seq', [(i, (i +...]
    ppermute x9 -> x6, starting transfers between devices: 19.1 us -> 8.84 us  [around(): lax.ppermute(x, 'seq', [(i, (i + d) % blocks) for i in range(blocks)])]
    all_to_all x2 -> x1, starting transfers between devices: 19.4 us -> 13.2 us  [to_heads(): return lax.all_to_all(x, 'head', split_axis=0, concat_axis=0, tiled=True)]
    all_to_all x2 -> x1, waiting for transfers between devices: 26.1 us -> 30.7 us  [to_heads(): return lax.all_to_all(x, 'head', split_axis=0, concat_axis=0, tiled=True)]
    all_to_all x1, blocking collectives: 32.7 us -> 28.9 us  [to_heads(): return lax.all_to_all(x, 'head', split_axis=0, concat_axis=0, tiled=True)]
    pallas_call x3, Pallas kernels: 2.65 us -> 5.62 us  [the longest x1 2.64 us: per_device(): call(pack_kernel, near(heads, 4 * n + 1, width, dtype=BF16), [], 0, 5)]
    unnamed x10 -> x0, local copies, waits for them, and re-layouts: 2.59 us -> none
    ppermute x9 -> x6, waiting for transfers between devices: 2.77 us -> 4.52 us  [around(): lax.ppermute(x, 'seq', [(i, (i + d) % blocks) for i in range(blocks)])]
  transfers between devices with their start and end apart: 17 -> 13, of which waited for: 6 -> 8; matrix products, arithmetic and copies ran while one was open for 1% -> 0% of each run, Pallas kernels for 4% -> 3%
where the time goes in v3:
time: 126 us
  waiting for transfers between devices  49.4 us (39%)
  blocking collectives  28.9 us (23%)
  starting transfers between devices  28 us (22%)
  Pallas kernels  17.8 us (14%)
  between operations  1.38 us (1%)
    all_to_all x1, waiting for transfers between devices, to_heads(): return lax.all_to_all(x, 'head', split_axis=0, concat_axis=0, tiled=True)  30.7 us
    all_to_all x1, blocking collectives, to_heads(): return lax.all_to_all(x, 'head', split_axis=0, concat_axis=0, tiled=True)  28.9 us
    ppermute x6, waiting for transfers between devices, exchange(): lax.ppermute(jnp.where(block + d < blocks, mine, after), 'seq', [(i, (i +...  14.1 us
    all_to_all x1, starting transfers between devices, to_heads(): return lax.all_to_all(x, 'head', split_axis=0, concat_axis=0, tiled=True)  13.2 us
    ppermute x6, starting transfers between devices, around(): lax.ppermute(x, 'seq', [(i, (i + d) % blocks) for i in range(blocks)])  8.84 us
    pallas_call x1, Pallas kernels, per_device(): call(functools.partial(cols_kernel, n, scale, beta), [near(rows, width),...  7.69 us
    ppermute x6, starting transfers between devices, exchange(): lax.ppermute(jnp.where(block + d < blocks, mine, after), 'seq', [(i, (i +...  5.98 us
    ppermute x6, waiting for transfers between devices, around(): lax.ppermute(x, 'seq', [(i, (i + d) % blocks) for i in range(blocks)])  4.52 us
  transfers between devices with their start and end apart: 13, of which 8 were waited for; matrix products, arithmetic and copies ran while one was open for 0% of the time, Pallas kernels for 3%

profile of v3, /device:TPU:1, one launch (start us, length us, event | category | flops | bytes accessed | tf_op | source)
XLA Modules:
  0.0 125.7 jit_solution(8738458914496866503)
XLA Ops:
  0.6 2.6 %shard_map.93 = bf16[64,65,128]{2,1,0:T(8,128)(2,1)} custom-call(bf16[16,64,128]{2,1,0:T(8,128)(2,1)} %refs_0_.1, bf16[16,64,128]{2,1,0:T(8,128)(2,1)} %refs_1_.1, bf16[16,64,128]{2,1,0:T(8,128)(2,1)} %refs_2_.1, bf16[16,64,128]{2,1,0:T(8,128)(2,1)} %refs_3_.1, bf16[16,64]{1,0:T(8,128)(2,1)} %refs_4_.1), custom_call_target="tpu_custom_call" | custom-call | tf_op jit(solution)/shard_map/pallas_call | solution.py:415
  3.3 13.2 %all-to-all-start = ((bf16[64,65,128]{2,1,0:T(8,128)(2,1)}), bf16[64,65,128]{2,1,0:T(8,128)(2,1)S(1)}, u32[]{:S(2)}, u32[]{:S(2)}) async-start(bf16[64,65,128]{2,1,0:T(8,128)(2,1)} %shard_map.93), calls=%async_computation | async-start | bytes 2359296 | tf_op jit(solution)/shard_map/all_to_all | solution.py:390
  17.1 30.7 %all-to-all-done.own_ref = bf16[64,65,128]{2,1,0:T(8,128)(2,1)S(1)} async-done(((bf16[64,65,128]{2,1,0:T(8,128)(2,1)}), bf16[64,65,128]{2,1,0:T(8,128)(2,1)S(1)}, u32[]{:S(2)}, u32[]{:S(2)}) %all-to-all-start) | async-done | bytes 1064992 | tf_op jit(solution)/shard_map/all_to_all | solution.py:390
  47.9 2.6 %collective-permute-start.2 = (bf16[64,16,128]{2,1,0:T(8,128)(2,1)S(1)}, bf16[64,16,128]{2,1,0:T(8,128)(2,1)S(1)}, u32[]{:S(2)}, u32[]{:S(2)}) collective-permute-start(bf16[64,16,128]{2,1,0:T(8,128)(2,1)S(1)} %get-tuple-element.38), channel_id=1, source_target_pairs={{0,192},{64,0},{128,64},{192,128},{1,193},{65,1},{129,65},{193,129... | collective-permute-start | bytes 786440 | tf_op jit(solution)/shard_map/ppermute | solution.py:402
  50.4 1.7 %collective-permute-start.1 = (bf16[64,16,128]{2,1,0:T(8,128)(2,1)S(1)}, bf16[64,16,128]{2,1,0:T(8,128)(2,1)S(1)}, u32[]{:S(2)}, u32[]{:S(2)}) collective-permute-start(bf16[64,16,128]{2,1,0:T(8,128)(2,1)S(1)} %get-tuple-element.40), channel_id=1, source_target_pairs={{0,128},{64,192},{128,0},{192,64},{1,129},{65,193},{129,1},{193,65... | collective-permute-start | bytes 786440 | tf_op jit(solution)/shard_map/ppermute | solution.py:402
  52.2 1.3 %shard_map.94 = (f32[8,1024]{1,0:T(8,128)S(1)}, f32[1024,128]{1,0:T(8,128)S(1)}, f32[1024,128]{1,0:T(8,128)S(1)}) custom-call(s32[1]{0:T(128)S(6)} %copy.10.level_ref, bf16[64,65,128]{2,1,0:T(8,128)(2,1)S(1)} %all-to-all-done.own_ref), custom_call_target="tpu_custom_call" | custom-call | tf_op jit(solution)/shard_map/pallas_call | solution.py:424
  53.5 1.0 collective-permute-start.5
  54.6 0.7 collective-permute-start.3
  55.2 6.4 %collective-permute-done.2.in3_ref.k3_ref.q3_ref = bf16[64,16,128]{2,1,0:T(8,128)(2,1)S(1)} collective-permute-done((bf16[64,16,128]{2,1,0:T(8,128)(2,1)S(1)}, bf16[64,16,128]{2,1,0:T(8,128)(2,1)S(1)}, u32[]{:S(2)}, u32[]{:S(2)}) %collective-permute-start.2) | collective-permute-done | bytes 262176 | tf_op jit(solution)/shard_map/ppermute | solution.py:402
  61.6 2.7 %collective-permute-done.in1_ref.k1_ref.q1_ref = bf16[64,16,128]{2,1,0:T(8,128)(2,1)S(1)} collective-permute-done((bf16[64,16,128]{2,1,0:T(8,128)(2,1)S(1)}, bf16[64,16,128]{2,1,0:T(8,128)(2,1)S(1)}, u32[]{:S(2)}, u32[]{:S(2)}) %collective-permute-start) | collective-permute-done | bytes 262176 | tf_op jit(solution)/shard_map/ppermute | solution.py:402
  64.3 0.6 shard_map.95.stats_ref
  64.9 4.4 %collective-permute-start.8 = (f32[8,1024]{1,0:T(8,128)S(1)}, f32[8,1024]{1,0:T(8,128)S(1)}, u32[]{:S(2)}, u32[]{:S(2)}) collective-permute-start(f32[8,1024]{1,0:T(8,128)S(1)} %shard_map.95.stats_ref), channel_id=1, source_target_pairs={{0,192},{64,0},{128,64},{192,128},{1,193},{65,1},{129,65},{193,129... | collective-permute-start | bytes 98312 | tf_op jit(solution)/shard_map/ppermute | solution.py:394
  69.4 3.8 %collective-permute-done.5.b3_ref.c3_ref = bf16[64,16,128]{2,1,0:T(8,128)(2,1)S(1)} collective-permute-done((bf16[64,16,128]{2,1,0:T(8,128)(2,1)S(1)}, bf16[64,16,128]{2,1,0:T(8,128)(2,1)S(1)}, u32[]{:S(2)}, u32[]{:S(2)}) %collective-permute-start.5) | collective-permute-done | bytes 262176 | tf_op jit(solution)/shard_map/ppermute | solution.py:402
  73.2 2.4 %shard_map.96 = (f32[1024,128]{1,0:T(8,128)S(1)}, f32[1024,128]{1,0:T(8,128)S(1)}, f32[8,128]{1,0:T(8,128)S(1)}) custom-call(bf16[64,65,128]{2,1,0:T(8,128)(2,1)S(1)} %all-to-all-done.own_ref, f32[8,1024]{1,0:T(8,128)S(1)} %shard_map.95.stats_ref), custom_call_target="tpu_custom_call" | custom-call | tf_op jit(solution)/shard_map/pallas_call | solution.py:434
  75.6 1.2 collective-permute-done.3.b1_ref.c1_ref
  76.8 1.6 %collective-permute-done.6.st1_ref = f32[8,1024]{1,0:T(8,128)S(1)} collective-permute-done((f32[8,1024]{1,0:T(8,128)S(1)}, f32[8,1024]{1,0:T(8,128)S(1)}, u32[]{:S(2)}, u32[]{:S(2)}) %collective-permute-start.6) | collective-permute-done | bytes 32800 | tf_op jit(solution)/shard_map/ppermute | solution.py:394
  78.4 1.1 shard_map.97
  79.5 7.7 %shard_map.98 = (f32[1024,128]{1,0:T(8,128)S(1)}, f32[8,128]{1,0:T(8,128)S(1)}) custom-call(s32[1]{0:T(128)} %bitcast.block_ref, bf16[64,65,128]{2,1,0:T(8,128)(2,1)S(1)} %all-to-all-done.own_ref, bf16[64,16,128]{2,1,0:T(8,128)(2,1)S(1)} %collective-permute-done.in1_ref.k1_ref.q1_ref, bf16[64,16,128]{2,1,0:T(8,128)(2,1)S(1)} %collective-permute-done.1.in2_ref.k2_ref.q2_ref, ...), custom_call_target="tpu_custom_call" | custom-call | tf_op jit(solution)/shard_map/pallas_call | solution.py:448
  87.2 3.2 %collective-permute-start.11 = (f32[8,128]{1,0:T(8,128)S(1)}, f32[8,128]{1,0:T(8,128)S(1)}, u32[]{:S(2)}, u32[]{:S(2)}) collective-permute-start(f32[8,128]{1,0:T(8,128)S(1)} %get-tuple-element.33.sums0_ref), channel_id=1, source_target_pairs={{0,192},{64,0},{128,64},{192,128},{1,193},{65,1},{129,65},{193,129... | collective-permute-start | bytes 12296 | tf_op jit(solution)/shard_map/ppermute | solution.py:394
  90.8 0.8 collective-permute-start.9
  91.6 2.8 %collective-permute-done.10.sums2_ref = f32[8,128]{1,0:T(8,128)S(1)} collective-permute-done((f32[8,128]{1,0:T(8,128)S(1)}, f32[8,128]{1,0:T(8,128)S(1)}, u32[]{:S(2)}, u32[]{:S(2)}) %collective-permute-start.10) | collective-permute-done | bytes 4128 | tf_op jit(solution)/shard_map/ppermute | solution.py:394
  94.5 0.9 shard_map.99
  95.5 28.9 %all_to_all.10 = f16[64,33,128]{2,1,0:T(8,128)(2,1)S(1)} all-to-all(f16[64,33,128]{2,1,0:T(8,128)(2,1)S(1)} %convert_element_type.6), channel_id=1, replica_groups=mesh['seq'=4,'head'=64] {'head'}, dimensions={0} | all-to-all | bytes 1081344 | tf_op jit(solution)/shard_map/all_to_all | solution.py:390
  124.4 1.2 shard_map.100
  (16 shorter events, 0.9 us)
Async XLA Ops:
  3.3 44.5 %all-to-all-start = ((bf16[64,65,128]{2,1,0:T(8,128)(2,1)}), bf16[64,65,128]{2,1,0:T(8,128)(2,1)S(1)}, u32[]{:S(2)}, u32[]{:S(2)}) async-start(bf16[64,65,128]{2,1,0:T(8,128)(2,1)} %shard_map.93), calls=%async_computation | async-start | bytes 2359296 | tf_op jit(solution)/shard_map/all_to_all | solution.py:390
  47.9 13.8 %collective-permute-start.2 = (bf16[64,16,128]{2,1,0:T(8,128)(2,1)S(1)}, bf16[64,16,128]{2,1,0:T(8,128)(2,1)S(1)}, u32[]{:S(2)}, u32[]{:S(2)}) collective-permute-start(bf16[64,16,128]{2,1,0:T(8,128)(2,1)S(1)} %get-tuple-element.38), channel_id=1, source_target_pairs={{0,192},{64,0},{128,64},{192,128},{1,193},{65,1},{129,65},{193,129... | collective-permute-start | bytes 786440 | tf_op jit(solution)/shard_map/ppermute | solution.py:402
  50.4 13.9 %collective-permute-start = (bf16[64,16,128]{2,1,0:T(8,128)(2,1)S(1)}, bf16[64,16,128]{2,1,0:T(8,128)(2,1)S(1)}, u32[]{:S(2)}, u32[]{:S(2)}) collective-permute-start(bf16[64,16,128]{2,1,0:T(8,128)(2,1)S(1)} %get-tuple-element.39), channel_id=1, source_target_pairs={{0,64},{64,128},{128,192},{192,0},{1,65},{65,129},{129,193},{193,1... | collective-permute-start | bytes 786440 | tf_op jit(solution)/shard_map/ppermute | solution.py:402
  50.4 13.9 %collective-permute-start.1 = (bf16[64,16,128]{2,1,0:T(8,128)(2,1)S(1)}, bf16[64,16,128]{2,1,0:T(8,128)(2,1)S(1)}, u32[]{:S(2)}, u32[]{:S(2)}) collective-permute-start(bf16[64,16,128]{2,1,0:T(8,128)(2,1)S(1)} %get-tuple-element.40), channel_id=1, source_target_pairs={{0,128},{64,192},{128,0},{192,64},{1,129},{65,193},{129,1},{193,65... | collective-permute-start | bytes 786440 | tf_op jit(solution)/shard_map/ppermute | solution.py:402
  53.5 19.7 %collective-permute-start.5 = (bf16[64,16,128]{2,1,0:T(8,128)(2,1)S(1)}, bf16[64,16,128]{2,1,0:T(8,128)(2,1)S(1)}, u32[]{:S(2)}, u32[]{:S(2)}) collective-permute-start(bf16[64,16,128]{2,1,0:T(8,128)(2,1)S(1)} %get-tuple-element.41), channel_id=1, source_target_pairs={{0,192},{64,0},{128,64},{192,128},{1,193},{65,1},{129,65},{193,129... | collective-permute-start | bytes 786440 | tf_op jit(solution)/shard_map/ppermute | solution.py:402
  54.6 22.2 %collective-permute-start.3 = (bf16[64,16,128]{2,1,0:T(8,128)(2,1)S(1)}, bf16[64,16,128]{2,1,0:T(8,128)(2,1)S(1)}, u32[]{:S(2)}, u32[]{:S(2)}) collective-permute-start(bf16[64,16,128]{2,1,0:T(8,128)(2,1)S(1)} %get-tuple-element.42), channel_id=1, source_target_pairs={{0,64},{64,128},{128,192},{192,0},{1,65},{65,129},{129,193},{193,1... | collective-permute-start | bytes 786440 | tf_op jit(solution)/shard_map/ppermute | solution.py:402
  61.6 15.2 %collective-permute-start.4 = (bf16[64,16,128]{2,1,0:T(8,128)(2,1)S(1)}, bf16[64,16,128]{2,1,0:T(8,128)(2,1)S(1)}, u32[]{:S(2)}, u32[]{:S(2)}) collective-permute-start(bf16[64,16,128]{2,1,0:T(8,128)(2,1)S(1)} %get-tuple-element.43), channel_id=1, source_target_pairs={{0,128},{64,192},{128,0},{192,64},{1,129},{65,193},{129,1},{193,65... | collective-permute-start | bytes 786440 | tf_op jit(solution)/shard_map/ppermute | solution.py:402
  64.9 11.9 %collective-permute-start.8 = (f32[8,1024]{1,0:T(8,128)S(1)}, f32[8,1024]{1,0:T(8,128)S(1)}, u32[]{:S(2)}, u32[]{:S(2)}) collective-permute-start(f32[8,1024]{1,0:T(8,128)S(1)} %shard_map.95.stats_ref), channel_id=1, source_target_pairs={{0,192},{64,0},{128,64},{192,128},{1,193},{65,1},{129,65},{193,129... | collective-permute-start | bytes 98312 | tf_op jit(solution)/shard_map/ppermute | solution.py:394
  69.3 7.5 %collective-permute-start.7 = (f32[8,1024]{1,0:T(8,128)S(1)}, f32[8,1024]{1,0:T(8,128)S(1)}, u32[]{:S(2)}, u32[]{:S(2)}) collective-permute-start(f32[8,1024]{1,0:T(8,128)S(1)} %shard_map.95.stats_ref), channel_id=1, source_target_pairs={{0,128},{64,192},{128,0},{192,64},{1,129},{65,193},{129,1},{193,65... | collective-permute-start | bytes 98312 | tf_op jit(solution)/shard_map/ppermute | solution.py:394
  73.2 5.2 %collective-permute-start.6 = (f32[8,1024]{1,0:T(8,128)S(1)}, f32[8,1024]{1,0:T(8,128)S(1)}, u32[]{:S(2)}, u32[]{:S(2)}) collective-permute-start(f32[8,1024]{1,0:T(8,128)S(1)} %shard_map.95.stats_ref), channel_id=1, source_target_pairs={{0,64},{64,128},{128,192},{192,0},{1,65},{65,129},{129,193},{193,1... | collective-permute-start | bytes 98312 | tf_op jit(solution)/shard_map/ppermute | solution.py:394
  87.2 4.4 %collective-permute-start.11 = (f32[8,128]{1,0:T(8,128)S(1)}, f32[8,128]{1,0:T(8,128)S(1)}, u32[]{:S(2)}, u32[]{:S(2)}) collective-permute-start(f32[8,128]{1,0:T(8,128)S(1)} %get-tuple-element.33.sums0_ref), channel_id=1, source_target_pairs={{0,192},{64,0},{128,64},{192,128},{1,193},{65,1},{129,65},{193,129... | collective-permute-start | bytes 12296 | tf_op jit(solution)/shard_map/ppermute | solution.py:394
  90.4 4.0 %collective-permute-start.10 = (f32[8,128]{1,0:T(8,128)S(1)}, f32[8,128]{1,0:T(8,128)S(1)}, u32[]{:S(2)}, u32[]{:S(2)}) collective-permute-start(f32[8,128]{1,0:T(8,128)S(1)} %get-tuple-element.33.sums0_ref), channel_id=1, source_target_pairs={{0,128},{64,192},{128,0},{192,64},{1,129},{65,193},{129,1},{193,65... | collective-permute-start | bytes 12296 | tf_op jit(solution)/shard_map/ppermute | solution.py:394
  90.8 3.7 %collective-permute-start.9 = (f32[8,128]{1,0:T(8,128)S(1)}, f32[8,128]{1,0:T(8,128)S(1)}, u32[]{:S(2)}, u32[]{:S(2)}) collective-permute-start(f32[8,128]{1,0:T(8,128)S(1)} %get-tuple-element.33.sums0_ref), channel_id=1, source_target_pairs={{0,64},{64,128},{128,192},{192,0},{1,65},{65,129},{129,193},{193,1... | collective-permute-start | bytes 12296 | tf_op jit(solution)/shard_map/ppermute | solution.py:394

commit v4 on v3

--- a/solution.py
+++ b/solution.py
@@ -13,6 +13,7 @@
 F16 = jnp.float16
 LOG2E = math.log2(math.e)
 TILE = 256
+TALL = 512
 WIDE = 512
 OWN = 512
 LOWEST = -1e30
@@ -129,9 +130,10 @@
 
 def stats_kernel(
     n, scale, block_ref, own_ref, in1_ref, in2_ref, in3_ref, local_ref, max_ref, sum_ref,
-    out_ref, q_s, k_s, max_s, sum_s,
+    out_ref, score_ref, q_s, k_s, max_s, sum_s,
 ):
     block = block_ref[0]
+    k_s[0, :, :] = take(own_ref, 0, n)
     rows = q_s.shape[0]
     q_s[...] = take(own_ref, 1, n)
     max_s[...] = max_ref[...]
@@ -141,7 +143,13 @@
 
     @pl.loop(1, block + 1)
     def _(d):
-        add_stats(dot_nt(q_s[...], k_s[d]), scale, max_s, sum_s, slice(None), False)
+        s = dot_nt(q_s[...], k_s[d])
+        score_ref[d - 1, :, :] = s
+        add_stats(s, scale, max_s, sum_s, slice(None), False)
+
+    @pl.loop(block + 1, 4)
+    def _(d):
+        score_ref[d - 1, :, :] = dot_nt(k_s[d], k_s[0])
 
     top = jnp.max(max_s[...], axis=1, keepdims=True)
     total = jnp.sum(sum_s[...] * jnp.exp2((max_s[...] - top) * scale), axis=1, keepdims=True)
@@ -206,17 +214,15 @@
 
 
 def rows_kernel(
-    n, scale, beta, block_ref, own_ref, k1_ref, k2_ref, k3_ref, b1_ref, b2_ref, b3_ref,
+    n, scale, beta, block_ref, own_ref, b1_ref, b2_ref, b3_ref, score_ref,
     stats_ref, st1_ref, st2_ref, st3_ref, gc_in_ref, sq_in_ref, gc_ref, out_ref, vec_ref,
-    q_s, c_s, k_s, b_s, cols_s, u_s, sq_s, cross_s,
+    c_s, b_s, cols_s, u_s, sq_s, cross_s,
 ):
     block = block_ref[0]
-    rows, width = q_s.shape
+    rows, width = c_s.shape
     fill_vec(block, (stats_ref, st1_ref, st2_ref, st3_ref), vec_ref)
-    q_s[...] = take(own_ref, 1, n)
     c_s[...] = take(own_ref, 3, n)
-    for d, (k_ref, b_ref) in enumerate(((k1_ref, b1_ref), (k2_ref, b2_ref), (k3_ref, b3_ref))):
-        k_s[d + 1, :, :] = take(k_ref, 0, n)
+    for d, b_ref in enumerate((b1_ref, b2_ref, b3_ref)):
         b_s[d + 1, :, :] = take(b_ref, 0, n)
     cols_s[...] = jnp.transpose(stats_ref[...])
     spread = jnp.transpose(vec_ref[...])
@@ -229,21 +235,23 @@
 
     @pl.loop(1, block + 1)
     def _(d):
-        q, c = q_s[...], c_s[...]
-        top_i, rinv_i, u_i = cols_s[:, 0:1], cols_s[:, 1:2], u_s[d]
-        gc = 0.0
+        cross = jnp.zeros((1, 1), F32)
         sq = sq_s[...]
-        for j in range(0, rows, WIDE):
-            tj = slice(j, j + WIDE)
-            k, b = k_s[d, tj, :], b_s[d, tj, :]
-            teacher = jnp.exp2((dot_nt(q, k) - top_i) * scale) * rinv_i
-            decay = u_i * vec_ref[pl.ds(d, 1), tj]
-            error = (dot_nt(c, b) * beta) * decay - teacher
-            sq = sq + fold_rows(error * error)
-            gc = gc + dot_nn((error * decay).astype(BF16), b)
-        cross = total_of(gc * c.astype(F32)) * beta
-        cross_s[...] += jnp.where((lane < block) & (lane >= block - d), cross, 0.0)
-        gc_ref[...] += gc
+        for i in range(0, rows, TALL):
+            ti = slice(i, i + TALL)
+            held = []
+            for j in range(0, rows, TILE):
+                tj = slice(j, j + TILE)
+                b = b_s[d, tj, :]
+                teacher = jnp.exp2((score_ref[d - 1, ti, tj] - cols_s[ti, 0:1]) * scale)
+                decay = u_s[d, ti, :] * vec_ref[pl.ds(d, 1), tj]
+                error = (dot_nt(c_s[ti, :], b) * beta) * decay - teacher * cols_s[ti, 1:2]
+                sq = sq + fold_rows(error * error)
+                held.append((error * decay).astype(BF16))
+            gc = dot_nn(jnp.concatenate(held, axis=1), b_s[d])
+            cross = cross + total_of(gc * c_s[ti, :].astype(F32))
+            gc_ref[ti, :] += gc
+        cross_s[...] += jnp.where((lane < block) & (lane >= block - d), cross * beta, 0.0)
         sq_s[...] = sq
 
     sums = jnp.where(lane == 3, total_of(sq_s[...]), cross_s[...])
@@ -251,19 +259,17 @@
 
 
 def cols_kernel(
-    n, scale, beta, block_ref, own_ref, q1_ref, q2_ref, q3_ref, c1_ref, c2_ref, c3_ref,
-    vec_ref, st1_ref, st2_ref, st3_ref, gb_in_ref, sums_in_ref, gb_ref, sums_ref,
-    k_s, b_s, q_s, c_s, cols_s, gbt_s,
+    n, scale, beta, block_ref, own_ref, c1_ref, c2_ref, c3_ref, score_ref, vec_ref,
+    st1_ref, st2_ref, st3_ref, gb_in_ref, sums_in_ref, gb_ref, sums_ref,
+    b_s, c_s, cols_s, gbt_s,
 ):
     block = block_ref[0]
-    rows, width = k_s.shape
+    rows, width = b_s.shape
     sums_ref[...] = sums_in_ref[...]
-    k_s[...] = take(own_ref, 0, n)
     b_s[...] = take(own_ref, 2, n)
     place = lax.broadcasted_iota(jnp.int32, (8, rows), 0)
-    incoming = ((q1_ref, c1_ref, st1_ref), (q2_ref, c2_ref, st2_ref), (q3_ref, c3_ref, st3_ref))
-    for d, (q_ref, c_ref, st_ref) in enumerate(incoming):
-        q_s[d + 1, :, :] = take(q_ref, 0, n)
+    incoming = ((c1_ref, st1_ref), (c2_ref, st2_ref), (c3_ref, st3_ref))
+    for d, (c_ref, st_ref) in enumerate(incoming):
         c_s[d + 1, :, :] = take(c_ref, 0, n)
         cols_s[d + 1, :, :] = jnp.transpose(
             jnp.where(place == 0, st_ref[0:1, :],
@@ -273,15 +279,14 @@
 
     @pl.loop(block + 1, 4)
     def _(d):
-        q, c = q_s[d], c_s[d]
+        c = c_s[d]
         ct = jnp.transpose(c.astype(F32)).astype(BF16)
         top_i, rinv_i, u_i = cols_s[d, :, 0:1], cols_s[d, :, 1:2], cols_s[d, :, 2:3]
         for j in range(0, rows, WIDE):
             tj = slice(j, j + WIDE)
-            k, b = k_s[tj, :], b_s[tj, :]
-            teacher = jnp.exp2((dot_nt(q, k) - top_i) * scale) * rinv_i
+            teacher = jnp.exp2((score_ref[d - 1, :, tj] - top_i) * scale) * rinv_i
             decay = u_i * vec_ref[pl.ds(d, 1), tj]
-            error = (dot_nt(c, b) * beta) * decay - teacher
+            error = (dot_nt(c, b_s[tj, :]) * beta) * decay - teacher
             gbt_s[:, tj] += dot_nn(ct, (error * decay).astype(BF16))
 
     gb_ref[...] = gb_in_ref[...] + jnp.transpose(gbt_s[...])
@@ -395,17 +400,17 @@
             for d in range(1, blocks)
         ]
 
-    def exchange(pair):
+    def exchange(pair, ahead=None):
         mine, after = pair[:, 0:n], pair[:, n:2 * n]
-        return [
-            held_near(
-                lax.ppermute(
-                    jnp.where(block + d < blocks, mine, after),
-                    "seq", [(i, (i + d) % blocks) for i in range(blocks)],
-                )
+        out = []
+        for d in range(1, blocks):
+            sent = jnp.where(block + d < blocks, mine, after)
+            if ahead is not None and d == 1:
+                sent, ahead[2] = lax.optimization_barrier((sent, ahead[2]))
+            out.append(
+                lax.ppermute(sent, "seq", [(i, (i + d) % blocks) for i in range(blocks)])
             )
-            for d in range(1, blocks)
-        ]
+        return out
 
     inputs = [
         pltpu.with_memory_space_constraint(x, pltpu.HBM)
@@ -426,9 +431,11 @@
         [near(8, rows), near(rows, 128), near(rows, 128)], [], 1, 2,
     )(rate_level, own)
     bc, local = lax.optimization_barrier((arrived[:, 2 * n:4 * n], local))
-    bc_from = exchange(bc)
-    stats = call(
-        functools.partial(stats_kernel, n, scale), near(8, rows), [mat, mats, state, state], 1, 8,
+    bc_from = exchange(bc, kq_from)
+    kq_from, bc_from = [[held_near(x) for x in y] for y in (kq_from, bc_from)]
+    stats, scores = call(
+        functools.partial(stats_kernel, n, scale),
+        [near(8, rows), near(blocks - 1, rows, rows)], [mat, mats, state, state], 1, 8,
     )(where, own, *kq_from, local, top, total)
     stats_from = [held_near(x) for x in around(stats)]
     gc, gb, sq = call(
@@ -440,17 +447,17 @@
         functools.partial(rows_kernel, n, scale, beta),
         [near(rows, width), near(8, 128), near(8, rows)],
         [
-            mat, mat, mats, mats, pltpu.VMEM((rows, 8), F32),
+            mat, mats, pltpu.VMEM((rows, 8), F32),
             pltpu.VMEM((4, rows, 1), F32), pltpu.VMEM((8, 128), F32), pltpu.VMEM((1, 128), F32),
         ],
-        1, 14,
-    )(where, own, *kq_from, *bc_from, stats, *stats_from, gc, sq)
+        1, 12,
+    )(where, own, *bc_from, scores, stats, *stats_from, gc, sq)
     gb, sums = call(
         functools.partial(cols_kernel, n, scale, beta),
         [near(rows, width), near(8, 128)],
-        [mat, mat, mats, mats, pltpu.VMEM((4, rows, 8), F32), flat],
-        1, 14,
-    )(where, own, *kq_from, *bc_from, vec, *stats_from, gb, sums)
+        [mat, mats, pltpu.VMEM((4, rows, 8), F32), flat],
+        1, 12,
+    )(where, own, *bc_from, scores, vec, *stats_from, gb, sums)
     sums_from = [held_near(x) for x in around(sums)]
     packed = call(
         functools.partial(finish_kernel, n, beta, float(seq_len)),

time: 126 us -> 122 us (0.968)
  waiting for transfers between devices: 49.4 us -> 42.2 us
  starting transfers between devices: 28 us -> 29.9 us
  Pallas kernels: 17.8 us -> 19.1 us
    ppermute x6, waiting for transfers between devices: 14.1 us -> 7.43 us  [exchange(): lax.ppermute(sent, 'seq', [(i, (i + d) % blocks) for i in range(blocks)])]
    pallas_call x1, Pallas kernels: 0.59 us -> 2.73 us  [per_device(): call(functools.partial(stats_kernel, n, scale), [near(8, rows), near(bloc...]
    ppermute x6, starting transfers between devices: 5.98 us -> 7.87 us  [exchange(): lax.ppermute(sent, 'seq', [(i, (i + d) % blocks) for i in range(blocks)])]
  transfers between devices with their start and end apart: 13 -> 13, of which waited for: 8 -> 5; matrix products, arithmetic and copies ran while one was open for 0% -> 0% of each run, Pallas kernels for 3% -> 5%
where the time goes in v4:
time: 122 us; the launch traced here: 121 us
  waiting for transfers between devices  42.2 us (35%)
  starting transfers between devices  29.9 us (25%)
  blocking collectives  28.4 us (23%)
  Pallas kernels  19.1 us (16%)
  between operations  1.38 us (1%)
    all_to_all x1, waiting for transfers between devices, to_heads(): return lax.all_to_all(x, 'head', split_axis=0, concat_axis=0, tiled=True)  30.7 us
    all_to_all x1, blocking collectives, to_heads(): return lax.all_to_all(x, 'head', split_axis=0, concat_axis=0, tiled=True)  28.4 us
    all_to_all x1, starting transfers between devices, to_heads(): return lax.all_to_all(x, 'head', split_axis=0, concat_axis=0, tiled=True)  13.2 us
    ppermute x6, starting transfers between devices, around(): lax.ppermute(x, 'seq', [(i, (i + d) % blocks) for i in range(blocks)])  8.88 us
    ppermute x6, starting transfers between devices, exchange(): lax.ppermute(sent, 'seq', [(i, (i + d) % blocks) for i in range(blocks)])  7.87 us
    ppermute x6, waiting for transfers between devices, exchange(): lax.ppermute(sent, 'seq', [(i, (i + d) % blocks) for i in range(blocks)])  7.43 us
    pallas_call x1, Pallas kernels, per_device(): call(functools.partial(cols_kernel, n, scale, beta), [near(rows, width),...  6.98 us
    ppermute x6, waiting for transfers between devices, around(): lax.ppermute(x, 'seq', [(i, (i + d) % blocks) for i in range(blocks)])  4.08 us
  transfers between devices with their start and end apart: 13, of which 5 were waited for; matrix products, arithmetic and copies ran while one was open for 0% of the time, Pallas kernels for 5%

profile of v4, /device:TPU:1, one launch (start us, length us, event | category | flops | bytes accessed | tf_op | source)
XLA Modules:
  0.0 121.4 jit_solution(7911287581355278746)
XLA Ops:
  0.6 2.6 %shard_map.93 = bf16[64,65,128]{2,1,0:T(8,128)(2,1)} custom-call(bf16[16,64,128]{2,1,0:T(8,128)(2,1)} %refs_0_.1, bf16[16,64,128]{2,1,0:T(8,128)(2,1)} %refs_1_.1, bf16[16,64,128]{2,1,0:T(8,128)(2,1)} %refs_2_.1, bf16[16,64,128]{2,1,0:T(8,128)(2,1)} %refs_3_.1, bf16[16,64]{1,0:T(8,128)(2,1)} %refs_4_.1), custom_call_target="tpu_custom_call" | custom-call | tf_op jit(solution)/shard_map/pallas_call | solution.py:420
  3.3 13.2 %all-to-all-start = ((bf16[64,65,128]{2,1,0:T(8,128)(2,1)}), bf16[64,65,128]{2,1,0:T(8,128)(2,1)S(1)}, u32[]{:S(2)}, u32[]{:S(2)}) async-start(bf16[64,65,128]{2,1,0:T(8,128)(2,1)} %shard_map.93), calls=%async_computation | async-start | bytes 2359296 | tf_op jit(solution)/shard_map/all_to_all | solution.py:395
  17.1 30.7 %all-to-all-done.own_ref = bf16[64,65,128]{2,1,0:T(8,128)(2,1)S(1)} async-done(((bf16[64,65,128]{2,1,0:T(8,128)(2,1)}), bf16[64,65,128]{2,1,0:T(8,128)(2,1)S(1)}, u32[]{:S(2)}, u32[]{:S(2)}) %all-to-all-start) | async-done | bytes 1064992 | tf_op jit(solution)/shard_map/all_to_all | solution.py:395
  47.9 2.8 %collective-permute-start.5 = (bf16[64,16,128]{2,1,0:T(8,128)(2,1)S(1)}, bf16[64,16,128]{2,1,0:T(8,128)(2,1)S(1)}, u32[]{:S(2)}, u32[]{:S(2)}) collective-permute-start(bf16[64,16,128]{2,1,0:T(8,128)(2,1)S(1)} %get-tuple-element.46), channel_id=1, source_target_pairs={{0,128},{64,192},{128,0},{192,64},{1,129},{65,193},{129,1},{193,65... | collective-permute-start | bytes 786440 | tf_op jit(solution)/shard_map/ppermute | solution.py:411
  50.7 0.9 collective-permute-start
  51.6 0.6 collective-permute-start.4
  52.2 1.3 %shard_map.94 = (f32[8,1024]{1,0:T(8,128)S(1)}, f32[1024,128]{1,0:T(8,128)S(1)}, f32[1024,128]{1,0:T(8,128)S(1)}) custom-call(s32[1]{0:T(128)S(6)} %copy.10.level_ref, bf16[64,65,128]{2,1,0:T(8,128)(2,1)S(1)} %all-to-all-done.own_ref), custom_call_target="tpu_custom_call" | custom-call | tf_op jit(solution)/shard_map/pallas_call | solution.py:429
  53.5 2.1 %collective-permute-start.3 = (bf16[64,16,128]{2,1,0:T(8,128)(2,1)S(1)}, bf16[64,16,128]{2,1,0:T(8,128)(2,1)S(1)}, u32[]{:S(2)}, u32[]{:S(2)}) collective-permute-start(bf16[64,16,128]{2,1,0:T(8,128)(2,1)S(1)} %get-tuple-element.49), channel_id=1, source_target_pairs={{0,192},{64,0},{128,64},{192,128},{1,193},{65,1},{129,65},{193,129... | collective-permute-start | bytes 786440 | tf_op jit(solution)/shard_map/ppermute | solution.py:411
  55.7 7.4 %collective-permute-done.in3_ref = bf16[64,16,128]{2,1,0:T(8,128)(2,1)S(1)} collective-permute-done((bf16[64,16,128]{2,1,0:T(8,128)(2,1)S(1)}, bf16[64,16,128]{2,1,0:T(8,128)(2,1)S(1)}, u32[]{:S(2)}, u32[]{:S(2)}) %collective-permute-start) | collective-permute-done | bytes 262176 | tf_op jit(solution)/shard_map/ppermute | solution.py:411
  63.1 1.4 %collective-permute-start.1 = (bf16[64,16,128]{2,1,0:T(8,128)(2,1)S(1)}, bf16[64,16,128]{2,1,0:T(8,128)(2,1)S(1)}, u32[]{:S(2)}, u32[]{:S(2)}) collective-permute-start(bf16[64,16,128]{2,1,0:T(8,128)(2,1)S(1)} %get-tuple-element.27), channel_id=1, source_target_pairs={{0,64},{64,128},{128,192},{192,0},{1,65},{65,129},{129,193},{193,1... | collective-permute-start | bytes 786440 | tf_op jit(solution)/shard_map/ppermute | solution.py:411
  64.5 2.7 %shard_map.95 = (f32[8,1024]{1,0:T(8,128)S(1)}, f32[3,1024,1024]{2,1,0:T(8,128)S(1)}) custom-call(s32[1]{0:T(128)} %bitcast.block_ref, bf16[64,65,128]{2,1,0:T(8,128)(2,1)S(1)} %all-to-all-done.own_ref, bf16[64,16,128]{2,1,0:T(8,128)(2,1)S(1)} %collective-permute-done.4.in1_ref, bf16[64,16,128]{2,1,0:T(8,128)(2,1)S(1)} %collective-permute-done.5.in2_ref, ...), custom_call_target="tpu_custom_call" | custom-call | tf_op jit(solution)/shard_map/pallas_call | solution.py:436
  67.3 2.8 %collective-permute-start.8 = (f32[8,1024]{1,0:T(8,128)S(1)}, f32[8,1024]{1,0:T(8,128)S(1)}, u32[]{:S(2)}, u32[]{:S(2)}) collective-permute-start(f32[8,1024]{1,0:T(8,128)S(1)} %get-tuple-element.33.stats_ref), channel_id=1, source_target_pairs={{0,192},{64,0},{128,64},{192,128},{1,193},{65,1},{129,65},{193,129... | collective-permute-start | bytes 98312 | tf_op jit(solution)/shard_map/ppermute | solution.py:399
  70.0 0.8 collective-permute-start.7
  70.8 0.8 collective-permute-start.6
  71.6 2.4 %shard_map.96 = (f32[1024,128]{1,0:T(8,128)S(1)}, f32[1024,128]{1,0:T(8,128)S(1)}, f32[8,128]{1,0:T(8,128)S(1)}) custom-call(bf16[64,65,128]{2,1,0:T(8,128)(2,1)S(1)} %all-to-all-done.own_ref, f32[8,1024]{1,0:T(8,128)S(1)} %get-tuple-element.33.stats_ref), custom_call_target="tpu_custom_call" | custom-call | tf_op jit(solution)/shard_map/pallas_call | solution.py:441
  74.0 1.1 collective-permute-done.8.st3_ref
  75.1 1.0 shard_map.97
  76.1 7.0 %shard_map.98 = (f32[1024,128]{1,0:T(8,128)S(1)}, f32[8,128]{1,0:T(8,128)S(1)}) custom-call(s32[1]{0:T(128)} %bitcast.block_ref, bf16[64,65,128]{2,1,0:T(8,128)(2,1)S(1)} %all-to-all-done.own_ref, bf16[64,16,128]{2,1,0:T(8,128)(2,1)S(1)} %collective-permute-done.1.b1_ref.c1_ref, bf16[64,16,128]{2,1,0:T(8,128)(2,1)S(1)} %collective-permute-done.2.b2_ref.c2_ref, ...), custom_call_target="tpu_custom_call" | custom-call | tf_op jit(solution)/shard_map/pallas_call | solution.py:455
  83.1 3.4 %collective-permute-start.11 = (f32[8,128]{1,0:T(8,128)S(1)}, f32[8,128]{1,0:T(8,128)S(1)}, u32[]{:S(2)}, u32[]{:S(2)}) collective-permute-start(f32[8,128]{1,0:T(8,128)S(1)} %get-tuple-element.41.sums0_ref), channel_id=1, source_target_pairs={{0,192},{64,0},{128,64},{192,128},{1,193},{65,1},{129,65},{193,129... | collective-permute-start | bytes 12296 | tf_op jit(solution)/shard_map/ppermute | solution.py:399
  87.0 0.7 collective-permute-start.9
  87.7 2.8 %collective-permute-done.10.sums2_ref = f32[8,128]{1,0:T(8,128)S(1)} collective-permute-done((f32[8,128]{1,0:T(8,128)S(1)}, f32[8,128]{1,0:T(8,128)S(1)}, u32[]{:S(2)}, u32[]{:S(2)}) %collective-permute-start.10) | collective-permute-done | bytes 4128 | tf_op jit(solution)/shard_map/ppermute | solution.py:399
  90.6 0.9 shard_map.99
  91.6 28.4 %all_to_all.10 = f16[64,33,128]{2,1,0:T(8,128)(2,1)S(1)} all-to-all(f16[64,33,128]{2,1,0:T(8,128)(2,1)S(1)} %convert_element_type.6), channel_id=1, replica_groups=mesh['seq'=4,'head'=64] {'head'}, dimensions={0} | all-to-all | bytes 1081344 | tf_op jit(solution)/shard_map/all_to_all | solution.py:395
  120.1 1.2 %shard_map.100 = (f32[16,64,128]{2,1,0:T(8,128)}, f32[16,64,128]{2,1,0:T(8,128)}, f32[16,64]{1,0:T(8,128)}, f32[1,1]{1,0:T(1,128)}) custom-call(f32[64,33,128]{2,1,0:T(8,128)S(1)} %convert_element_type.7.x_ref), custom_call_target="tpu_custom_call" | custom-call | tf_op jit(solution)/shard_map/pallas_call | solution.py:467
  (16 shorter events, 1.0 us)
Async XLA Ops:
  3.3 44.5 %all-to-all-start = ((bf16[64,65,128]{2,1,0:T(8,128)(2,1)}), bf16[64,65,128]{2,1,0:T(8,128)(2,1)S(1)}, u32[]{:S(2)}, u32[]{:S(2)}) async-start(bf16[64,65,128]{2,1,0:T(8,128)(2,1)} %shard_map.93), calls=%async_computation | async-start | bytes 2359296 | tf_op jit(solution)/shard_map/all_to_all | solution.py:395
  47.9 16.7 %collective-permute-start.5 = (bf16[64,16,128]{2,1,0:T(8,128)(2,1)S(1)}, bf16[64,16,128]{2,1,0:T(8,128)(2,1)S(1)}, u32[]{:S(2)}, u32[]{:S(2)}) collective-permute-start(bf16[64,16,128]{2,1,0:T(8,128)(2,1)S(1)} %get-tuple-element.46), channel_id=1, source_target_pairs={{0,128},{64,192},{128,0},{192,64},{1,129},{65,193},{129,1},{193,65... | collective-permute-start | bytes 786440 | tf_op jit(solution)/shard_map/ppermute | solution.py:411
  50.7 12.4 %collective-permute-start = (bf16[64,16,128]{2,1,0:T(8,128)(2,1)S(1)}, bf16[64,16,128]{2,1,0:T(8,128)(2,1)S(1)}, u32[]{:S(2)}, u32[]{:S(2)}) collective-permute-start(bf16[64,16,128]{2,1,0:T(8,128)(2,1)S(1)} %get-tuple-element.47), channel_id=1, source_target_pairs={{0,192},{64,0},{128,64},{192,128},{1,193},{65,1},{129,65},{193,129... | collective-permute-start | bytes 786440 | tf_op jit(solution)/shard_map/ppermute | solution.py:411
  51.6 13.0 %collective-permute-start.4 = (bf16[64,16,128]{2,1,0:T(8,128)(2,1)S(1)}, bf16[64,16,128]{2,1,0:T(8,128)(2,1)S(1)}, u32[]{:S(2)}, u32[]{:S(2)}) collective-permute-start(bf16[64,16,128]{2,1,0:T(8,128)(2,1)S(1)} %get-tuple-element.48), channel_id=1, source_target_pairs={{0,64},{64,128},{128,192},{192,0},{1,65},{65,129},{129,193},{193,1... | collective-permute-start | bytes 786440 | tf_op jit(solution)/shard_map/ppermute | solution.py:411
  53.5 17.3 %collective-permute-start.3 = (bf16[64,16,128]{2,1,0:T(8,128)(2,1)S(1)}, bf16[64,16,128]{2,1,0:T(8,128)(2,1)S(1)}, u32[]{:S(2)}, u32[]{:S(2)}) collective-permute-start(bf16[64,16,128]{2,1,0:T(8,128)(2,1)S(1)} %get-tuple-element.49), channel_id=1, source_target_pairs={{0,192},{64,0},{128,64},{192,128},{1,193},{65,1},{129,65},{193,129... | collective-permute-start | bytes 786440 | tf_op jit(solution)/shard_map/ppermute | solution.py:411
  55.7 18.3 %collective-permute-start.2 = (bf16[64,16,128]{2,1,0:T(8,128)(2,1)S(1)}, bf16[64,16,128]{2,1,0:T(8,128)(2,1)S(1)}, u32[]{:S(2)}, u32[]{:S(2)}) collective-permute-start(bf16[64,16,128]{2,1,0:T(8,128)(2,1)S(1)} %get-tuple-element.51), channel_id=1, source_target_pairs={{0,128},{64,192},{128,0},{192,64},{1,129},{65,193},{129,1},{193,65... | collective-permute-start | bytes 786440 | tf_op jit(solution)/shard_map/ppermute | solution.py:411
  63.1 12.0 %collective-permute-start.1 = (bf16[64,16,128]{2,1,0:T(8,128)(2,1)S(1)}, bf16[64,16,128]{2,1,0:T(8,128)(2,1)S(1)}, u32[]{:S(2)}, u32[]{:S(2)}) collective-permute-start(bf16[64,16,128]{2,1,0:T(8,128)(2,1)S(1)} %get-tuple-element.27), channel_id=1, source_target_pairs={{0,64},{64,128},{128,192},{192,0},{1,65},{65,129},{129,193},{193,1... | collective-permute-start | bytes 786440 | tf_op jit(solution)/shard_map/ppermute | solution.py:411
  67.3 7.8 %collective-permute-start.8 = (f32[8,1024]{1,0:T(8,128)S(1)}, f32[8,1024]{1,0:T(8,128)S(1)}, u32[]{:S(2)}, u32[]{:S(2)}) collective-permute-start(f32[8,1024]{1,0:T(8,128)S(1)} %get-tuple-element.33.stats_ref), channel_id=1, source_target_pairs={{0,192},{64,0},{128,64},{192,128},{1,193},{65,1},{129,65},{193,129... | collective-permute-start | bytes 98312 | tf_op jit(solution)/shard_map/ppermute | solution.py:399
  70.0 5.1 %collective-permute-start.7 = (f32[8,1024]{1,0:T(8,128)S(1)}, f32[8,1024]{1,0:T(8,128)S(1)}, u32[]{:S(2)}, u32[]{:S(2)}) collective-permute-start(f32[8,1024]{1,0:T(8,128)S(1)} %get-tuple-element.33.stats_ref), channel_id=1, source_target_pairs={{0,128},{64,192},{128,0},{192,64},{1,129},{65,193},{129,1},{193,65... | collective-permute-start | bytes 98312 | tf_op jit(solution)/shard_map/ppermute | solution.py:399
  70.8 4.3 %collective-permute-start.6 = (f32[8,1024]{1,0:T(8,128)S(1)}, f32[8,1024]{1,0:T(8,128)S(1)}, u32[]{:S(2)}, u32[]{:S(2)}) collective-permute-start(f32[8,1024]{1,0:T(8,128)S(1)} %get-tuple-element.33.stats_ref), channel_id=1, source_target_pairs={{0,64},{64,128},{128,192},{192,0},{1,65},{65,129},{129,193},{193,1... | collective-permute-start | bytes 98312 | tf_op jit(solution)/shard_map/ppermute | solution.py:399
  83.1 4.6 %collective-permute-start.11 = (f32[8,128]{1,0:T(8,128)S(1)}, f32[8,128]{1,0:T(8,128)S(1)}, u32[]{:S(2)}, u32[]{:S(2)}) collective-permute-start(f32[8,128]{1,0:T(8,128)S(1)} %get-tuple-element.41.sums0_ref), channel_id=1, source_target_pairs={{0,192},{64,0},{128,64},{192,128},{1,193},{65,1},{129,65},{193,129... | collective-permute-start | bytes 12296 | tf_op jit(solution)/shard_map/ppermute | solution.py:399
  86.5 4.0 %collective-permute-start.10 = (f32[8,128]{1,0:T(8,128)S(1)}, f32[8,128]{1,0:T(8,128)S(1)}, u32[]{:S(2)}, u32[]{:S(2)}) collective-permute-start(f32[8,128]{1,0:T(8,128)S(1)} %get-tuple-element.41.sums0_ref), channel_id=1, source_target_pairs={{0,128},{64,192},{128,0},{192,64},{1,129},{65,193},{129,1},{193,65... | collective-permute-start | bytes 12296 | tf_op jit(solution)/shard_map/ppermute | solution.py:399
  87.0 3.7 %collective-permute-start.9 = (f32[8,128]{1,0:T(8,128)S(1)}, f32[8,128]{1,0:T(8,128)S(1)}, u32[]{:S(2)}, u32[]{:S(2)}) collective-permute-start(f32[8,128]{1,0:T(8,128)S(1)} %get-tuple-element.41.sums0_ref), channel_id=1, source_target_pairs={{0,64},{64,128},{128,192},{192,0},{1,65},{65,129},{129,193},{193,1... | collective-permute-start | bytes 12296 | tf_op jit(solution)/shard_map/ppermute | solution.py:399

commit v5 on v4

--- a/solution.py
+++ b/solution.py
@@ -84,14 +84,14 @@
     return high, y - high
 
 
-def add_stats(s, scale, max_ref, sum_ref, ti, first):
+def add_stats(s, max_ref, sum_ref, ti, first):
     new = LOWEST if first else max_ref[ti, :]
     size = s.shape[1]
     for g in range(0, size, 128):
         new = jnp.maximum(new, s[:, g:g + 128])
-    acc = 0.0 if first else sum_ref[ti, :] * jnp.exp2((max_ref[ti, :] - new) * scale)
+    acc = 0.0 if first else sum_ref[ti, :] * jnp.exp2(max_ref[ti, :] - new)
     for g in range(0, size, 128):
-        acc = acc + jnp.exp2((s[:, g:g + 128] - new) * scale)
+        acc = acc + jnp.exp2(s[:, g:g + 128] - new)
     max_ref[ti, :] = new
     sum_ref[ti, :] = acc
 
@@ -117,10 +117,10 @@
     k, q = take(own_ref, 0, n), take(own_ref, 1, n)
     for at in range(0, rows, TILE):
         ti = slice(at, at + TILE)
-        s = dot_nt(q[ti, :], k[0:at + TILE, :])
+        s = dot_nt(q[ti, :], k[0:at + TILE, :]) * scale
         row = lax.broadcasted_iota(jnp.int32, s.shape, 0) + at
         col = lax.broadcasted_iota(jnp.int32, s.shape, 1)
-        add_stats(jnp.where(col <= row, s, LOWEST), scale, max_ref, sum_ref, ti, True)
+        add_stats(jnp.where(col <= row, s, LOWEST), max_ref, sum_ref, ti, True)
 
     level = jnp.full((1, 1), level_ref[0], jnp.int32).astype(F32)
     steps = own_ref[:, 4 * n:4 * n + 1, :].astype(F32).reshape(heads, 128)
@@ -143,18 +143,17 @@
 
     @pl.loop(1, block + 1)
     def _(d):
-        s = dot_nt(q_s[...], k_s[d])
+        s = dot_nt(q_s[...], k_s[d]) * scale
         score_ref[d - 1, :, :] = s
-        add_stats(s, scale, max_s, sum_s, slice(None), False)
+        add_stats(s, max_s, sum_s, slice(None), False)
 
     @pl.loop(block + 1, 4)
     def _(d):
-        score_ref[d - 1, :, :] = dot_nt(k_s[d], k_s[0])
+        score_ref[d - 1, :, :] = dot_nt(k_s[d], k_s[0]) * scale
 
     top = jnp.max(max_s[...], axis=1, keepdims=True)
-    total = jnp.sum(sum_s[...] * jnp.exp2((max_s[...] - top) * scale), axis=1, keepdims=True)
-    lane = lax.broadcasted_iota(jnp.int32, (rows, 8), 1)
-    out_ref[...] = jnp.transpose(jnp.where(lane == 0, top, 1.0 / total))
+    total = jnp.sum(sum_s[...] * jnp.exp2(max_s[...] - top), axis=1, keepdims=True)
+    out_ref[...] = jnp.transpose(jnp.broadcast_to(top + jnp.log2(total), (rows, 8)))
     out_ref[2:3, :] = local_ref[0:1, :]
 
 
@@ -189,19 +188,19 @@
     for i in range(0, rows, OWN):
         ti = slice(i, i + OWN)
         q, c = q_all[ti, :], c_all[ti, :]
-        top_i, rinv_i, sum_i = cols_s[ti, 0:1], cols_s[ti, 1:2], cols_s[ti, 2:3]
+        top_i, sum_i = cols_s[ti, 0:1], cols_s[ti, 2:3]
         gc = 0.0
         for j in range(0, i + OWN, OWN):
             tj = slice(j, j + OWN)
             k, b = k_all[tj, :], b_all[tj, :]
-            s = dot_nt(q, k) - top_i
+            s = dot_nt(q, k) * scale - top_i
             gap = sum_i - stats_ref[2:3, tj]
             if i == j:
                 row = lax.broadcasted_iota(jnp.int32, s.shape, 0)
                 col = lax.broadcasted_iota(jnp.int32, s.shape, 1)
                 s = jnp.where(col <= row, s, LOWEST)
                 gap = jnp.where(col <= row, gap, LOWEST)
-            teacher = jnp.exp2(s * scale) * rinv_i
+            teacher = jnp.exp2(s)
             decay = jnp.exp2(gap * LOG2E)
             error = (dot_nt(c, b) * beta) * decay - teacher
             sq = sq + fold_rows(error * error)
@@ -213,24 +212,27 @@
     sq_ref[...] = sq
 
 
-def rows_kernel(
-    n, scale, beta, block_ref, own_ref, b1_ref, b2_ref, b3_ref, score_ref,
-    stats_ref, st1_ref, st2_ref, st3_ref, gc_in_ref, sq_in_ref, gc_ref, out_ref, vec_ref,
-    c_s, b_s, cols_s, u_s, sq_s, cross_s,
+def blocks_kernel(
+    n, beta, block_ref, own_ref, in1_ref, in2_ref, in3_ref, score_ref,
+    stats_ref, st1_ref, st2_ref, st3_ref, gc_in_ref, gb_in_ref, sq_in_ref,
+    gc_ref, gb_ref, out_ref,
+    b_s, c_s, in_s, vec_s, cols_s, gbt_s, sq_s, cross_s,
 ):
     block = block_ref[0]
     rows, width = c_s.shape
-    fill_vec(block, (stats_ref, st1_ref, st2_ref, st3_ref), vec_ref)
+    b_s[...] = take(own_ref, 2, n)
     c_s[...] = take(own_ref, 3, n)
-    for d, b_ref in enumerate((b1_ref, b2_ref, b3_ref)):
-        b_s[d + 1, :, :] = take(b_ref, 0, n)
-    cols_s[...] = jnp.transpose(stats_ref[...])
-    spread = jnp.transpose(vec_ref[...])
-    for d in range(1, 4):
-        u_s[d, :, :] = spread[:, 3 + d:4 + d]
+    fill_vec(block, (stats_ref, st1_ref, st2_ref, st3_ref), vec_s)
+    place = lax.broadcasted_iota(jnp.int32, (8, rows), 0)
+    incoming = ((in1_ref, st1_ref), (in2_ref, st2_ref), (in3_ref, st3_ref))
+    for d, (in_ref, st_ref) in enumerate(incoming, 1):
+        in_s[d, :, :] = take(in_ref, 0, n)
+        top = jnp.where(block >= d, stats_ref[0:1, :], st_ref[0:1, :])
+        cols_s[d, :, :] = jnp.transpose(jnp.where(place == 0, top, vec_s[3 + d:4 + d, :]))
     gc_ref[...] = gc_in_ref[...]
     sq_s[...] = sq_in_ref[...]
     cross_s[...] = jnp.zeros(cross_s.shape, F32)
+    gbt_s[...] = jnp.zeros(gbt_s.shape, F32)
     lane = lax.broadcasted_iota(jnp.int32, (1, 128), 1)
 
     @pl.loop(1, block + 1)
@@ -242,54 +244,32 @@
             held = []
             for j in range(0, rows, TILE):
                 tj = slice(j, j + TILE)
-                b = b_s[d, tj, :]
-                teacher = jnp.exp2((score_ref[d - 1, ti, tj] - cols_s[ti, 0:1]) * scale)
-                decay = u_s[d, ti, :] * vec_ref[pl.ds(d, 1), tj]
-                error = (dot_nt(c_s[ti, :], b) * beta) * decay - teacher * cols_s[ti, 1:2]
+                teacher = jnp.exp2(score_ref[d - 1, ti, tj] - cols_s[d, ti, 0:1])
+                decay = cols_s[d, ti, 1:2] * vec_s[pl.ds(d, 1), tj]
+                error = (dot_nt(c_s[ti, :], in_s[d, tj, :]) * beta) * decay - teacher
                 sq = sq + fold_rows(error * error)
                 held.append((error * decay).astype(BF16))
-            gc = dot_nn(jnp.concatenate(held, axis=1), b_s[d])
+            gc = dot_nn(jnp.concatenate(held, axis=1), in_s[d])
             cross = cross + total_of(gc * c_s[ti, :].astype(F32))
             gc_ref[ti, :] += gc
         cross_s[...] += jnp.where((lane < block) & (lane >= block - d), cross * beta, 0.0)
         sq_s[...] = sq
 
+    @pl.loop(block + 1, 4)
+    def _(d):
+        c = in_s[d]
+        ct = jnp.transpose(c.astype(F32)).astype(BF16)
+        top_i, u_i = cols_s[d, :, 0:1], cols_s[d, :, 1:2]
+        for j in range(0, rows, WIDE):
+            tj = slice(j, j + WIDE)
+            teacher = jnp.exp2(score_ref[d - 1, :, tj] - top_i)
+            decay = u_i * vec_s[pl.ds(d, 1), tj]
+            error = (dot_nt(c, b_s[tj, :]) * beta) * decay - teacher
+            gbt_s[:, tj] += dot_nn(ct, (error * decay).astype(BF16))
+
+    gb_ref[...] = gb_in_ref[...] + jnp.transpose(gbt_s[...])
     sums = jnp.where(lane == 3, total_of(sq_s[...]), cross_s[...])
     out_ref[...] = jnp.broadcast_to(sums, out_ref.shape)
-
-
-def cols_kernel(
-    n, scale, beta, block_ref, own_ref, c1_ref, c2_ref, c3_ref, score_ref, vec_ref,
-    st1_ref, st2_ref, st3_ref, gb_in_ref, sums_in_ref, gb_ref, sums_ref,
-    b_s, c_s, cols_s, gbt_s,
-):
-    block = block_ref[0]
-    rows, width = b_s.shape
-    sums_ref[...] = sums_in_ref[...]
-    b_s[...] = take(own_ref, 2, n)
-    place = lax.broadcasted_iota(jnp.int32, (8, rows), 0)
-    incoming = ((c1_ref, st1_ref), (c2_ref, st2_ref), (c3_ref, st3_ref))
-    for d, (c_ref, st_ref) in enumerate(incoming):
-        c_s[d + 1, :, :] = take(c_ref, 0, n)
-        cols_s[d + 1, :, :] = jnp.transpose(
-            jnp.where(place == 0, st_ref[0:1, :],
-                      jnp.where(place == 1, st_ref[1:2, :], vec_ref[4 + d:5 + d, :]))
-        )
-    gbt_s[...] = jnp.zeros(gbt_s.shape, F32)
-
-    @pl.loop(block + 1, 4)
-    def _(d):
-        c = c_s[d]
-        ct = jnp.transpose(c.astype(F32)).astype(BF16)
-        top_i, rinv_i, u_i = cols_s[d, :, 0:1], cols_s[d, :, 1:2], cols_s[d, :, 2:3]
-        for j in range(0, rows, WIDE):
-            tj = slice(j, j + WIDE)
-            teacher = jnp.exp2((score_ref[d - 1, :, tj] - top_i) * scale) * rinv_i
-            decay = u_i * vec_ref[pl.ds(d, 1), tj]
-            error = (dot_nt(c, b_s[tj, :]) * beta) * decay - teacher
-            gbt_s[:, tj] += dot_nn(ct, (error * decay).astype(BF16))
-
-    gb_ref[...] = gb_in_ref[...] + jnp.transpose(gbt_s[...])
 
 
 def finish_kernel(
@@ -443,21 +423,15 @@
         [near(rows, width), near(rows, width), near(8, 128)],
         [flat, pltpu.VMEM((rows, 8), F32)], 0, 2,
     )(own, stats)
-    gc, sums, vec = call(
-        functools.partial(rows_kernel, n, scale, beta),
-        [near(rows, width), near(8, 128), near(8, rows)],
+    gc, gb, sums = call(
+        functools.partial(blocks_kernel, n, beta),
+        [near(rows, width), near(rows, width), near(8, 128)],
         [
-            mat, mats, pltpu.VMEM((rows, 8), F32),
-            pltpu.VMEM((4, rows, 1), F32), pltpu.VMEM((8, 128), F32), pltpu.VMEM((1, 128), F32),
+            mat, mat, mats, pltpu.VMEM((8, rows), F32), pltpu.VMEM((4, rows, 8), F32), flat,
+            pltpu.VMEM((8, 128), F32), pltpu.VMEM((1, 128), F32),
         ],
-        1, 12,
-    )(where, own, *bc_from, scores, stats, *stats_from, gc, sq)
-    gb, sums = call(
-        functools.partial(cols_kernel, n, scale, beta),
-        [near(rows, width), near(8, 128)],
-        [mat, mats, pltpu.VMEM((4, rows, 8), F32), flat],
-        1, 12,
-    )(where, own, *bc_from, scores, vec, *stats_from, gb, sums)
+        1, 13,
+    )(where, own, *bc_from, scores, stats, *stats_from, gc, gb, sq)
     sums_from = [held_near(x) for x in around(sums)]
     packed = call(
         functools.partial(finish_kernel, n, beta, float(seq_len)),

time: 122 us -> 120 us (0.984)
  Pallas kernels: 19.1 us -> 17.8 us
    pallas_call x2 -> x1, Pallas kernels: 7.98 us -> 6.71 us  [per_device(): call(functools.partial(blocks_kernel, n, beta), [near(rows, width), near(...]
  transfers between devices with their start and end apart: 13 -> 13, of which waited for: 5 -> 6; matrix products, arithmetic and copies ran while one was open for 0% -> 0% of each run, Pallas kernels for 5% -> 5%
where the time goes in v5:
time: 120 us
  waiting for transfers between devices  42.3 us (35%)
  starting transfers between devices  29.6 us (25%)
  blocking collectives  28.7 us (24%)
  Pallas kernels  17.8 us (15%)
  between operations  1.38 us (1%)
    all_to_all x1, waiting for transfers between devices, to_heads(): return lax.all_to_all(x, 'head', split_axis=0, concat_axis=0, tiled=True)  30.7 us
    all_to_all x1, blocking collectives, to_heads(): return lax.all_to_all(x, 'head', split_axis=0, concat_axis=0, tiled=True)  28.7 us
    all_to_all x1, starting transfers between devices, to_heads(): return lax.all_to_all(x, 'head', split_axis=0, concat_axis=0, tiled=True)  13.2 us
    ppermute x6, starting transfers between devices, around(): lax.ppermute(x, 'seq', [(i, (i + d) % blocks) for i in range(blocks)])  8.51 us
    ppermute x6, starting transfers between devices, exchange(): lax.ppermute(sent, 'seq', [(i, (i + d) % blocks) for i in range(blocks)])  7.89 us
    ppermute x6, waiting for transfers between devices, exchange(): lax.ppermute(sent, 'seq', [(i, (i + d) % blocks) for i in range(blocks)])  7.38 us
    pallas_call x1, Pallas kernels, per_device(): call(functools.partial(blocks_kernel, n, beta), [near(rows, width), near(...  6.71 us
    ppermute x6, waiting for transfers between devices, around(): lax.ppermute(x, 'seq', [(i, (i + d) % blocks) for i in range(blocks)])  4.27 us
  transfers between devices with their start and end apart: 13, of which 6 were waited for; matrix products, arithmetic and copies ran while one was open for 0% of the time, Pallas kernels for 5%

profile of v5, /device:TPU:1, one launch (start us, length us, event | category | flops | bytes accessed | tf_op | source)
XLA Modules:
  0.0 120.1 jit_solution(14495565851677046194)
XLA Ops:
  0.6 2.6 %shard_map.93 = bf16[64,65,128]{2,1,0:T(8,128)(2,1)} custom-call(bf16[16,64,128]{2,1,0:T(8,128)(2,1)} %refs_0_.1, bf16[16,64,128]{2,1,0:T(8,128)(2,1)} %refs_1_.1, bf16[16,64,128]{2,1,0:T(8,128)(2,1)} %refs_2_.1, bf16[16,64,128]{2,1,0:T(8,128)(2,1)} %refs_3_.1, bf16[16,64]{1,0:T(8,128)(2,1)} %refs_4_.1), custom_call_target="tpu_custom_call" | custom-call | tf_op jit(solution)/shard_map/pallas_call | solution.py:400
  3.3 13.2 %all-to-all-start = ((bf16[64,65,128]{2,1,0:T(8,128)(2,1)}), bf16[64,65,128]{2,1,0:T(8,128)(2,1)S(1)}, u32[]{:S(2)}, u32[]{:S(2)}) async-start(bf16[64,65,128]{2,1,0:T(8,128)(2,1)} %shard_map.93), calls=%async_computation | async-start | bytes 2359296 | tf_op jit(solution)/shard_map/all_to_all | solution.py:375
  17.1 30.7 %all-to-all-done.own_ref = bf16[64,65,128]{2,1,0:T(8,128)(2,1)S(1)} async-done(((bf16[64,65,128]{2,1,0:T(8,128)(2,1)}), bf16[64,65,128]{2,1,0:T(8,128)(2,1)S(1)}, u32[]{:S(2)}, u32[]{:S(2)}) %all-to-all-start) | async-done | bytes 1064992 | tf_op jit(solution)/shard_map/all_to_all | solution.py:375
  47.9 2.8 %collective-permute-start.5 = (bf16[64,16,128]{2,1,0:T(8,128)(2,1)S(1)}, bf16[64,16,128]{2,1,0:T(8,128)(2,1)S(1)}, u32[]{:S(2)}, u32[]{:S(2)}) collective-permute-start(bf16[64,16,128]{2,1,0:T(8,128)(2,1)S(1)} %get-tuple-element.42), channel_id=1, source_target_pairs={{0,128},{64,192},{128,0},{192,64},{1,129},{65,193},{129,1},{193,65... | collective-permute-start | bytes 786440 | tf_op jit(solution)/shard_map/ppermute | solution.py:391
  50.7 0.9 collective-permute-start
  51.6 0.6 collective-permute-start.4
  52.2 1.3 %shard_map.94 = (f32[8,1024]{1,0:T(8,128)S(1)}, f32[1024,128]{1,0:T(8,128)S(1)}, f32[1024,128]{1,0:T(8,128)S(1)}) custom-call(s32[1]{0:T(128)S(6)} %copy.10.level_ref, bf16[64,65,128]{2,1,0:T(8,128)(2,1)S(1)} %all-to-all-done.own_ref), custom_call_target="tpu_custom_call" | custom-call | tf_op jit(solution)/shard_map/pallas_call | solution.py:409
  53.6 2.2 %collective-permute-start.3 = (bf16[64,16,128]{2,1,0:T(8,128)(2,1)S(1)}, bf16[64,16,128]{2,1,0:T(8,128)(2,1)S(1)}, u32[]{:S(2)}, u32[]{:S(2)}) collective-permute-start(bf16[64,16,128]{2,1,0:T(8,128)(2,1)S(1)} %get-tuple-element.45), channel_id=1, source_target_pairs={{0,192},{64,0},{128,64},{192,128},{1,193},{65,1},{129,65},{193,129... | collective-permute-start | bytes 786440 | tf_op jit(solution)/shard_map/ppermute | solution.py:391
  55.8 7.4 %collective-permute-done.in3_ref = bf16[64,16,128]{2,1,0:T(8,128)(2,1)S(1)} collective-permute-done((bf16[64,16,128]{2,1,0:T(8,128)(2,1)S(1)}, bf16[64,16,128]{2,1,0:T(8,128)(2,1)S(1)}, u32[]{:S(2)}, u32[]{:S(2)}) %collective-permute-start) | collective-permute-done | bytes 262176 | tf_op jit(solution)/shard_map/ppermute | solution.py:391
  63.1 1.4 %collective-permute-start.1 = (bf16[64,16,128]{2,1,0:T(8,128)(2,1)S(1)}, bf16[64,16,128]{2,1,0:T(8,128)(2,1)S(1)}, u32[]{:S(2)}, u32[]{:S(2)}) collective-permute-start(bf16[64,16,128]{2,1,0:T(8,128)(2,1)S(1)} %get-tuple-element.25), channel_id=1, source_target_pairs={{0,64},{64,128},{128,192},{192,0},{1,65},{65,129},{129,193},{193,1... | collective-permute-start | bytes 786440 | tf_op jit(solution)/shard_map/ppermute | solution.py:391
  64.5 2.7 %shard_map.95 = (f32[8,1024]{1,0:T(8,128)S(1)}, f32[3,1024,1024]{2,1,0:T(8,128)S(1)}) custom-call(s32[1]{0:T(128)} %bitcast.block_ref, bf16[64,65,128]{2,1,0:T(8,128)(2,1)S(1)} %all-to-all-done.own_ref, bf16[64,16,128]{2,1,0:T(8,128)(2,1)S(1)} %collective-permute-done.4.in1_ref, bf16[64,16,128]{2,1,0:T(8,128)(2,1)S(1)} %collective-permute-done.5.in2_ref, ...), custom_call_target="tpu_custom_call" | custom-call | tf_op jit(solution)/shard_map/pallas_call | solution.py:416
  67.3 3.2 %collective-permute-start.8 = (f32[8,1024]{1,0:T(8,128)S(1)}, f32[8,1024]{1,0:T(8,128)S(1)}, u32[]{:S(2)}, u32[]{:S(2)}) collective-permute-start(f32[8,1024]{1,0:T(8,128)S(1)} %get-tuple-element.31.stats_ref), channel_id=1, source_target_pairs={{0,192},{64,0},{128,64},{192,128},{1,193},{65,1},{129,65},{193,129... | collective-permute-start | bytes 98312 | tf_op jit(solution)/shard_map/ppermute | solution.py:379
  70.5 0.7 collective-permute-start.7
  71.1 0.8 collective-permute-start.6
  71.9 2.3 %shard_map.96 = (f32[1024,128]{1,0:T(8,128)S(1)}, f32[1024,128]{1,0:T(8,128)S(1)}, f32[8,128]{1,0:T(8,128)S(1)}) custom-call(bf16[64,65,128]{2,1,0:T(8,128)(2,1)S(1)} %all-to-all-done.own_ref, f32[8,1024]{1,0:T(8,128)S(1)} %get-tuple-element.31.stats_ref), custom_call_target="tpu_custom_call" | custom-call | tf_op jit(solution)/shard_map/pallas_call | solution.py:421
  74.2 0.6 collective-permute-done.8.st3_ref
  75.1 6.7 %shard_map.97 = (f32[1024,128]{1,0:T(8,128)S(1)}, f32[1024,128]{1,0:T(8,128)S(1)}, f32[8,128]{1,0:T(8,128)S(1)}) custom-call(s32[1]{0:T(128)} %bitcast.block_ref, bf16[64,65,128]{2,1,0:T(8,128)(2,1)S(1)} %all-to-all-done.own_ref, bf16[64,16,128]{2,1,0:T(8,128)(2,1)S(1)} %collective-permute-done.1.in1_ref, ...), custom_call_target="tpu_custom_call" | custom-call | tf_op jit(solution)/shard_map/pallas_call | solution.py:426
  81.8 2.5 %collective-permute-start.11 = (f32[8,128]{1,0:T(8,128)S(1)}, f32[8,128]{1,0:T(8,128)S(1)}, u32[]{:S(2)}, u32[]{:S(2)}) collective-permute-start(f32[8,128]{1,0:T(8,128)S(1)} %get-tuple-element.37.sums0_ref), channel_id=1, source_target_pairs={{0,192},{64,0},{128,64},{192,128},{1,193},{65,1},{129,65},{193,129... | collective-permute-start | bytes 12296 | tf_op jit(solution)/shard_map/ppermute | solution.py:379
  84.4 1.0 collective-permute-start.10
  85.7 2.6 %collective-permute-done.10.sums2_ref = f32[8,128]{1,0:T(8,128)S(1)} collective-permute-done((f32[8,128]{1,0:T(8,128)S(1)}, f32[8,128]{1,0:T(8,128)S(1)}, u32[]{:S(2)}, u32[]{:S(2)}) %collective-permute-start.10) | collective-permute-done | bytes 4128 | tf_op jit(solution)/shard_map/ppermute | solution.py:379
  88.3 0.7 collective-permute-done.9.sums1_ref
  89.1 0.9 shard_map.98
  90.0 28.7 %all_to_all.10 = f16[64,33,128]{2,1,0:T(8,128)(2,1)S(1)} all-to-all(f16[64,33,128]{2,1,0:T(8,128)(2,1)S(1)} %convert_element_type.6), channel_id=1, replica_groups=mesh['seq'=4,'head'=64] {'head'}, dimensions={0} | all-to-all | bytes 1081344 | tf_op jit(solution)/shard_map/all_to_all | solution.py:375
  118.9 1.2 %shard_map.99 = (f32[16,64,128]{2,1,0:T(8,128)}, f32[16,64,128]{2,1,0:T(8,128)}, f32[16,64]{1,0:T(8,128)}, f32[1,1]{1,0:T(1,128)}) custom-call(f32[64,33,128]{2,1,0:T(8,128)S(1)} %convert_element_type.7.x_ref), custom_call_target="tpu_custom_call" | custom-call | tf_op jit(solution)/shard_map/pallas_call | solution.py:441
  (15 shorter events, 1.0 us)
Async XLA Ops:
  3.3 44.5 %all-to-all-start = ((bf16[64,65,128]{2,1,0:T(8,128)(2,1)}), bf16[64,65,128]{2,1,0:T(8,128)(2,1)S(1)}, u32[]{:S(2)}, u32[]{:S(2)}) async-start(bf16[64,65,128]{2,1,0:T(8,128)(2,1)} %shard_map.93), calls=%async_computation | async-start | bytes 2359296 | tf_op jit(solution)/shard_map/all_to_all | solution.py:375
  47.9 16.7 %collective-permute-start.5 = (bf16[64,16,128]{2,1,0:T(8,128)(2,1)S(1)}, bf16[64,16,128]{2,1,0:T(8,128)(2,1)S(1)}, u32[]{:S(2)}, u32[]{:S(2)}) collective-permute-start(bf16[64,16,128]{2,1,0:T(8,128)(2,1)S(1)} %get-tuple-element.42), channel_id=1, source_target_pairs={{0,128},{64,192},{128,0},{192,64},{1,129},{65,193},{129,1},{193,65... | collective-permute-start | bytes 786440 | tf_op jit(solution)/shard_map/ppermute | solution.py:391
  50.7 12.4 %collective-permute-start = (bf16[64,16,128]{2,1,0:T(8,128)(2,1)S(1)}, bf16[64,16,128]{2,1,0:T(8,128)(2,1)S(1)}, u32[]{:S(2)}, u32[]{:S(2)}) collective-permute-start(bf16[64,16,128]{2,1,0:T(8,128)(2,1)S(1)} %get-tuple-element.43), channel_id=1, source_target_pairs={{0,192},{64,0},{128,64},{192,128},{1,193},{65,1},{129,65},{193,129... | collective-permute-start | bytes 786440 | tf_op jit(solution)/shard_map/ppermute | solution.py:391
  51.6 13.0 %collective-permute-start.4 = (bf16[64,16,128]{2,1,0:T(8,128)(2,1)S(1)}, bf16[64,16,128]{2,1,0:T(8,128)(2,1)S(1)}, u32[]{:S(2)}, u32[]{:S(2)}) collective-permute-start(bf16[64,16,128]{2,1,0:T(8,128)(2,1)S(1)} %get-tuple-element.44), channel_id=1, source_target_pairs={{0,64},{64,128},{128,192},{192,0},{1,65},{65,129},{129,193},{193,1... | collective-permute-start | bytes 786440 | tf_op jit(solution)/shard_map/ppermute | solution.py:391
  53.6 17.6 %collective-permute-start.3 = (bf16[64,16,128]{2,1,0:T(8,128)(2,1)S(1)}, bf16[64,16,128]{2,1,0:T(8,128)(2,1)S(1)}, u32[]{:S(2)}, u32[]{:S(2)}) collective-permute-start(bf16[64,16,128]{2,1,0:T(8,128)(2,1)S(1)} %get-tuple-element.45), channel_id=1, source_target_pairs={{0,192},{64,0},{128,64},{192,128},{1,193},{65,1},{129,65},{193,129... | collective-permute-start | bytes 786440 | tf_op jit(solution)/shard_map/ppermute | solution.py:391
  55.7 18.4 %collective-permute-start.2 = (bf16[64,16,128]{2,1,0:T(8,128)(2,1)S(1)}, bf16[64,16,128]{2,1,0:T(8,128)(2,1)S(1)}, u32[]{:S(2)}, u32[]{:S(2)}) collective-permute-start(bf16[64,16,128]{2,1,0:T(8,128)(2,1)S(1)} %get-tuple-element.47), channel_id=1, source_target_pairs={{0,128},{64,192},{128,0},{192,64},{1,129},{65,193},{129,1},{193,65... | collective-permute-start | bytes 786440 | tf_op jit(solution)/shard_map/ppermute | solution.py:391
  63.1 12.0 %collective-permute-start.1 = (bf16[64,16,128]{2,1,0:T(8,128)(2,1)S(1)}, bf16[64,16,128]{2,1,0:T(8,128)(2,1)S(1)}, u32[]{:S(2)}, u32[]{:S(2)}) collective-permute-start(bf16[64,16,128]{2,1,0:T(8,128)(2,1)S(1)} %get-tuple-element.25), channel_id=1, source_target_pairs={{0,64},{64,128},{128,192},{192,0},{1,65},{65,129},{129,193},{193,1... | collective-permute-start | bytes 786440 | tf_op jit(solution)/shard_map/ppermute | solution.py:391
  67.3 7.5 %collective-permute-start.8 = (f32[8,1024]{1,0:T(8,128)S(1)}, f32[8,1024]{1,0:T(8,128)S(1)}, u32[]{:S(2)}, u32[]{:S(2)}) collective-permute-start(f32[8,1024]{1,0:T(8,128)S(1)} %get-tuple-element.31.stats_ref), channel_id=1, source_target_pairs={{0,192},{64,0},{128,64},{192,128},{1,193},{65,1},{129,65},{193,129... | collective-permute-start | bytes 98312 | tf_op jit(solution)/shard_map/ppermute | solution.py:379
  70.5 4.3 %collective-permute-start.7 = (f32[8,1024]{1,0:T(8,128)S(1)}, f32[8,1024]{1,0:T(8,128)S(1)}, u32[]{:S(2)}, u32[]{:S(2)}) collective-permute-start(f32[8,1024]{1,0:T(8,128)S(1)} %get-tuple-element.31.stats_ref), channel_id=1, source_target_pairs={{0,128},{64,192},{128,0},{192,64},{1,129},{65,193},{129,1},{193,65... | collective-permute-start | bytes 98312 | tf_op jit(solution)/shard_map/ppermute | solution.py:379
  71.1 4.0 %collective-permute-start.6 = (f32[8,1024]{1,0:T(8,128)S(1)}, f32[8,1024]{1,0:T(8,128)S(1)}, u32[]{:S(2)}, u32[]{:S(2)}) collective-permute-start(f32[8,1024]{1,0:T(8,128)S(1)} %get-tuple-element.31.stats_ref), channel_id=1, source_target_pairs={{0,64},{64,128},{128,192},{192,0},{1,65},{65,129},{129,193},{193,1... | collective-permute-start | bytes 98312 | tf_op jit(solution)/shard_map/ppermute | solution.py:379
  81.8 3.9 %collective-permute-start.11 = (f32[8,128]{1,0:T(8,128)S(1)}, f32[8,128]{1,0:T(8,128)S(1)}, u32[]{:S(2)}, u32[]{:S(2)}) collective-permute-start(f32[8,128]{1,0:T(8,128)S(1)} %get-tuple-element.37.sums0_ref), channel_id=1, source_target_pairs={{0,192},{64,0},{128,64},{192,128},{1,193},{65,1},{129,65},{193,129... | collective-permute-start | bytes 12296 | tf_op jit(solution)/shard_map/ppermute | solution.py:379
  84.4 4.0 %collective-permute-start.10 = (f32[8,128]{1,0:T(8,128)S(1)}, f32[8,128]{1,0:T(8,128)S(1)}, u32[]{:S(2)}, u32[]{:S(2)}) collective-permute-start(f32[8,128]{1,0:T(8,128)S(1)} %get-tuple-element.37.sums0_ref), channel_id=1, source_target_pairs={{0,128},{64,192},{128,0},{192,64},{1,129},{65,193},{129,1},{193,65... | collective-permute-start | bytes 12296 | tf_op jit(solution)/shard_map/ppermute | solution.py:379
  85.4 3.7 %collective-permute-start.9 = (f32[8,128]{1,0:T(8,128)S(1)}, f32[8,128]{1,0:T(8,128)S(1)}, u32[]{:S(2)}, u32[]{:S(2)}) collective-permute-start(f32[8,128]{1,0:T(8,128)S(1)} %get-tuple-element.37.sums0_ref), channel_id=1, source_target_pairs={{0,64},{64,128},{128,192},{192,0},{1,65},{65,129},{129,193},{193,1... | collective-permute-start | bytes 12296 | tf_op jit(solution)/shard_map/ppermute | solution.py:379

commit v6 on v5

--- a/solution.py
+++ b/solution.py
@@ -272,11 +272,7 @@
     out_ref[...] = jnp.broadcast_to(sums, out_ref.shape)
 
 
-def finish_kernel(
-    n, beta, seq_len, block_ref, level_ref, own_ref, gc_ref, gb_ref,
-    sums0_ref, sums1_ref, sums2_ref, sums3_ref, out_ref,
-):
-    block = block_ref[0]
+def prepare_kernel(n, beta, own_ref, gc_ref, gb_ref, out_ref, tail_ref, exp_ref):
     heads, _, width = own_ref.shape
     rows = heads * n
     gb = gb_ref[...]
@@ -296,6 +292,21 @@
     down = lax.broadcasted_iota(jnp.int32, (heads, heads), 0)
     right = lax.broadcasted_iota(jnp.int32, (heads, heads), 1)
     behind = dot_full(jnp.where(right > down, 1.0, 0.0).astype(F32), whole)
+    tail_ref[...] = inside + behind
+    eb, ec = exponent_of(gb), exponent_of(gc)
+    out_ref[:, 0:n, :] = (gb * jnp.exp2(14.0 - eb)).reshape(heads, n, width)
+    out_ref[:, n:2 * n, :] = (gc * jnp.exp2(14.0 - ec)).reshape(heads, n, width)
+    place = lax.broadcasted_iota(jnp.int32, exp_ref.shape, 0)
+    exp_ref[...] = jnp.where(place == 0, eb, ec)
+
+
+def finish_kernel(
+    n, seq_len, block_ref, level_ref, grads_ref, tail_ref, exp_ref,
+    sums0_ref, sums1_ref, sums2_ref, sums3_ref, out_ref,
+):
+    block = block_ref[0]
+    heads = out_ref.shape[0]
+    out_ref[:, 0:2 * n, :] = grads_ref[...]
     lane1 = lax.broadcasted_iota(jnp.int32, (1, 128), 1)
     sums = (sums0_ref[0:1, :] + sums1_ref[0:1, :]) + (sums2_ref[0:1, :] + sums3_ref[0:1, :])
     after = jnp.sum(
@@ -305,13 +316,10 @@
     norm = jnp.sqrt(error_sq + 1e-06)
     factor = seq_len / norm
     rate = jnp.exp2(-0.5 * jnp.full((1, 1), level_ref[0], jnp.int32).astype(F32))
-    step = (inside + behind + after) * (-(rate * factor))
+    step = (tail_ref[...] + after) * (-(rate * factor))
     lane = lax.broadcasted_iota(jnp.int32, (heads, 128), 1)
-    gb = gb * (factor * beta)
-    gc = gc * (factor * beta)
-    eb, ec, es, en = exponent_of(gb), exponent_of(gc), exponent_of(step), exponent_of(norm)
-    out_ref[:, 0:n, :] = (gb * jnp.exp2(14.0 - eb)).reshape(heads, n, width)
-    out_ref[:, n:2 * n, :] = (gc * jnp.exp2(14.0 - ec)).reshape(heads, n, width)
+    eb, ec = exp_ref[0:1, 0:1], exp_ref[1:2, 0:1]
+    es, en = exponent_of(step), exponent_of(norm)
     high, low = split_scaled(step, es)
     norm_high, norm_low = split_scaled(norm, en)
     last = jnp.where(lane < n, high, low)
@@ -320,7 +328,7 @@
     out_ref[:, 2 * n:2 * n + 1, :] = last.reshape(heads, 1, 128)
 
 
-def unpack_kernel(x_ref, gb_ref, gc_ref, step_ref, loss_ref):
+def unpack_kernel(beta, seq_len, x_ref, gb_ref, gc_ref, step_ref, loss_ref):
     heads = x_ref.shape[0]
     n = gb_ref.shape[0]
     last = x_ref[:, 2 * n:2 * n + 1, :].reshape(heads, 128)
@@ -331,6 +339,7 @@
 
     scale_b, scale_c, scale_s = (jnp.exp2(pick(at) - 14.0) for at in range(3))
     norm = (pick(3) + pick(4)) * jnp.exp2(pick(5) - 14.0)
+    scale_b, scale_c = (x * (seq_len / norm * beta) for x in (scale_b, scale_c))
     gb_ref[...] = jnp.swapaxes(x_ref[:, 0:n, :] * scale_b[:, :, None], 0, 1)
     gc_ref[...] = jnp.swapaxes(x_ref[:, n:2 * n, :] * scale_c[:, :, None], 0, 1)
     step = jnp.transpose(last * scale_s)
@@ -433,13 +442,17 @@
         1, 13,
     )(where, own, *bc_from, scores, stats, *stats_from, gc, gb, sq)
     sums_from = [held_near(x) for x in around(sums)]
+    packed, tail, exps = call(
+        functools.partial(prepare_kernel, n, beta),
+        [near(heads, 2 * n, width), near(heads, 128), near(8, 128)], [], 0, 3,
+    )(own, gc, gb)
     packed = call(
-        functools.partial(finish_kernel, n, beta, float(seq_len)),
+        functools.partial(finish_kernel, n, float(seq_len)),
         near(heads, 2 * n + 1, width), [], 2, 9,
-    )(where, rate_level, own, gc, gb, sums, *sums_from)
+    )(where, rate_level, packed, tail, exps, sums, *sums_from)
     back = to_heads(packed.astype(F16)).astype(F32)
     grad_b, grad_c, grad_step, loss = pl.pallas_call(
-        unpack_kernel,
+        functools.partial(unpack_kernel, beta, float(seq_len)),
         out_shape=[
             shape(n, heads, width), shape(n, heads, width), shape(n, heads), shape(1, 1),
         ],

time: 120 us -> 120 us (level)
  transfers between devices with their start and end apart: 13 -> 13, of which waited for: 6 -> 6; matrix products, arithmetic and copies ran while one was open for 0% -> 0% of each run, Pallas kernels for 5% -> 6%
where the time goes in v6:
time: 120 us; the launch traced here: 119 us
  waiting for transfers between devices  41.6 us (35%)
  starting transfers between devices  29.5 us (25%)
  blocking collectives  28.7 us (24%)
  Pallas kernels  17.8 us (15%)
  between operations  1.4 us (1%)
    all_to_all x1, waiting for transfers between devices, to_heads(): return lax.all_to_all(x, 'head', split_axis=0, concat_axis=0, tiled=True)  30.7 us
    all_to_all x1, blocking collectives, to_heads(): return lax.all_to_all(x, 'head', split_axis=0, concat_axis=0, tiled=True)  28.7 us
    all_to_all x1, starting transfers between devices, to_heads(): return lax.all_to_all(x, 'head', split_axis=0, concat_axis=0, tiled=True)  13.2 us
    ppermute x6, starting transfers between devices, around(): lax.ppermute(x, 'seq', [(i, (i + d) % blocks) for i in range(blocks)])  8.52 us
    ppermute x6, starting transfers between devices, exchange(): lax.ppermute(sent, 'seq', [(i, (i + d) % blocks) for i in range(blocks)])  7.87 us
    ppermute x6, waiting for transfers between devices, exchange(): lax.ppermute(sent, 'seq', [(i, (i + d) % blocks) for i in range(blocks)])  7.39 us
    pallas_call x1, Pallas kernels, per_device(): call(functools.partial(blocks_kernel, n, beta), [near(rows, width), near(...  6.71 us
    ppermute x6, waiting for transfers between devices, around(): lax.ppermute(x, 'seq', [(i, (i + d) % blocks) for i in range(blocks)])  3.53 us
  transfers between devices with their start and end apart: 13, of which 6 were waited for; matrix products, arithmetic and copies ran while one was open for 0% of the time, Pallas kernels for 6%

profile of v6, /device:TPU:1, one launch (start us, length us, event | category | flops | bytes accessed | tf_op | source)
XLA Modules:
  0.0 119.5 jit_solution(15573528148598576239)
XLA Ops:
  0.6 2.6 %shard_map.93 = bf16[64,65,128]{2,1,0:T(8,128)(2,1)} custom-call(bf16[16,64,128]{2,1,0:T(8,128)(2,1)} %refs_0_.1, bf16[16,64,128]{2,1,0:T(8,128)(2,1)} %refs_1_.1, bf16[16,64,128]{2,1,0:T(8,128)(2,1)} %refs_2_.1, bf16[16,64,128]{2,1,0:T(8,128)(2,1)} %refs_3_.1, bf16[16,64]{1,0:T(8,128)(2,1)} %refs_4_.1), custom_call_target="tpu_custom_call" | custom-call | tf_op jit(solution)/shard_map/pallas_call | solution.py:409
  3.3 13.2 %all-to-all-start = ((bf16[64,65,128]{2,1,0:T(8,128)(2,1)}), bf16[64,65,128]{2,1,0:T(8,128)(2,1)S(1)}, u32[]{:S(2)}, u32[]{:S(2)}) async-start(bf16[64,65,128]{2,1,0:T(8,128)(2,1)} %shard_map.93), calls=%async_computation | async-start | bytes 2359296 | tf_op jit(solution)/shard_map/all_to_all | solution.py:384
  17.1 30.7 %all-to-all-done.own_ref = bf16[64,65,128]{2,1,0:T(8,128)(2,1)S(1)} async-done(((bf16[64,65,128]{2,1,0:T(8,128)(2,1)}), bf16[64,65,128]{2,1,0:T(8,128)(2,1)S(1)}, u32[]{:S(2)}, u32[]{:S(2)}) %all-to-all-start) | async-done | bytes 1064992 | tf_op jit(solution)/shard_map/all_to_all | solution.py:384
  47.9 2.8 %collective-permute-start.5 = (bf16[64,16,128]{2,1,0:T(8,128)(2,1)S(1)}, bf16[64,16,128]{2,1,0:T(8,128)(2,1)S(1)}, u32[]{:S(2)}, u32[]{:S(2)}) collective-permute-start(bf16[64,16,128]{2,1,0:T(8,128)(2,1)S(1)} %get-tuple-element.48), channel_id=1, source_target_pairs={{0,128},{64,192},{128,0},{192,64},{1,129},{65,193},{129,1},{193,65... | collective-permute-start | bytes 786440 | tf_op jit(solution)/shard_map/ppermute | solution.py:400
  50.7 0.9 collective-permute-start
  51.6 0.6 collective-permute-start.4
  52.2 1.3 %shard_map.94 = (f32[8,1024]{1,0:T(8,128)S(1)}, f32[1024,128]{1,0:T(8,128)S(1)}, f32[1024,128]{1,0:T(8,128)S(1)}) custom-call(s32[1]{0:T(128)S(6)} %copy.10.level_ref, bf16[64,65,128]{2,1,0:T(8,128)(2,1)S(1)} %all-to-all-done.own_ref), custom_call_target="tpu_custom_call" | custom-call | tf_op jit(solution)/shard_map/pallas_call | solution.py:418
  53.6 2.1 %collective-permute-start.3 = (bf16[64,16,128]{2,1,0:T(8,128)(2,1)S(1)}, bf16[64,16,128]{2,1,0:T(8,128)(2,1)S(1)}, u32[]{:S(2)}, u32[]{:S(2)}) collective-permute-start(bf16[64,16,128]{2,1,0:T(8,128)(2,1)S(1)} %get-tuple-element.51), channel_id=1, source_target_pairs={{0,192},{64,0},{128,64},{192,128},{1,193},{65,1},{129,65},{193,129... | collective-permute-start | bytes 786440 | tf_op jit(solution)/shard_map/ppermute | solution.py:400
  55.8 7.4 %collective-permute-done.in3_ref = bf16[64,16,128]{2,1,0:T(8,128)(2,1)S(1)} collective-permute-done((bf16[64,16,128]{2,1,0:T(8,128)(2,1)S(1)}, bf16[64,16,128]{2,1,0:T(8,128)(2,1)S(1)}, u32[]{:S(2)}, u32[]{:S(2)}) %collective-permute-start) | collective-permute-done | bytes 262176 | tf_op jit(solution)/shard_map/ppermute | solution.py:400
  63.1 1.4 %collective-permute-start.1 = (bf16[64,16,128]{2,1,0:T(8,128)(2,1)S(1)}, bf16[64,16,128]{2,1,0:T(8,128)(2,1)S(1)}, u32[]{:S(2)}, u32[]{:S(2)}) collective-permute-start(bf16[64,16,128]{2,1,0:T(8,128)(2,1)S(1)} %get-tuple-element.28), channel_id=1, source_target_pairs={{0,64},{64,128},{128,192},{192,0},{1,65},{65,129},{129,193},{193,1... | collective-permute-start | bytes 786440 | tf_op jit(solution)/shard_map/ppermute | solution.py:400
  64.5 2.7 %shard_map.95 = (f32[8,1024]{1,0:T(8,128)S(1)}, f32[3,1024,1024]{2,1,0:T(8,128)S(1)}) custom-call(s32[1]{0:T(128)} %bitcast.block_ref, bf16[64,65,128]{2,1,0:T(8,128)(2,1)S(1)} %all-to-all-done.own_ref, bf16[64,16,128]{2,1,0:T(8,128)(2,1)S(1)} %collective-permute-done.4.in1_ref, bf16[64,16,128]{2,1,0:T(8,128)(2,1)S(1)} %collective-permute-done.5.in2_ref, ...), custom_call_target="tpu_custom_call" | custom-call | tf_op jit(solution)/shard_map/pallas_call | solution.py:425
  67.3 3.2 %collective-permute-start.8 = (f32[8,1024]{1,0:T(8,128)S(1)}, f32[8,1024]{1,0:T(8,128)S(1)}, u32[]{:S(2)}, u32[]{:S(2)}) collective-permute-start(f32[8,1024]{1,0:T(8,128)S(1)} %get-tuple-element.34.stats_ref), channel_id=1, source_target_pairs={{0,192},{64,0},{128,64},{192,128},{1,193},{65,1},{129,65},{193,129... | collective-permute-start | bytes 98312 | tf_op jit(solution)/shard_map/ppermute | solution.py:388
  70.5 0.6 collective-permute-start.7
  71.1 0.8 collective-permute-start.6
  71.9 2.3 %shard_map.96 = (f32[1024,128]{1,0:T(8,128)S(1)}, f32[1024,128]{1,0:T(8,128)S(1)}, f32[8,128]{1,0:T(8,128)S(1)}) custom-call(bf16[64,65,128]{2,1,0:T(8,128)(2,1)S(1)} %all-to-all-done.own_ref, f32[8,1024]{1,0:T(8,128)S(1)} %get-tuple-element.34.stats_ref), custom_call_target="tpu_custom_call" | custom-call | tf_op jit(solution)/shard_map/pallas_call | solution.py:430
  74.2 0.6 collective-permute-done.8.st3_ref
  75.1 6.7 %shard_map.97 = (f32[1024,128]{1,0:T(8,128)S(1)}, f32[1024,128]{1,0:T(8,128)S(1)}, f32[8,128]{1,0:T(8,128)S(1)}) custom-call(s32[1]{0:T(128)} %bitcast.block_ref, bf16[64,65,128]{2,1,0:T(8,128)(2,1)S(1)} %all-to-all-done.own_ref, bf16[64,16,128]{2,1,0:T(8,128)(2,1)S(1)} %collective-permute-done.1.in1_ref, ...), custom_call_target="tpu_custom_call" | custom-call | tf_op jit(solution)/shard_map/pallas_call | solution.py:435
  81.8 2.5 %collective-permute-start.11 = (f32[8,128]{1,0:T(8,128)S(1)}, f32[8,128]{1,0:T(8,128)S(1)}, u32[]{:S(2)}, u32[]{:S(2)}) collective-permute-start(f32[8,128]{1,0:T(8,128)S(1)} %get-tuple-element.43.sums0_ref), channel_id=1, source_target_pairs={{0,192},{64,0},{128,64},{192,128},{1,193},{65,1},{129,65},{193,129... | collective-permute-start | bytes 12296 | tf_op jit(solution)/shard_map/ppermute | solution.py:388
  84.4 1.0 collective-permute-start.10
  85.7 0.7 shard_map.98
  86.5 1.9 %collective-permute-done.10.sums2_ref = f32[8,128]{1,0:T(8,128)S(1)} collective-permute-done((f32[8,128]{1,0:T(8,128)S(1)}, f32[8,128]{1,0:T(8,128)S(1)}, u32[]{:S(2)}, u32[]{:S(2)}) %collective-permute-start.10) | collective-permute-done | bytes 4128 | tf_op jit(solution)/shard_map/ppermute | solution.py:388
  88.3 0.7 collective-permute-done.9.sums1_ref
  89.4 28.7 %all_to_all.10 = f16[64,33,128]{2,1,0:T(8,128)(2,1)S(1)} all-to-all(f16[64,33,128]{2,1,0:T(8,128)(2,1)S(1)} %convert_element_type.6), channel_id=1, replica_groups=mesh['seq'=4,'head'=64] {'head'}, dimensions={0} | all-to-all | bytes 1081344 | tf_op jit(solution)/shard_map/all_to_all | solution.py:384
  118.2 1.2 %shard_map.100 = (f32[16,64,128]{2,1,0:T(8,128)}, f32[16,64,128]{2,1,0:T(8,128)}, f32[16,64]{1,0:T(8,128)}, f32[1,1]{1,0:T(1,128)}) custom-call(f32[64,33,128]{2,1,0:T(8,128)S(1)} %convert_element_type.7.x_ref), custom_call_target="tpu_custom_call" | custom-call | tf_op jit(solution)/shard_map/pallas_call | solution.py:454
  (16 shorter events, 1.2 us)
Async XLA Ops:
  3.3 44.5 %all-to-all-start = ((bf16[64,65,128]{2,1,0:T(8,128)(2,1)}), bf16[64,65,128]{2,1,0:T(8,128)(2,1)S(1)}, u32[]{:S(2)}, u32[]{:S(2)}) async-start(bf16[64,65,128]{2,1,0:T(8,128)(2,1)} %shard_map.93), calls=%async_computation | async-start | bytes 2359296 | tf_op jit(solution)/shard_map/all_to_all | solution.py:384
  47.9 16.7 %collective-permute-start.5 = (bf16[64,16,128]{2,1,0:T(8,128)(2,1)S(1)}, bf16[64,16,128]{2,1,0:T(8,128)(2,1)S(1)}, u32[]{:S(2)}, u32[]{:S(2)}) collective-permute-start(bf16[64,16,128]{2,1,0:T(8,128)(2,1)S(1)} %get-tuple-element.48), channel_id=1, source_target_pairs={{0,128},{64,192},{128,0},{192,64},{1,129},{65,193},{129,1},{193,65... | collective-permute-start | bytes 786440 | tf_op jit(solution)/shard_map/ppermute | solution.py:400
  50.7 12.4 %collective-permute-start = (bf16[64,16,128]{2,1,0:T(8,128)(2,1)S(1)}, bf16[64,16,128]{2,1,0:T(8,128)(2,1)S(1)}, u32[]{:S(2)}, u32[]{:S(2)}) collective-permute-start(bf16[64,16,128]{2,1,0:T(8,128)(2,1)S(1)} %get-tuple-element.49), channel_id=1, source_target_pairs={{0,192},{64,0},{128,64},{192,128},{1,193},{65,1},{129,65},{193,129... | collective-permute-start | bytes 786440 | tf_op jit(solution)/shard_map/ppermute | solution.py:400
  51.6 13.0 %collective-permute-start.4 = (bf16[64,16,128]{2,1,0:T(8,128)(2,1)S(1)}, bf16[64,16,128]{2,1,0:T(8,128)(2,1)S(1)}, u32[]{:S(2)}, u32[]{:S(2)}) collective-permute-start(bf16[64,16,128]{2,1,0:T(8,128)(2,1)S(1)} %get-tuple-element.50), channel_id=1, source_target_pairs={{0,64},{64,128},{128,192},{192,0},{1,65},{65,129},{129,193},{193,1... | collective-permute-start | bytes 786440 | tf_op jit(solution)/shard_map/ppermute | solution.py:400
  53.6 17.5 %collective-permute-start.3 = (bf16[64,16,128]{2,1,0:T(8,128)(2,1)S(1)}, bf16[64,16,128]{2,1,0:T(8,128)(2,1)S(1)}, u32[]{:S(2)}, u32[]{:S(2)}) collective-permute-start(bf16[64,16,128]{2,1,0:T(8,128)(2,1)S(1)} %get-tuple-element.51), channel_id=1, source_target_pairs={{0,192},{64,0},{128,64},{192,128},{1,193},{65,1},{129,65},{193,129... | collective-permute-start | bytes 786440 | tf_op jit(solution)/shard_map/ppermute | solution.py:400
  55.7 18.4 %collective-permute-start.2 = (bf16[64,16,128]{2,1,0:T(8,128)(2,1)S(1)}, bf16[64,16,128]{2,1,0:T(8,128)(2,1)S(1)}, u32[]{:S(2)}, u32[]{:S(2)}) collective-permute-start(bf16[64,16,128]{2,1,0:T(8,128)(2,1)S(1)} %get-tuple-element.53), channel_id=1, source_target_pairs={{0,128},{64,192},{128,0},{192,64},{1,129},{65,193},{129,1},{193,65... | collective-permute-start | bytes 786440 | tf_op jit(solution)/shard_map/ppermute | solution.py:400
  63.1 12.0 %collective-permute-start.1 = (bf16[64,16,128]{2,1,0:T(8,128)(2,1)S(1)}, bf16[64,16,128]{2,1,0:T(8,128)(2,1)S(1)}, u32[]{:S(2)}, u32[]{:S(2)}) collective-permute-start(bf16[64,16,128]{2,1,0:T(8,128)(2,1)S(1)} %get-tuple-element.28), channel_id=1, source_target_pairs={{0,64},{64,128},{128,192},{192,0},{1,65},{65,129},{129,193},{193,1... | collective-permute-start | bytes 786440 | tf_op jit(solution)/shard_map/ppermute | solution.py:400
  67.3 7.5 %collective-permute-start.8 = (f32[8,1024]{1,0:T(8,128)S(1)}, f32[8,1024]{1,0:T(8,128)S(1)}, u32[]{:S(2)}, u32[]{:S(2)}) collective-permute-start(f32[8,1024]{1,0:T(8,128)S(1)} %get-tuple-element.34.stats_ref), channel_id=1, source_target_pairs={{0,192},{64,0},{128,64},{192,128},{1,193},{65,1},{129,65},{193,129... | collective-permute-start | bytes 98312 | tf_op jit(solution)/shard_map/ppermute | solution.py:388
  70.5 4.3 %collective-permute-start.7 = (f32[8,1024]{1,0:T(8,128)S(1)}, f32[8,1024]{1,0:T(8,128)S(1)}, u32[]{:S(2)}, u32[]{:S(2)}) collective-permute-start(f32[8,1024]{1,0:T(8,128)S(1)} %get-tuple-element.34.stats_ref), channel_id=1, source_target_pairs={{0,128},{64,192},{128,0},{192,64},{1,129},{65,193},{129,1},{193,65... | collective-permute-start | bytes 98312 | tf_op jit(solution)/shard_map/ppermute | solution.py:388
  71.1 4.0 %collective-permute-start.6 = (f32[8,1024]{1,0:T(8,128)S(1)}, f32[8,1024]{1,0:T(8,128)S(1)}, u32[]{:S(2)}, u32[]{:S(2)}) collective-permute-start(f32[8,1024]{1,0:T(8,128)S(1)} %get-tuple-element.34.stats_ref), channel_id=1, source_target_pairs={{0,64},{64,128},{128,192},{192,0},{1,65},{65,129},{129,193},{193,1... | collective-permute-start | bytes 98312 | tf_op jit(solution)/shard_map/ppermute | solution.py:388
  81.8 4.6 %collective-permute-start.11 = (f32[8,128]{1,0:T(8,128)S(1)}, f32[8,128]{1,0:T(8,128)S(1)}, u32[]{:S(2)}, u32[]{:S(2)}) collective-permute-start(f32[8,128]{1,0:T(8,128)S(1)} %get-tuple-element.43.sums0_ref), channel_id=1, source_target_pairs={{0,192},{64,0},{128,64},{192,128},{1,193},{65,1},{129,65},{193,129... | collective-permute-start | bytes 12296 | tf_op jit(solution)/shard_map/ppermute | solution.py:388
  84.4 4.0 %collective-permute-start.10 = (f32[8,128]{1,0:T(8,128)S(1)}, f32[8,128]{1,0:T(8,128)S(1)}, u32[]{:S(2)}, u32[]{:S(2)}) collective-permute-start(f32[8,128]{1,0:T(8,128)S(1)} %get-tuple-element.43.sums0_ref), channel_id=1, source_target_pairs={{0,128},{64,192},{128,0},{192,64},{1,129},{65,193},{129,1},{193,65... | collective-permute-start | bytes 12296 | tf_op jit(solution)/shard_map/ppermute | solution.py:388
  85.4 3.7 %collective-permute-start.9 = (f32[8,128]{1,0:T(8,128)S(1)}, f32[8,128]{1,0:T(8,128)S(1)}, u32[]{:S(2)}, u32[]{:S(2)}) collective-permute-start(f32[8,128]{1,0:T(8,128)S(1)} %get-tuple-element.43.sums0_ref), channel_id=1, source_target_pairs={{0,64},{64,128},{128,192},{192,0},{1,65},{65,129},{129,193},{193,1... | collective-permute-start | bytes 12296 | tf_op jit(solution)/shard_map/ppermute | solution.py:388

commit v7 on v6

--- a/solution.py
+++ b/solution.py
@@ -14,7 +14,7 @@
 LOG2E = math.log2(math.e)
 TILE = 256
 TALL = 512
-WIDE = 512
+WIDE = 1024
 OWN = 512
 LOWEST = -1e30
 VMEM_BYTES = 32 * 1024 * 1024
@@ -143,9 +143,11 @@
 
     @pl.loop(1, block + 1)
     def _(d):
-        s = dot_nt(q_s[...], k_s[d]) * scale
-        score_ref[d - 1, :, :] = s
-        add_stats(s, max_s, sum_s, slice(None), False)
+        for at in range(0, q_s.shape[0], TALL):
+            ti = slice(at, at + TALL)
+            s = dot_nt(q_s[ti, :], k_s[d]) * scale
+            score_ref[d - 1, ti, :] = s
+            add_stats(s, max_s, sum_s, ti, False)
 
     @pl.loop(block + 1, 4)
     def _(d):

time: 120 us -> 120 us (level)
  no operation moved by 1% of the time
where the time goes in v7:
time: 120 us; the launch traced here: 119 us
  waiting for transfers between devices  41.6 us (35%)
  starting transfers between devices  29.6 us (25%)
  blocking collectives  28.6 us (24%)
  Pallas kernels  17.8 us (15%)
  between operations  1.4 us (1%)
    all_to_all x1, waiting for transfers between devices, to_heads(): return lax.all_to_all(x, 'head', split_axis=0, concat_axis=0, tiled=True)  30.7 us
    all_to_all x1, blocking collectives, to_heads(): return lax.all_to_all(x, 'head', split_axis=0, concat_axis=0, tiled=True)  28.6 us
    all_to_all x1, starting transfers between devices, to_heads(): return lax.all_to_all(x, 'head', split_axis=0, concat_axis=0, tiled=True)  13.2 us
    ppermute x6, starting transfers between devices, around(): lax.ppermute(x, 'seq', [(i, (i + d) % blocks) for i in range(blocks)])  8.53 us
    ppermute x6, starting transfers between devices, exchange(): lax.ppermute(sent, 'seq', [(i, (i + d) % blocks) for i in range(blocks)])  7.87 us
    ppermute x6, waiting for transfers between devices, exchange(): lax.ppermute(sent, 'seq', [(i, (i + d) % blocks) for i in range(blocks)])  7.39 us
    pallas_call x1, Pallas kernels, per_device(): call(functools.partial(blocks_kernel, n, beta), [near(rows, width), near(...  6.63 us
    ppermute x6, waiting for transfers between devices, around(): lax.ppermute(x, 'seq', [(i, (i + d) % blocks) for i in range(blocks)])  3.56 us
  transfers between devices with their start and end apart: 13, of which 6 were waited for; matrix products, arithmetic and copies ran while one was open for 0% of the time, Pallas kernels for 6%

profile of v7, /device:TPU:1, one launch (start us, length us, event | category | flops | bytes accessed | tf_op | source)
XLA Modules:
  0.0 119.3 jit_solution(3031001854884732232)
XLA Ops:
  0.6 2.6 %shard_map.93 = bf16[64,65,128]{2,1,0:T(8,128)(2,1)} custom-call(bf16[16,64,128]{2,1,0:T(8,128)(2,1)} %refs_0_.1, bf16[16,64,128]{2,1,0:T(8,128)(2,1)} %refs_1_.1, bf16[16,64,128]{2,1,0:T(8,128)(2,1)} %refs_2_.1, bf16[16,64,128]{2,1,0:T(8,128)(2,1)} %refs_3_.1, bf16[16,64]{1,0:T(8,128)(2,1)} %refs_4_.1), custom_call_target="tpu_custom_call" | custom-call | tf_op jit(solution)/shard_map/pallas_call | solution.py:411
  3.3 13.2 %all-to-all-start = ((bf16[64,65,128]{2,1,0:T(8,128)(2,1)}), bf16[64,65,128]{2,1,0:T(8,128)(2,1)S(1)}, u32[]{:S(2)}, u32[]{:S(2)}) async-start(bf16[64,65,128]{2,1,0:T(8,128)(2,1)} %shard_map.93), calls=%async_computation | async-start | bytes 2359296 | tf_op jit(solution)/shard_map/all_to_all | solution.py:386
  17.1 30.7 %all-to-all-done.own_ref = bf16[64,65,128]{2,1,0:T(8,128)(2,1)S(1)} async-done(((bf16[64,65,128]{2,1,0:T(8,128)(2,1)}), bf16[64,65,128]{2,1,0:T(8,128)(2,1)S(1)}, u32[]{:S(2)}, u32[]{:S(2)}) %all-to-all-start) | async-done | bytes 1064992 | tf_op jit(solution)/shard_map/all_to_all | solution.py:386
  47.9 2.8 %collective-permute-start.5 = (bf16[64,16,128]{2,1,0:T(8,128)(2,1)S(1)}, bf16[64,16,128]{2,1,0:T(8,128)(2,1)S(1)}, u32[]{:S(2)}, u32[]{:S(2)}) collective-permute-start(bf16[64,16,128]{2,1,0:T(8,128)(2,1)S(1)} %get-tuple-element.48), channel_id=1, source_target_pairs={{0,128},{64,192},{128,0},{192,64},{1,129},{65,193},{129,1},{193,65... | collective-permute-start | bytes 786440 | tf_op jit(solution)/shard_map/ppermute | solution.py:402
  50.7 0.9 collective-permute-start
  51.6 0.6 collective-permute-start.4
  52.2 1.3 %shard_map.94 = (f32[8,1024]{1,0:T(8,128)S(1)}, f32[1024,128]{1,0:T(8,128)S(1)}, f32[1024,128]{1,0:T(8,128)S(1)}) custom-call(s32[1]{0:T(128)S(6)} %copy.10.level_ref, bf16[64,65,128]{2,1,0:T(8,128)(2,1)S(1)} %all-to-all-done.own_ref), custom_call_target="tpu_custom_call" | custom-call | tf_op jit(solution)/shard_map/pallas_call | solution.py:420
  53.6 2.1 %collective-permute-start.3 = (bf16[64,16,128]{2,1,0:T(8,128)(2,1)S(1)}, bf16[64,16,128]{2,1,0:T(8,128)(2,1)S(1)}, u32[]{:S(2)}, u32[]{:S(2)}) collective-permute-start(bf16[64,16,128]{2,1,0:T(8,128)(2,1)S(1)} %get-tuple-element.51), channel_id=1, source_target_pairs={{0,192},{64,0},{128,64},{192,128},{1,193},{65,1},{129,65},{193,129... | collective-permute-start | bytes 786440 | tf_op jit(solution)/shard_map/ppermute | solution.py:402
  55.8 7.4 %collective-permute-done.in3_ref = bf16[64,16,128]{2,1,0:T(8,128)(2,1)S(1)} collective-permute-done((bf16[64,16,128]{2,1,0:T(8,128)(2,1)S(1)}, bf16[64,16,128]{2,1,0:T(8,128)(2,1)S(1)}, u32[]{:S(2)}, u32[]{:S(2)}) %collective-permute-start) | collective-permute-done | bytes 262176 | tf_op jit(solution)/shard_map/ppermute | solution.py:402
  63.1 1.4 %collective-permute-start.1 = (bf16[64,16,128]{2,1,0:T(8,128)(2,1)S(1)}, bf16[64,16,128]{2,1,0:T(8,128)(2,1)S(1)}, u32[]{:S(2)}, u32[]{:S(2)}) collective-permute-start(bf16[64,16,128]{2,1,0:T(8,128)(2,1)S(1)} %get-tuple-element.28), channel_id=1, source_target_pairs={{0,64},{64,128},{128,192},{192,0},{1,65},{65,129},{129,193},{193,1... | collective-permute-start | bytes 786440 | tf_op jit(solution)/shard_map/ppermute | solution.py:402
  64.5 2.7 %shard_map.95 = (f32[8,1024]{1,0:T(8,128)S(1)}, f32[3,1024,1024]{2,1,0:T(8,128)S(1)}) custom-call(s32[1]{0:T(128)} %bitcast.block_ref, bf16[64,65,128]{2,1,0:T(8,128)(2,1)S(1)} %all-to-all-done.own_ref, bf16[64,16,128]{2,1,0:T(8,128)(2,1)S(1)} %collective-permute-done.4.in1_ref, bf16[64,16,128]{2,1,0:T(8,128)(2,1)S(1)} %collective-permute-done.5.in2_ref, ...), custom_call_target="tpu_custom_call" | custom-call | tf_op jit(solution)/shard_map/pallas_call | solution.py:427
  67.3 3.1 %collective-permute-start.8 = (f32[8,1024]{1,0:T(8,128)S(1)}, f32[8,1024]{1,0:T(8,128)S(1)}, u32[]{:S(2)}, u32[]{:S(2)}) collective-permute-start(f32[8,1024]{1,0:T(8,128)S(1)} %get-tuple-element.34.stats_ref), channel_id=1, source_target_pairs={{0,192},{64,0},{128,64},{192,128},{1,193},{65,1},{129,65},{193,129... | collective-permute-start | bytes 98312 | tf_op jit(solution)/shard_map/ppermute | solution.py:390
  70.4 0.7 collective-permute-start.7
  71.1 0.8 collective-permute-start.6
  71.8 2.3 %shard_map.96 = (f32[1024,128]{1,0:T(8,128)S(1)}, f32[1024,128]{1,0:T(8,128)S(1)}, f32[8,128]{1,0:T(8,128)S(1)}) custom-call(bf16[64,65,128]{2,1,0:T(8,128)(2,1)S(1)} %all-to-all-done.own_ref, f32[8,1024]{1,0:T(8,128)S(1)} %get-tuple-element.34.stats_ref), custom_call_target="tpu_custom_call" | custom-call | tf_op jit(solution)/shard_map/pallas_call | solution.py:432
  74.1 0.7 collective-permute-done.8.st3_ref
  75.1 6.6 %shard_map.97 = (f32[1024,128]{1,0:T(8,128)S(1)}, f32[1024,128]{1,0:T(8,128)S(1)}, f32[8,128]{1,0:T(8,128)S(1)}) custom-call(s32[1]{0:T(128)} %bitcast.block_ref, bf16[64,65,128]{2,1,0:T(8,128)(2,1)S(1)} %all-to-all-done.own_ref, bf16[64,16,128]{2,1,0:T(8,128)(2,1)S(1)} %collective-permute-done.1.in1_ref, ...), custom_call_target="tpu_custom_call" | custom-call | tf_op jit(solution)/shard_map/pallas_call | solution.py:437
  81.7 2.6 %collective-permute-start.11 = (f32[8,128]{1,0:T(8,128)S(1)}, f32[8,128]{1,0:T(8,128)S(1)}, u32[]{:S(2)}, u32[]{:S(2)}) collective-permute-start(f32[8,128]{1,0:T(8,128)S(1)} %get-tuple-element.43.sums0_ref), channel_id=1, source_target_pairs={{0,192},{64,0},{128,64},{192,128},{1,193},{65,1},{129,65},{193,129... | collective-permute-start | bytes 12296 | tf_op jit(solution)/shard_map/ppermute | solution.py:390
  84.4 1.0 collective-permute-start.10
  85.7 0.7 shard_map.98
  86.4 1.9 %collective-permute-done.10.sums2_ref = f32[8,128]{1,0:T(8,128)S(1)} collective-permute-done((f32[8,128]{1,0:T(8,128)S(1)}, f32[8,128]{1,0:T(8,128)S(1)}, u32[]{:S(2)}, u32[]{:S(2)}) %collective-permute-start.10) | collective-permute-done | bytes 4128 | tf_op jit(solution)/shard_map/ppermute | solution.py:390
  88.3 0.7 collective-permute-done.9.sums1_ref
  89.4 28.6 %all_to_all.10 = f16[64,33,128]{2,1,0:T(8,128)(2,1)S(1)} all-to-all(f16[64,33,128]{2,1,0:T(8,128)(2,1)S(1)} %convert_element_type.6), channel_id=1, replica_groups=mesh['seq'=4,'head'=64] {'head'}, dimensions={0} | all-to-all | bytes 1081344 | tf_op jit(solution)/shard_map/all_to_all | solution.py:386
  118.1 1.2 %shard_map.100 = (f32[16,64,128]{2,1,0:T(8,128)}, f32[16,64,128]{2,1,0:T(8,128)}, f32[16,64]{1,0:T(8,128)}, f32[1,1]{1,0:T(1,128)}) custom-call(f32[64,33,128]{2,1,0:T(8,128)S(1)} %convert_element_type.7.x_ref), custom_call_target="tpu_custom_call" | custom-call | tf_op jit(solution)/shard_map/pallas_call | solution.py:456
  (16 shorter events, 1.3 us)
Async XLA Ops:
  3.3 44.5 %all-to-all-start = ((bf16[64,65,128]{2,1,0:T(8,128)(2,1)}), bf16[64,65,128]{2,1,0:T(8,128)(2,1)S(1)}, u32[]{:S(2)}, u32[]{:S(2)}) async-start(bf16[64,65,128]{2,1,0:T(8,128)(2,1)} %shard_map.93), calls=%async_computation | async-start | bytes 2359296 | tf_op jit(solution)/shard_map/all_to_all | solution.py:386
  47.9 16.7 %collective-permute-start.5 = (bf16[64,16,128]{2,1,0:T(8,128)(2,1)S(1)}, bf16[64,16,128]{2,1,0:T(8,128)(2,1)S(1)}, u32[]{:S(2)}, u32[]{:S(2)}) collective-permute-start(bf16[64,16,128]{2,1,0:T(8,128)(2,1)S(1)} %get-tuple-element.48), channel_id=1, source_target_pairs={{0,128},{64,192},{128,0},{192,64},{1,129},{65,193},{129,1},{193,65... | collective-permute-start | bytes 786440 | tf_op jit(solution)/shard_map/ppermute | solution.py:402
  50.7 12.4 %collective-permute-start = (bf16[64,16,128]{2,1,0:T(8,128)(2,1)S(1)}, bf16[64,16,128]{2,1,0:T(8,128)(2,1)S(1)}, u32[]{:S(2)}, u32[]{:S(2)}) collective-permute-start(bf16[64,16,128]{2,1,0:T(8,128)(2,1)S(1)} %get-tuple-element.49), channel_id=1, source_target_pairs={{0,192},{64,0},{128,64},{192,128},{1,193},{65,1},{129,65},{193,129... | collective-permute-start | bytes 786440 | tf_op jit(solution)/shard_map/ppermute | solution.py:402
  51.6 13.0 %collective-permute-start.4 = (bf16[64,16,128]{2,1,0:T(8,128)(2,1)S(1)}, bf16[64,16,128]{2,1,0:T(8,128)(2,1)S(1)}, u32[]{:S(2)}, u32[]{:S(2)}) collective-permute-start(bf16[64,16,128]{2,1,0:T(8,128)(2,1)S(1)} %get-tuple-element.50), channel_id=1, source_target_pairs={{0,64},{64,128},{128,192},{192,0},{1,65},{65,129},{129,193},{193,1... | collective-permute-start | bytes 786440 | tf_op jit(solution)/shard_map/ppermute | solution.py:402
  53.6 17.5 %collective-permute-start.3 = (bf16[64,16,128]{2,1,0:T(8,128)(2,1)S(1)}, bf16[64,16,128]{2,1,0:T(8,128)(2,1)S(1)}, u32[]{:S(2)}, u32[]{:S(2)}) collective-permute-start(bf16[64,16,128]{2,1,0:T(8,128)(2,1)S(1)} %get-tuple-element.51), channel_id=1, source_target_pairs={{0,192},{64,0},{128,64},{192,128},{1,193},{65,1},{129,65},{193,129... | collective-permute-start | bytes 786440 | tf_op jit(solution)/shard_map/ppermute | solution.py:402
  55.7 18.4 %collective-permute-start.2 = (bf16[64,16,128]{2,1,0:T(8,128)(2,1)S(1)}, bf16[64,16,128]{2,1,0:T(8,128)(2,1)S(1)}, u32[]{:S(2)}, u32[]{:S(2)}) collective-permute-start(bf16[64,16,128]{2,1,0:T(8,128)(2,1)S(1)} %get-tuple-element.53), channel_id=1, source_target_pairs={{0,128},{64,192},{128,0},{192,64},{1,129},{65,193},{129,1},{193,65... | collective-permute-start | bytes 786440 | tf_op jit(solution)/shard_map/ppermute | solution.py:402
  63.1 12.0 %collective-permute-start.1 = (bf16[64,16,128]{2,1,0:T(8,128)(2,1)S(1)}, bf16[64,16,128]{2,1,0:T(8,128)(2,1)S(1)}, u32[]{:S(2)}, u32[]{:S(2)}) collective-permute-start(bf16[64,16,128]{2,1,0:T(8,128)(2,1)S(1)} %get-tuple-element.28), channel_id=1, source_target_pairs={{0,64},{64,128},{128,192},{192,0},{1,65},{65,129},{129,193},{193,1... | collective-permute-start | bytes 786440 | tf_op jit(solution)/shard_map/ppermute | solution.py:402
  67.3 7.5 %collective-permute-start.8 = (f32[8,1024]{1,0:T(8,128)S(1)}, f32[8,1024]{1,0:T(8,128)S(1)}, u32[]{:S(2)}, u32[]{:S(2)}) collective-permute-start(f32[8,1024]{1,0:T(8,128)S(1)} %get-tuple-element.34.stats_ref), channel_id=1, source_target_pairs={{0,192},{64,0},{128,64},{192,128},{1,193},{65,1},{129,65},{193,129... | collective-permute-start | bytes 98312 | tf_op jit(solution)/shard_map/ppermute | solution.py:390
  70.4 4.4 %collective-permute-start.7 = (f32[8,1024]{1,0:T(8,128)S(1)}, f32[8,1024]{1,0:T(8,128)S(1)}, u32[]{:S(2)}, u32[]{:S(2)}) collective-permute-start(f32[8,1024]{1,0:T(8,128)S(1)} %get-tuple-element.34.stats_ref), channel_id=1, source_target_pairs={{0,128},{64,192},{128,0},{192,64},{1,129},{65,193},{129,1},{193,65... | collective-permute-start | bytes 98312 | tf_op jit(solution)/shard_map/ppermute | solution.py:390
  71.1 4.0 %collective-permute-start.6 = (f32[8,1024]{1,0:T(8,128)S(1)}, f32[8,1024]{1,0:T(8,128)S(1)}, u32[]{:S(2)}, u32[]{:S(2)}) collective-permute-start(f32[8,1024]{1,0:T(8,128)S(1)} %get-tuple-element.34.stats_ref), channel_id=1, source_target_pairs={{0,64},{64,128},{128,192},{192,0},{1,65},{65,129},{129,193},{193,1... | collective-permute-start | bytes 98312 | tf_op jit(solution)/shard_map/ppermute | solution.py:390
  81.7 4.7 %collective-permute-start.11 = (f32[8,128]{1,0:T(8,128)S(1)}, f32[8,128]{1,0:T(8,128)S(1)}, u32[]{:S(2)}, u32[]{:S(2)}) collective-permute-start(f32[8,128]{1,0:T(8,128)S(1)} %get-tuple-element.43.sums0_ref), channel_id=1, source_target_pairs={{0,192},{64,0},{128,64},{192,128},{1,193},{65,1},{129,65},{193,129... | collective-permute-start | bytes 12296 | tf_op jit(solution)/shard_map/ppermute | solution.py:390
  84.4 4.0 %collective-permute-start.10 = (f32[8,128]{1,0:T(8,128)S(1)}, f32[8,128]{1,0:T(8,128)S(1)}, u32[]{:S(2)}, u32[]{:S(2)}) collective-permute-start(f32[8,128]{1,0:T(8,128)S(1)} %get-tuple-element.43.sums0_ref), channel_id=1, source_target_pairs={{0,128},{64,192},{128,0},{192,64},{1,129},{65,193},{129,1},{193,65... | collective-permute-start | bytes 12296 | tf_op jit(solution)/shard_map/ppermute | solution.py:390
  85.3 3.7 %collective-permute-start.9 = (f32[8,128]{1,0:T(8,128)S(1)}, f32[8,128]{1,0:T(8,128)S(1)}, u32[]{:S(2)}, u32[]{:S(2)}) collective-permute-start(f32[8,128]{1,0:T(8,128)S(1)} %get-tuple-element.43.sums0_ref), channel_id=1, source_target_pairs={{0,64},{64,128},{128,192},{192,0},{1,65},{65,129},{129,193},{193,1... | collective-permute-start | bytes 12296 | tf_op jit(solution)/shard_map/ppermute | solution.py:390
